TPU v7x, 128 devices: a whole 4x4x4 slice. The times are simulated.
128 devices in a mesh: wide: 16 (over y, z), narrow: 8 (over x, core).
Axes of the slice: x: 4, y: 4, z: 4, core: 2. Of those that a mesh axis runs over, the one named last changes fastest.
Arguments:
- stream_hat: bfloat16 [2, 8192, 8192], P(None, ('wide', 'narrow')), may hold values from -2.682209e-07 to 2.682209e-07
- dye: bfloat16 [8192, 8192], P(('wide', 'narrow')), may hold values from -6 to 6
- float_slot: int32 [1048576], P(('wide', 'narrow')), may hold values from 0 to 255, as said below
- float_row: int32 [1048576], P(('wide', 'narrow')), may hold values from 0 to 62
- float_col: int32 [1048576], P(('wide', 'narrow')), may hold values from 0 to 126
- float_frac: float32 [2, 1048576], P(None, ('wide', 'narrow')), may hold values from 0 to 1
- float_dye: float32 [1048576], P(('wide', 'narrow')), may hold values from 0.1 to 10
- tile_lists: int32 [16, 256], replicated, may hold values from -1 to 8191, as said below
Outputs:
- float_velocity: float32 [2, 1048576], P(None, ('wide', 'narrow'))
- dye_hat: float32 [2, 8192, 8192], P(None, ('wide', 'narrow'))
Inputs may be any that keep to these rules, and one draw needn't show every extreme that they name: `tile_lists`: row g holds the distinct tiles needed by floats of group g, in no particular order, followed by -1 entries; tile t covers x cells from 128 (t % 64) and y cells from 64 (t // 64), and lies on device t // 64. At most 2 entries of a row lie on one device, every row has exactly 2 on some device, and some row has no -1 entry. `float_slot`: float f names a used entry of row f // 65536 of tile_lists.
All inputs are finite; a program needn't handle non-finite values.
Results may differ from a plain program's by a relative error of at most 0.0065.
Values may be sent and summed in bfloat16 or wider, within the bound.
No kernel may reach another device: no remote copies, remote signals or barrier semaphores. Data moves between devices by JAX's collectives and lax.ppermute only.
A program may use at most 192 MiB of HBM per device.

v0:
```python
from functools import partial
import math

import jax
import jax.numpy as jnp
from jax import lax
from jax.sharding import PartitionSpec as P

N2 = 128
TX = 128
TY = 64
CAPO = 2


TWO_PI = 2.0 * math.pi


def wave_tables(first, second, sign):
    total = first * second
    lower = jnp.arange(first, dtype=jnp.int32)
    upper = jnp.arange(second, dtype=jnp.int32)

    def trig_pair(counter, period):
        angle = sign * TWO_PI / period * counter.astype(jnp.float32)
        return (jnp.cos(angle), jnp.sin(angle))

    return (
        trig_pair(lower[:, None] * lower[None, :] % first, first),
        trig_pair(upper[:, None] * upper[None, :] % second, second),
        trig_pair(lower[:, None] * upper[None, :] % total, total),
    )


def complex_product(pattern, part_re, part_im, table):
    cosine_table, sine_table = table
    product = partial(jnp.einsum, precision=lax.Precision.HIGHEST)
    if part_im is None:
        return (product(pattern, part_re, cosine_table), product(pattern, part_re, sine_table))
    return (
        product(pattern, part_re, cosine_table) - product(pattern, part_im, sine_table),
        product(pattern, part_re, sine_table) + product(pattern, part_im, cosine_table),
    )


def along_first(part_re, part_im, second, sign, real_only):
    length = part_re.shape[0]
    first = length // second
    outer, inner, twist = wave_tables(first, second, sign)
    shaped_re = part_re.reshape(first, second, -1)
    shaped_im = part_im.reshape(first, second, -1)
    middle_re, middle_im = complex_product("mnb,mk->knb", shaped_re, shaped_im, outer)
    twist_cos = twist[0][:, :, None]
    twist_sin = twist[1][:, :, None]
    turned_re = middle_re * twist_cos - middle_im * twist_sin
    turned_im = middle_re * twist_sin + middle_im * twist_cos
    if real_only:
        product = partial(jnp.einsum, precision=lax.Precision.HIGHEST)
        result = product("knb,nj->jkb", turned_re, inner[0]) - product(
            "knb,nj->jkb", turned_im, inner[1]
        )
        return result.reshape(length, -1)
    final_re, final_im = complex_product("knb,nj->jkb", turned_re, turned_im, inner)
    return (final_re.reshape(length, -1), final_im.reshape(length, -1))


def along_last(part_re, part_im, second, sign):
    length = part_re.shape[-1]
    first = length // second
    batch = part_re.shape[0]
    outer, inner, twist = wave_tables(first, second, sign)
    shaped_re = part_re.reshape(batch, first, second)
    shaped_im = None if part_im is None else part_im.reshape(batch, first, second)
    middle_re, middle_im = complex_product("bmn,mk->bkn", shaped_re, shaped_im, outer)
    twist_cos = twist[0][None]
    twist_sin = twist[1][None]
    turned_re = middle_re * twist_cos - middle_im * twist_sin
    turned_im = middle_re * twist_sin + middle_im * twist_cos
    final_re, final_im = complex_product("bkn,nj->bjk", turned_re, turned_im, inner)
    return (final_re.reshape(batch, length), final_im.reshape(batch, length))


def signed_wave(index, length):
    return jnp.where(index >= length // 2, index - length, index).astype(jnp.float32)


def pencil_turn(blocks):
    return lax.all_to_all(blocks, ("wide", "narrow"), split_axis=1, concat_axis=0, tiled=True)


def sample_store(store_rows, tile_pos, row_in_tile, col_in_tile, frac_y, frac_x, amount, tiles):
    lanes = jnp.arange(2 * TY)[None, :]
    levels = lanes % TY
    weight_y = jnp.where(levels == row_in_tile[:, None], 1.0 - frac_y, 0.0) + jnp.where(
        levels == row_in_tile[:, None] + 1, frac_y, 0.0
    )
    cell_row = tile_pos * TX + col_in_tile
    nearer = store_rows[cell_row].astype(jnp.float32)
    farther = store_rows[cell_row + 1].astype(jnp.float32)
    mixed = ((1.0 - frac_x) * nearer + frac_x * farther) * weight_y
    selector = (jnp.arange(2 * TY)[:, None] // TY == jnp.arange(2)[None, :]).astype(jnp.float32)
    speed = jnp.dot(mixed, selector, precision=lax.Precision.HIGHEST)
    columns = jnp.arange(TX)[None, :]
    weight_x = jnp.where(columns == col_in_tile[:, None], 1.0 - frac_x, 0.0) + jnp.where(
        columns == col_in_tile[:, None] + 1, frac_x, 0.0
    )
    lower_part = amount * (1.0 - frac_y) * weight_x
    upper_part = amount * frac_y * weight_x
    base_row = tile_pos * TY + row_in_tile
    deposit = jax.ops.segment_sum(
        jnp.concatenate([lower_part, upper_part]),
        jnp.concatenate([base_row, base_row + 1]),
        num_segments=tiles * TY,
    )
    return (speed, deposit)


def shards(stream_hat, dye, float_slot, float_row, float_col, float_frac, float_dye, tile_lists):
    slab_rows = stream_hat.shape[1]
    length = stream_hat.shape[2]
    devices = lax.axis_size(("wide", "narrow"))
    narrow = lax.axis_size("narrow")
    groups = tile_lists.shape[0]
    slots = tile_lists.shape[1]
    device_index = lax.axis_index(("wide", "narrow"))
    group_index = lax.axis_index("wide")
    tiles_dev = slab_rows // TY * (length // TX)
    capacity = CAPO
    spec_re = stream_hat[0].astype(jnp.float32)
    spec_im = stream_hat[1].astype(jnp.float32)
    wave_x = signed_wave(device_index * slab_rows + jnp.arange(slab_rows), length)[:, None]
    wave_y = signed_wave(jnp.arange(length), length)[None, :]
    real_parts = jnp.concatenate([wave_y * spec_im, -wave_x * spec_im])
    imag_parts = jnp.concatenate([-wave_y * spec_re, wave_x * spec_re])
    half_re, half_im = along_last(real_parts, imag_parts, N2, 1.0)
    packed = jnp.stack(
        [
            half_re.reshape(2, slab_rows, devices, slab_rows),
            half_im.reshape(2, slab_rows, devices, slab_rows),
        ],
        axis=1,
    )
    packed = packed.transpose(2, 3, 0, 1, 4).reshape(slab_rows, devices, 4 * slab_rows)
    turned = pencil_turn(packed).reshape(length, 2, 2, slab_rows)
    column_re = turned[:, :, 0, :].reshape(length, 2 * slab_rows)
    column_im = turned[:, :, 1, :].reshape(length, 2 * slab_rows)
    velocity = along_first(column_re, column_im, N2, 1.0, True).astype(jnp.bfloat16)
    owned_tiles = velocity.reshape(length // TX, TX, 2, slab_rows // TY, TY)
    owned_tiles = owned_tiles.transpose(3, 0, 1, 2, 4).reshape(tiles_dev, TX, 2 * TY)
    valid = tile_lists >= 0
    holder = jnp.where(valid, tile_lists // tiles_dev, devices)
    onehot = (holder[:, :, None] == jnp.arange(devices)[None, None, :]).astype(jnp.int32)
    place = jnp.sum(jnp.cumsum(onehot, axis=1) * onehot, axis=-1) - 1
    mine = valid & (holder == device_index)
    group_rows = jnp.broadcast_to(jnp.arange(groups)[:, None], (groups, slots))
    send_index = jnp.full((groups, capacity), tiles_dev, jnp.int32)
    send_index = send_index.at[group_rows, jnp.where(mine, place, capacity)].set(
        tile_lists - device_index * tiles_dev, mode="drop"
    )
    padded_tiles = jnp.concatenate([owned_tiles, jnp.zeros((1, TX, 2 * TY), jnp.bfloat16)])
    outgoing = padded_tiles[send_index]
    holder_mine = lax.dynamic_index_in_dim(holder, group_index, 0, keepdims=False)
    place_mine = lax.dynamic_index_in_dim(place, group_index, 0, keepdims=False)
    matches = float_slot[:, None] == jnp.arange(slots)[None, :]
    frac_y = float_frac[0][:, None]
    frac_x = float_frac[1][:, None]
    amount = float_dye[:, None]
    fanned = jnp.broadcast_to(outgoing[:, None], (groups, narrow, capacity, TX, 2 * TY))
    store = lax.all_to_all(
        fanned.reshape(devices, capacity, TX, 2 * TY),
        ("wide", "narrow"),
        split_axis=0,
        concat_axis=0,
        tiled=True,
    )
    store_rows = store.reshape(devices * capacity * TX, 2 * TY)
    position = holder_mine * capacity + place_mine
    flat_tile = jnp.sum(jnp.where(matches, position[None, :], 0), axis=1)
    speed, deposit = sample_store(
        store_rows, flat_tile, float_row, float_col, frac_y, frac_x, amount, devices * capacity
    )
    float_velocity = speed.T
    returned = lax.all_to_all(
        deposit.reshape(devices, capacity, TY, TX).astype(jnp.bfloat16),
        ("wide", "narrow"),
        split_axis=0,
        concat_axis=0,
        tiled=True,
    ).astype(jnp.float32)
    target = jnp.broadcast_to(send_index[:, None], (groups, narrow, capacity)).reshape(-1)
    placed = jax.ops.segment_sum(returned.reshape(-1, TY, TX), target, num_segments=tiles_dev + 1)[
        :tiles_dev
    ]
    slab = (
        placed.reshape(slab_rows // TY, length // TX, TY, TX)
        .transpose(0, 2, 1, 3)
        .reshape(slab_rows, length)
    )
    total = dye.astype(jnp.float32) + slab
    front_re, front_im = along_last(total, None, N2, -1.0)
    packed = jnp.stack(
        [
            front_re.reshape(slab_rows, devices, slab_rows),
            front_im.reshape(slab_rows, devices, slab_rows),
        ],
        axis=2,
    )
    turned = pencil_turn(packed.reshape(slab_rows, devices, 2 * slab_rows)).reshape(
        length, 2, slab_rows
    )
    spectrum_re, spectrum_im = along_first(turned[:, 0, :], turned[:, 1, :], N2, -1.0, False)
    dye_hat = jnp.stack([spectrum_re.T, spectrum_im.T]) / length
    return (float_velocity, dye_hat)


def solution(mesh):
    return jax.shard_map(
        shards,
        mesh=mesh,
        in_specs=(
            P(None, ("wide", "narrow"), None),
            P(("wide", "narrow"), None),
            P(("wide", "narrow")),
            P(("wide", "narrow")),
            P(("wide", "narrow")),
            P(None, ("wide", "narrow")),
            P(("wide", "narrow")),
            P(),
        ),
        out_specs=(P(None, ("wide", "narrow")), P(None, ("wide", "narrow"), None)),
        check_vma=False,
    )
```

profile of v0, /device:TPU:1, one launch (start us, length us, event | category | flops | bytes accessed | tf_op | source)
XLA Modules:
  0.0 659.2 jit_solution(7267035466150819897)
XLA Ops:
  2.5 5.7 select_reduce_fusion.1
  8.7 2.6 select_reduce_fusion
  12.5 8.9 %fusion.9 = (f32[8192,128]{1,0:T(8,128)}, f32[8192,128]{1,0:T(8,128)}) fusion(s32[8192]{0:T(1024)S(1)} %get-tuple-element.29, s32[8192]{0:T(1024)S(1)} %copy-done.10, f32[8192]{0:T(1024)S(1)} %get-tuple-element.22, f32[8192]{0:T(1024)S(1)} %bitcast.227, f32[8192]{0:T(1024)S(1)} %get-tuple-element.37, f32[8192]{0:T(1024)S(1)} %get-tuple-element.23), kind=kLoop, calls=%fused_computation.27 | loop fusion | flops 7340032 | bytes 8585216 | tf_op jit(solution)/shard_map/mul | solution.py:106
  21.5 93.6 %scatter_custom_fusion = f32[16384,128]{1,0:T(8,128)} fusion(s32[16384]{0:T(1024)S(1)} %pad_add_fusion, f32[8192,128]{1,0:T(8,128)} %get-tuple-element.19, f32[]{:T(128)} %constant.202, f32[8192,128]{1,0:T(8,128)} %get-tuple-element.18, f32[]{:T(128)} %constant.182.clone.1), kind=kCustom, calls=%fused_computation.9 | custom fusion | flops 4194304 | bytes 16777224 | tf_op jit(solution)/shard_map/scatter-add | solution.py:109
  115.1 5.1 convert_element_type.208
  120.2 12.1 %all-to-all-start.2 = ((bf16[128,2,64,128]{3,2,1,0:T(8,128)(2,1)}), bf16[128,2,64,128]{3,2,1,0:T(8,128)(2,1)}, u32[]{:S(2)}, u32[]{:S(2)}) async-start(bf16[128,2,64,128]{3,2,1,0:T(8,128)(2,1)} %bitcast.209), calls=%async_computation.2 | async-start | bytes 8388608 | tf_op jit(solution)/shard_map/all_to_all | solution.py:182
  134.1 4.1 fusion.40
  138.2 4.2 fusion.39
  142.7 4.5 fusion.43
  147.1 5.4 subtract_bitcast_fusion
  152.5 7.4 %fusion.31 = f32[128,128,64]{0,1,2:T(8,128)S(1)} fusion(f32[128,64,128]{2,1,0:T(8,128)S(1)} %get-tuple-element.7), kind=kOutput, calls=%fused_computation.55 | convolution fusion | flops 1610842112 | bytes 8388608 | tf_op jit(solution)/shard_map/bkn,nj->bjk/dot_general | solution.py:41
  159.9 7.1 %fusion.48 = f32[128,128,64]{0,1,2:T(8,128)S(1)} fusion(f32[128,128,64]{0,1,2:T(8,128)S(1)} %fusion.31, f32[128,64,128]{2,1,0:T(8,128)S(1)} %get-tuple-element.6), kind=kOutput, calls=%fused_computation.70 | convolution fusion | flops 1611890688 | bytes 12582912 | tf_op jit(solution)/shard_map/bkn,nj->bjk/dot_general | solution.py:41
  167.0 2.4 copy.245
  169.5 7.1 %fusion.33 = f32[128,128,64]{0,1,2:T(8,128)S(1)} fusion(f32[128,64,128]{2,1,0:T(8,128)S(1)} %get-tuple-element.7), kind=kOutput, calls=%fused_computation.57 | convolution fusion | flops 1610842112 | bytes 8388608 | tf_op jit(solution)/shard_map/bkn,nj->bjk/dot_general | solution.py:40
  176.6 7.5 %fusion.45 = f32[128,128,64]{0,1,2:T(8,128)S(1)} fusion(f32[128,128,64]{0,1,2:T(8,128)S(1)} %fusion.33, f32[128,64,128]{2,1,0:T(8,128)S(1)} %get-tuple-element.6), kind=kOutput, calls=%fused_computation.69 | convolution fusion | flops 1611890688 | bytes 12582912 | tf_op jit(solution)/shard_map/bkn,nj->bjk/dot_general | solution.py:40
  184.1 2.4 copy.244
  186.5 4.1 pad_maximum_fusion
  190.6 9.2 %copy.246 = f32[64,128,256]{2,0,1:T(8,128)} copy(f32[64,128,256]{1,2,0:T(8,128)} %bitcast.202) | data formatting | bytes 16777216 | tf_op jit(solution)/shard_map/reshape | solution.py:142
  199.8 10.2 %all-to-all-start = ((f32[64,128,256]{2,0,1:T(8,128)}), f32[64,128,256]{2,0,1:T(8,128)}, u32[]{:S(2)}, u32[]{:S(2)}) async-start(f32[64,128,256]{2,0,1:T(8,128)} %copy.246), calls=%async_computation | async-start | bytes 16777216 | tf_op jit(solution)/shard_map/all_to_all | solution.py:87
  210.9 15.5 %scatter_custom_fusion.2 = s32[32]{0:T(128)S(1)} fusion(s32[4096]{0:T(1024)S(1)} %bitcast.232, s32[4096]{0:T(1024)S(1)} %bitcast.233, s32[]{:T(128)} %constant.165.clone.1), kind=kCustom, calls=%fused_computation.284 | custom fusion | bytes 132
  227.0 6.5 bitcast_convert_fusion
  233.8 26.8 %scatter_fusion = f32[65,64,128]{2,1,0:T(8,128)S(1)} fusion(f32[65,64,128]{2,1,0:T(8,128)S(1)} %broadcast_in_dim.84, s32[256]{0:T(256)S(1)} %reshape.388, f32[256,64,128]{2,1,0:T(8,128)} %bitcast_convert_fusion), kind=kCustom, calls=%fused_computation.4 | custom fusion | flops 2097152 | bytes 25166848 | tf_op jit(solution)/shard_map/scatter-add | solution.py:190
  263.8 2.1 fusion.118
  265.9 2.1 fusion.123
  268.0 2.2 fusion.60
  270.2 2.1 add_bitcast_fusion.1
  272.3 2.4 fusion.62
  274.7 2.1 subtract_bitcast_fusion.1
  277.4 2.3 copy.271
  279.8 5.4 copy.272
  285.2 25.5 %all-to-all-done = f32[64,128,256]{2,0,1:T(8,128)} async-done(((f32[64,128,256]{2,0,1:T(8,128)}), f32[64,128,256]{2,0,1:T(8,128)}, u32[]{:S(2)}, u32[]{:S(2)}) %all-to-all-start) | async-done | bytes 8388640 | tf_op jit(solution)/shard_map/all_to_all | solution.py:87
  310.7 13.0 %all-to-all-start.3 = ((f32[64,128,128]{2,0,1:T(8,128)}), f32[64,128,128]{2,0,1:T(8,128)}, u32[]{:S(2)}, u32[]{:S(2)}) async-start(f32[64,128,128]{2,0,1:T(8,128)} %copy.272), calls=%async_computation.3 | async-start | bytes 8388608 | tf_op jit(solution)/shard_map/all_to_all | solution.py:87
  323.7 17.0 %reshape.424 = f32[8192,2,2,64]{3,2,1,0:T(2,128)} reshape(f32[128,64,1,256]{3,1,0,2:T(8,128)} %bitcast.15) | data formatting | bytes 16777216 | tf_op jit(solution)/shard_map/reshape | solution.py:143
  340.7 35.1 %slice_reduce_fusion = f32[8192,2,64]{2,1,0:T(2,128)} fusion(f32[8192,2,2,64]{3,2,1,0:T(2,128)} %reshape.424), kind=kLoop, calls=%fused_computation.6 | loop fusion | bytes 8388608 | tf_op jit(solution)/shard_map/slice | solution.py:145
  375.8 9.2 %reshape.428 = f32[64,128,128]{2,1,0:T(8,128)} reshape(f32[8192,2,64]{2,1,0:T(2,128)} %slice_reduce_fusion) | data formatting | bytes 8388608 | tf_op jit(solution)/shard_map/reshape;reshape;squeeze | solution.py:50
  385.0 31.9 %slice_reduce_fusion.1 = f32[8192,2,64]{2,1,0:T(2,128)} fusion(f32[8192,2,2,64]{3,2,1,0:T(2,128)} %reshape.424), kind=kLoop, calls=%fused_computation.7 | loop fusion | bytes 8388608 | tf_op jit(solution)/shard_map/slice | solution.py:144
  416.9 8.8 %reshape.427 = f32[64,128,128]{2,1,0:T(8,128)} reshape(f32[8192,2,64]{2,1,0:T(2,128)} %slice_reduce_fusion.1) | data formatting | bytes 8388608 | tf_op jit(solution)/shard_map/reshape;reshape;squeeze | solution.py:49
  425.7 8.8 %fusion.25 = f32[64,128,128]{2,0,1:T(8,128)S(1)} fusion(f32[64,128,128]{2,1,0:T(8,128)} %reshape.428), kind=kOutput, calls=%fused_computation.49 | convolution fusion | flops 805363712 | bytes 8388608 | tf_op jit(solution)/shard_map/mnb,mk->knb/dot_general | solution.py:40
  434.5 6.3 fusion.23
  440.8 6.4 fusion.51
  447.2 9.4 %multiply_subtract_fusion = (f32[64,128,128]{2,0,1:T(8,128)S(1)}, f32[64,128,128]{2,0,1:T(8,128)S(1)}) fusion(f32[64,128,128]{2,0,1:T(8,128)S(1)} %fusion.51, f32[64,128]{0,1:T(8,128)S(1)} %copy.253, f32[64,128]{0,1:T(8,128)S(1)} %copy.250, f32[64,128,128]{2,0,1:T(8,128)S(1)} %fusion.23, f32[64,128,128]{2,1,0:T(8,128)S(1)} %copy-done), kind=kOutput, calls=%fused_computation.42 | convolution fusion | flops 812703744 | bytes 21037056 | tf_op jit(solution)/shard_map/mnb,mk->knb/dot_general | solution.py:41
  456.6 6.3 fusion.4
  462.9 8.2 %subtract_convert_fusion = bf16[128,64,128]{2,0,1:T(8,128)(2,1)S(1)} fusion(f32[128,64,128]{2,0,1:T(8,128)S(1)} %fusion.4, f32[64,128,128]{2,0,1:T(8,128)S(1)} %get-tuple-element.4), kind=kOutput, calls=%fused_computation.40 | convolution fusion | flops 1612939264 | bytes 10485760 | tf_op jit(solution)/shard_map/knb,nj->jkb/dot_general | solution.py:58
  473.4 5.4 broadcast_in_dim.75
  478.8 10.2 %all-to-all-start.1 = ((bf16[128,2,128,128]{3,2,1,0:T(8,128)(2,1)}), bf16[128,2,128,128]{3,2,1,0:T(8,128)(2,1)}, u32[]{:S(2)}, u32[]{:S(2)}) async-start(bf16[128,2,128,128]{3,2,1,0:T(8,128)(2,1)} %bitcast.201), calls=%async_computation.1 | async-start | bytes 16777216 | tf_op jit(solution)/shard_map/all_to_all | solution.py:168
  489.0 9.2 %reshape.425 = f32[8192,2,64]{2,1,0:T(2,128)} reshape(f32[128,64,1,128]{3,1,0,2:T(8,128)} %bitcast.45) | data formatting | bytes 8388608 | tf_op jit(solution)/shard_map/reshape | solution.py:207
  498.2 11.7 %fusion.320 = (f32[8192,1,64]{2,1,0:T(1,128)}, f32[8192,1,64]{2,1,0:T(1,128)}) fusion(f32[8192,2,64]{2,1,0:T(2,128)} %reshape.425), kind=kLoop, calls=%fused_computation.377 | loop fusion | bytes 8388608 | tf_op jit(solution)/shard_map/slice | solution.py:210
  510.0 4.2 copy.294
  514.1 3.9 copy.295
  518.1 3.8 fusion.121
  524.0 2.2 convolution_subtract_fusion
  526.2 2.7 multiply_add_fusion.1
  531.3 2.3 fusion.106
  533.6 2.1 fusion.104
  537.4 3.9 copy.279
  541.3 4.8 reshape.345
  548.1 2.1 fusion.105
  550.6 2.8 copy.276
  553.4 5.1 reshape.344
  558.5 4.0 maximum_multiply_fusion
  562.5 27.1 %all-to-all-done.1 = bf16[128,2,128,128]{3,2,1,0:T(8,128)(2,1)} async-done(((bf16[128,2,128,128]{3,2,1,0:T(8,128)(2,1)}), bf16[128,2,128,128]{3,2,1,0:T(8,128)(2,1)}, u32[]{:S(2)}, u32[]{:S(2)}) %all-to-all-start.1) | async-done | bytes 8388640 | tf_op jit(solution)/shard_map/all_to_all | solution.py:168
  589.7 26.4 %gather_fusion.2 = bf16[8192,128]{1,0:T(8,128)(2,1)S(1)} fusion(bf16[32768,128]{1,0:T(8,128)(2,1)} %bitcast.27, s32[8192]{0:T(1024)S(1)} %copy-done.12), kind=kCustom, calls=%fused_computation.2 | custom fusion | bytes 4227072 | tf_op jit(solution)/shard_map/gather | solution.py:98
  616.1 32.5 %gather_fusion.1 = bf16[8192,128]{1,0:T(8,128)(2,1)} fusion(bf16[32768,128]{1,0:T(8,128)(2,1)} %bitcast.27, s32[8192]{0:T(1024)S(1)} %copy-done.11), kind=kCustom, calls=%fused_computation.1 | custom fusion | bytes 4227072 | tf_op jit(solution)/shard_map/gather | solution.py:97
  648.6 10.4 %fusion.11 = f32[2,8192]{1,0:T(2,128)} fusion(bf16[8192,128]{1,0:T(8,128)(2,1)S(1)} %gather_fusion.2, bf16[8192,128]{1,0:T(8,128)(2,1)} %gather_fusion.1, f32[8192]{0:T(1024)S(1)} %bitcast.230, f32[8192]{0:T(1024)S(1)} %copy-done.23, s32[128]{0:T(128)S(1)} %get-tuple-element.35, f32[8192]{0:T(1024)S(1)} %bitcast.228, f32[8192]{0:T(1024)S(1)} %copy-done.14, ...), kind=kOutput, calls=%fused_computation.30 | convolution fusion | flops 36700672 | bytes 4457472 | tf_op jit(solution)/shard_map/dot_general | solution.py:101
  (116 shorter events, 21.9 us)
Async XLA Ops:
  1.5 6.7 %copy-start.18 = (f32[2,8192]{1,0:T(2,128)S(1)}, f32[2,8192]{1,0:T(2,128)}, u32[]{:S(2)}) copy-start(f32[2,8192]{1,0:T(2,128)} %param.13) | copy-start | bytes 196612
  2.3 6.4 copy-start.24
  2.3 8.9 %copy-start.10 = (s32[8192]{0:T(1024)S(1)}, s32[8192]{0:T(1024)}, u32[]{:S(2)}) copy-start(s32[8192]{0:T(1024)} %param.12) | copy-start | bytes 98308
  2.3 8.9 %copy-start.20 = (s32[8192]{0:T(1024)S(1)}, s32[8192]{0:T(1024)}, u32[]{:S(2)}) copy-start(s32[8192]{0:T(1024)} %param.11) | copy-start | bytes 98308
  2.3 9.6 %copy-start.19 = (f32[8192]{0:T(1024)S(1)}, f32[8192]{0:T(1024)}, u32[]{:S(2)}) copy-start(f32[8192]{0:T(1024)} %param.14) | copy-start | bytes 98308
  8.3 13.2 %copy-start.8 = (f32[1,8192]{1,0:T(1,128)}, f32[1,8192]{1,0:T(1,128)S(1)}, u32[]{:S(2)}) copy-start(f32[1,8192]{1,0:T(1,128)S(1)} %get-tuple-element.24) | copy-start | bytes 98308
  8.3 13.2 %copy-start.15 = (f32[1,8192]{1,0:T(1,128)}, f32[1,8192]{1,0:T(1,128)S(1)}, u32[]{:S(2)}) copy-start(f32[1,8192]{1,0:T(1,128)S(1)} %get-tuple-element.25) | copy-start | bytes 98308
  12.5 9.0 %copy-start.13 = (f32[8192]{0:T(1024)}, f32[8192]{0:T(1024)S(1)}, u32[]{:S(2)}) copy-start(f32[8192]{0:T(1024)S(1)} %get-tuple-element.37) | copy-start | bytes 98308
  120.2 12.4 %copy-start.6 = (bf16[2,64,8192]{2,1,0:T(8,128)(2,1)S(1)}, bf16[2,64,8192]{2,1,0:T(8,128)(2,1)}, u32[]{:S(2)}) copy-start(bf16[2,64,8192]{2,1,0:T(8,128)(2,1)} %param.8) | copy-start | bytes 6291460
  120.2 79.6 %all-to-all-start.2 = ((bf16[128,2,64,128]{3,2,1,0:T(8,128)(2,1)}), bf16[128,2,64,128]{3,2,1,0:T(8,128)(2,1)}, u32[]{:S(2)}, u32[]{:S(2)}) async-start(bf16[128,2,64,128]{3,2,1,0:T(8,128)(2,1)} %bitcast.209), calls=%async_computation.2 | async-start | bytes 8388608 | tf_op jit(solution)/shard_map/all_to_all | solution.py:182
  199.8 10.5 %copy-start.26 = (s32[2]{0:T(128)S(1)}, s32[2]{0:T(128)}, u32[]{:S(2)}) copy-start(s32[2]{0:T(128)} %constant.194) | copy-start | bytes 28
  199.8 10.7 %copy-start.25 = (s32[2]{0:T(128)S(1)}, s32[2]{0:T(128)}, u32[]{:S(2)}) copy-start(s32[2]{0:T(128)} %constant.191) | copy-start | bytes 28
  199.8 11.0 %copy-start.17 = (s32[16,256]{1,0:T(8,128)S(1)}, s32[16,256]{1,0:T(8,128)}, u32[]{:S(2)}) copy-start(s32[16,256]{1,0:T(8,128)} %param.15) | copy-start | bytes 49156
  199.8 110.9 %all-to-all-start = ((f32[64,128,256]{2,0,1:T(8,128)}), f32[64,128,256]{2,0,1:T(8,128)}, u32[]{:S(2)}, u32[]{:S(2)}) async-start(f32[64,128,256]{2,0,1:T(8,128)} %copy.246), calls=%async_computation | async-start | bytes 16777216 | tf_op jit(solution)/shard_map/all_to_all | solution.py:87
  260.6 1.5 copy-start.7
  310.7 162.8 %all-to-all-start.3 = ((f32[64,128,128]{2,0,1:T(8,128)}), f32[64,128,128]{2,0,1:T(8,128)}, u32[]{:S(2)}, u32[]{:S(2)}) async-start(f32[64,128,128]{2,0,1:T(8,128)} %copy.272), calls=%async_computation.3 | async-start | bytes 8388608 | tf_op jit(solution)/shard_map/all_to_all | solution.py:87
  425.7 8.8 %copy-start.1 = (f32[64,128,128]{2,1,0:T(8,128)S(1)}, f32[64,128,128]{2,1,0:T(8,128)}, u32[]{:S(2)}) copy-start(f32[64,128,128]{2,1,0:T(8,128)} %reshape.428) | copy-start | bytes 12582916
  434.5 6.3 copy-start
  478.8 110.8 %all-to-all-start.1 = ((bf16[128,2,128,128]{3,2,1,0:T(8,128)(2,1)}), bf16[128,2,128,128]{3,2,1,0:T(8,128)(2,1)}, u32[]{:S(2)}, u32[]{:S(2)}) async-start(bf16[128,2,128,128]{3,2,1,0:T(8,128)(2,1)} %bitcast.201), calls=%async_computation.1 | async-start | bytes 16777216 | tf_op jit(solution)/shard_map/all_to_all | solution.py:168
  518.1 3.8 copy-start.2
  531.3 4.4 copy-start.3
  546.0 2.1 copy-start.4
  553.4 5.1 copy-start.5
  558.5 31.1 %copy-start.12 = (s32[8192]{0:T(1024)S(1)}, s32[8192]{0:T(1024)}, u32[]{:S(2)}) copy-start(s32[8192]{0:T(1024)} %get-tuple-element.27) | copy-start | bytes 98308
  589.7 26.4 %copy-start.11 = (s32[8192]{0:T(1024)S(1)}, s32[8192]{0:T(1024)}, u32[]{:S(2)}) copy-start(s32[8192]{0:T(1024)} %get-tuple-element.26) | copy-start | bytes 98308
  616.0 32.5 %copy-start.9 = (f32[1,8192]{1,0:T(1,128)S(1)}, f32[1,8192]{1,0:T(1,128)}, u32[]{:S(2)}) copy-start(f32[1,8192]{1,0:T(1,128)} %copy-done.8) | copy-start | bytes 98308
  616.0 32.5 %copy-start.14 = (f32[8192]{0:T(1024)S(1)}, f32[8192]{0:T(1024)}, u32[]{:S(2)}) copy-start(f32[8192]{0:T(1024)} %copy-done.13) | copy-start | bytes 98308
  616.1 32.5 %copy-start.16 = (f32[1,8192]{1,0:T(1,128)S(1)}, f32[1,8192]{1,0:T(1,128)}, u32[]{:S(2)}) copy-start(f32[1,8192]{1,0:T(1,128)} %copy-done.15) | copy-start | bytes 98308
  616.1 32.5 %copy-start.21 = (s32[8192]{0:T(1024)S(1)}, s32[8192]{0:T(1024)}, u32[]{:S(2)}) copy-start(s32[8192]{0:T(1024)} %param.11) | copy-start | bytes 98308
  616.1 32.5 %copy-start.22 = (s32[8192]{0:T(1024)S(1)}, s32[8192]{0:T(1024)}, u32[]{:S(2)}) copy-start(s32[8192]{0:T(1024)} %get-tuple-element.32) | copy-start | bytes 98308
  616.1 32.5 %copy-start.23 = (f32[8192]{0:T(1024)S(1)}, f32[8192]{0:T(1024)}, u32[]{:S(2)}) copy-start(f32[8192]{0:T(1024)} %get-tuple-element.28) | copy-start | bytes 98308
where the time goes:
time: 671 us; the launch traced here: 659 us
  local copies, waits for them, and re-layouts  259 us (39%)
  other arithmetic  165 us (25%)
  matrix products  135 us (20%)
  waiting for transfers between devices  52.6 us (8%)
  starting transfers between devices  45.6 us (7%)
    scatter-add x1, other arithmetic, sample_store(): jax.ops.segment_sum(jnp.concatenate([lower_part, upper_part]), jnp.concat...  93.6 us
    slice x1, local copies, waits for them, and re-layouts, shards(): column_im = turned[:, :, 1, :].reshape(length, 2 * slab_rows)  35.1 us
    gather x1, local copies, waits for them, and re-layouts, sample_store(): nearer = store_rows[cell_row].astype(jnp.float32)  32.5 us
    slice x1, local copies, waits for them, and re-layouts, shards(): column_re = turned[:, :, 0, :].reshape(length, 2 * slab_rows)  31.9 us
    dot_general x6, matrix products, complex_product(): product(pattern, part_re, sine_table)  28.1 us
    all_to_all x1, waiting for transfers between devices, shards(): lax.all_to_all(fanned.reshape(devices, capacity, TX, 2 * TY), ('wide', 'n...  27.1 us
    scatter-add x1, other arithmetic, shards(): jax.ops.segment_sum(returned.reshape(-1, TY, TX), target, num_segments=ti...  26.8 us
    gather x1, local copies, waits for them, and re-layouts, sample_store(): farther = store_rows[cell_row + 1].astype(jnp.float32)  26.4 us
  transfers between devices with their start and end apart: 4, of which 2 were waited for; matrix products, arithmetic and copies ran while one was open for 55% of the time, Pallas kernels for 0%

commit v1 on v0

v1 whole, which is shorter than its diff:
```python
import numpy as np, math

import jax, jax.numpy as jnp
from jax import lax
from jax.sharding import PartitionSpec as P
from jax.experimental import pallas as pl
from jax.experimental.pallas import tpu as pltpu

BF = jnp.bfloat16
F32 = jnp.float32
VLIM = 60 * 1024 * 1024
NT = (((1,), (1,)), ((), ()))


def cs(num, den, sign):
    ang = sign * 2.0 * math.pi * (num % den) / den
    return np.cos(ang), np.sin(ang)


def cplx(c, s):
    return np.stack([np.stack([c, -s]), np.stack([s, c])])


def bf(x):
    return np.asarray(x, np.float32).astype(jnp.bfloat16)


def send_tables(sign, stream):
    p = np.arange(64)
    q = np.arange(128)
    c, s = cs(p[:, None] * p[None, :], 64, sign)
    w = cplx(c, s).transpose(0, 2, 1, 3)
    if stream:
        a = w.reshape(128, 128)
        signed = np.where(p >= 32, p - 64, p) * 128.0
        b = (w * signed).reshape(128, 128)
        g = np.concatenate([a, b])
    else:
        g = w[:, :, 0, :].reshape(128, 64)
    tc, ts = cs(p[:, None] * q[None, :], 8192, sign)
    c, s = cs(q[:, None] * q[None, :], 128, sign)
    w2 = cplx(c, s).transpose(2, 0, 1, 3).reshape(256, 256)
    return bf(g), np.float32(tc), np.float32(ts), bf(w2)


def recv_tables(sign, stream):
    k = np.arange(128)
    r = np.arange(64)
    c, s = cs(k[:, None] * k[None, :], 128, sign)
    w1 = cplx(c, s).transpose(0, 2, 3, 1).reshape(256, 256)
    tc, ts = cs(k[:, None] * r[None, :], 8192, sign)
    tc = np.concatenate([tc, tc], 1)
    ts = np.concatenate([ts, ts], 1)
    c, s = cs(r[:, None] * r[None, :], 64, sign)
    w = cplx(c, s)
    v = np.zeros((2, 2, 64, 2, 2, 64))
    for e in range(2):
        v[:, e, :, :, e, :] = w.transpose(0, 2, 1, 3)
    if stream:
        v = v[0].reshape(128, 256)
    else:
        v = v.reshape(256, 256) / 8192.0
    return bf(w1), np.float32(tc), np.float32(ts), bf(v)


def stream_send_kernel(wa_ref, s_ref, g_ref, tc_ref, ts_ref, w2_ref, o_ref, xs, tre, tim, of):
    def load(p, carry):
        at = pl.multiple_of(p * 128, 128)
        for c in range(2):
            row = pl.multiple_of((c * 64 + p) * 64, 64)
            xs[pl.ds(row, 64), :] = s_ref[c, :, pl.ds(at, 128)].astype(F32)
        return carry

    lax.fori_loop(0, 64, load, 0, unroll=4)
    q = lax.broadcasted_iota(jnp.int32, (64, 128), 1).astype(F32)

    def rows(r, carry):
        x = xs[pl.ds(r, 128, stride=64), :].astype(BF)
        z = jnp.dot(g_ref[...], x, preferred_element_type=F32)
        tc = tc_ref[...]
        ts = ts_ref[...]
        are, aim, bre, bim = z[:64], z[64:128], z[128:192], z[192:]
        ure = bre + q * are
        uim = bim + q * aim
        wa = wa_ref[0, r]
        base = pl.multiple_of(r * 128, 128)
        vre = are * tc - aim * ts
        vim = are * ts + aim * tc
        tre[pl.ds(base, 64), :] = ure * ts + uim * tc
        tim[pl.ds(base, 64), :] = uim * ts - ure * tc
        tre[pl.ds(base + 64, 64), :] = -wa * vim
        tim[pl.ds(base + 64, 64), :] = wa * vre
        return carry

    lax.fori_loop(0, 64, rows, 0, unroll=2)

    def cols(t, carry):
        parts = []
        for f in range(2):
            at = pl.ds(f * 64 + t, 64, stride=128)
            parts.append(jnp.concatenate([tre[at, :].astype(BF), tim[at, :].astype(BF)], axis=1))
        m = jnp.concatenate(parts, axis=0)
        of[pl.ds(t, 256, stride=64), :] = lax.dot_general(w2_ref[...], m, NT, preferred_element_type=F32)
        return carry

    lax.fori_loop(0, 64, cols, 0, unroll=2)

    def store(i, carry):
        o_ref[i] = of[pl.ds(pl.multiple_of(i * 64, 64), 64), :].astype(BF)
        return carry

    lax.fori_loop(0, 256, store, 0, unroll=8)


VM = pl.BlockSpec(memory_space=pltpu.VMEM)
SM = pl.BlockSpec(memory_space=pltpu.SMEM)


def call(kernel, outs, specs, scratch, cost, name, *args):
    return pl.pallas_call(
        kernel,
        out_shape=outs,
        in_specs=specs,
        out_specs=jax.tree.map(lambda _: VM, outs),
        scratch_shapes=scratch,
        compiler_params=pltpu.CompilerParams(vmem_limit_bytes=VLIM),
        cost_estimate=pl.CostEstimate(flops=cost, bytes_accessed=1 << 20, transcendentals=0),
        name=name,
    )(*args)


def stream_send(stream, wa):
    return call(
        stream_send_kernel,
        jax.ShapeDtypeStruct((256, 64, 128), BF),
        [SM] + [VM] * 5,
        [pltpu.VMEM((8192, 128), F32)] * 3 + [pltpu.VMEM((16384, 128), F32)],
        int(6e9), "stream_send",
        wa, stream, *send_tables(1.0, True),
    )


def stream_recv_kernel(x_ref, w1_ref, tc_ref, ts_ref, v_ref, o_ref, xf, of):
    def load(i, carry):
        xf[pl.ds(pl.multiple_of(i * 64, 64), 64), :] = x_ref[i].astype(F32)
        return carry

    lax.fori_loop(0, 256, load, 0, unroll=8)

    def step(t, carry):
        d = xf[pl.ds(t, 256, stride=64), :].astype(BF)
        z = jnp.dot(w1_ref[...], d, preferred_element_type=F32)
        re, im = z[:128], z[128:]
        tc = tc_ref[...]
        ts = ts_ref[...]
        m = jnp.concatenate([(re * tc - im * ts).astype(BF), (re * ts + im * tc).astype(BF)], axis=1)
        out = lax.dot_general(v_ref[...], m, NT, preferred_element_type=F32)
        for f in range(2):
            of[pl.ds(2 * t + f, 64, stride=128), :] = out[f * 64 : f * 64 + 64]
        return carry

    lax.fori_loop(0, 64, step, 0, unroll=2)

    def store(i, carry):
        o_ref[i] = of[pl.ds(pl.multiple_of(i * 128, 128), 128), :].astype(BF)
        return carry

    lax.fori_loop(0, 64, store, 0, unroll=4)


def stream_recv(x):
    return call(
        stream_recv_kernel,
        jax.ShapeDtypeStruct((64, 128, 128), BF),
        [VM] * 5,
        [pltpu.VMEM((16384, 128), F32), pltpu.VMEM((8192, 128), F32)],
        int(6e9), "stream_recv",
        x, *recv_tables(1.0, True),
    )


def dye_send_kernel(idx_ref, dye_ref, ret_ref, g_ref, tc_ref, ts_ref, w2_ref, o_ref, xs, tre, tim, of):
    def load(p, carry):
        at = pl.multiple_of(p * 128, 128)
        xs[pl.ds(pl.multiple_of(p * 64, 64), 64), :] = dye_ref[:, pl.ds(at, 128)].astype(F32)
        return carry

    lax.fori_loop(0, 64, load, 0, unroll=4)

    def place(n, carry):
        tile = idx_ref[0, n]

        @pl.when(tile >= 0)
        def _():
            g = n // 2
            e = n % 2
            total = ret_ref[g * 8 + e].astype(F32)
            for x in range(1, 4):
                total = total + ret_ref[g * 8 + 2 * x + e].astype(F32)
            at = pl.ds(pl.multiple_of(tile * 64, 64), 64)
            xs[at, :] = xs[at, :] + total

        return carry

    lax.fori_loop(0, 32, place, 0)

    def rows(r, carry):
        x = xs[pl.ds(r, 64, stride=64), :].astype(BF)
        z = jnp.dot(g_ref[...], x, preferred_element_type=F32)
        re, im = z[:64], z[64:]
        tc = tc_ref[...]
        ts = ts_ref[...]
        base = pl.multiple_of(r * 64, 64)
        tre[pl.ds(base, 64), :] = re * tc - im * ts
        tim[pl.ds(base, 64), :] = re * ts + im * tc
        return carry

    lax.fori_loop(0, 64, rows, 0, unroll=2)

    def cols(t, carry):
        parts = []
        for e in range(2):
            at = pl.ds(2 * t + e, 64, stride=64)
            parts.append(jnp.concatenate([tre[at, :].astype(BF), tim[at, :].astype(BF)], axis=1))
        m = jnp.concatenate(parts, axis=0)
        of[pl.ds(t, 256, stride=32), :] = lax.dot_general(w2_ref[...], m, NT, preferred_element_type=F32)
        return carry

    lax.fori_loop(0, 32, cols, 0, unroll=2)

    def store(i, carry):
        o_ref[i] = of[pl.ds(pl.multiple_of(i * 32, 32), 32), :].astype(BF)
        return carry

    lax.fori_loop(0, 256, store, 0, unroll=8)


def dye_send(idx, dye, ret):
    return call(
        dye_send_kernel,
        jax.ShapeDtypeStruct((256, 32, 128), BF),
        [SM] + [VM] * 6,
        [pltpu.VMEM((4096, 128), F32)] * 3 + [pltpu.VMEM((8192, 128), F32)],
        int(4e9), "dye_send",
        idx, dye, ret, *send_tables(-1.0, False),
    )


def dye_recv_kernel(x_ref, w1_ref, tc_ref, ts_ref, v_ref, o_ref, xf, of):
    def load(i, carry):
        xf[pl.ds(pl.multiple_of(i * 32, 32), 32), :] = x_ref[i].astype(F32)
        return carry

    lax.fori_loop(0, 256, load, 0, unroll=8)

    def step(t, carry):
        d = xf[pl.ds(t, 256, stride=32), :].astype(BF)
        z = jnp.dot(w1_ref[...], d, preferred_element_type=F32)
        re, im = z[:128], z[128:]
        tc = tc_ref[...]
        ts = ts_ref[...]
        m = jnp.concatenate([(re * tc - im * ts).astype(BF), (re * ts + im * tc).astype(BF)], axis=1)
        out = lax.dot_general(v_ref[...], m, NT, preferred_element_type=F32)
        for c in range(2):
            for e in range(2):
                row = c * 4096 + (t // 4) * 512 + (2 * t + e) % 8
                of[pl.ds(row, 64, stride=8), :] = out[(2 * c + e) * 64 : (2 * c + e) * 64 + 64]
        return carry

    lax.fori_loop(0, 32, step, 0, unroll=2)

    def store(n, carry):
        c = n // 8
        t8 = n % 8
        base = pl.multiple_of(n * 512, 512)
        at = pl.ds(pl.multiple_of(t8 * 8, 8), 8)
        for j in range(64):
            o_ref[c, at, j * 128 : j * 128 + 128] = of[pl.ds(base + j * 8, 8), :]
        return carry

    lax.fori_loop(0, 16, store, 0)


def dye_recv(x):
    return call(
        dye_recv_kernel,
        jax.ShapeDtypeStruct((2, 64, 8192), F32),
        [VM] * 5,
        [pltpu.VMEM((8192, 128), F32)] * 2,
        int(4e9), "dye_recv",
        x, *recv_tables(-1.0, False),
    )

CAPO = 2


def deposit_kernel(mb_ref, nb_ref, fy_ref, fx_ref, am_ref, o_ref, m_ref, acc):
    step = pl.program_id(0)
    width = mb_ref.shape[1]
    am = am_ref[...]
    hi = am * fy_ref[...]
    lo = am - hi
    mb = mb_ref[...]
    nb = nb_ref[...]
    fx = fx_ref[...]
    gx = 1.0 - fx

    def build_m(i, carry):
        at = pl.multiple_of(i * 64, 64)
        d = lax.broadcasted_iota(jnp.int32, (64, width), 0) + (i * 64 - mb)
        w = jnp.where(d == 0, lo, jnp.where(d == 1, hi, 0.0))
        m_ref[pl.ds(at, 64), :] = w.astype(BF)
        return carry

    lax.fori_loop(0, 16, build_m, 0)

    def part(i, first):
        d = lax.broadcasted_iota(jnp.int32, (256, width), 0) + (i * 256 - nb)
        w = jnp.where(d == 0, gx, jnp.where(d == 1, fx, 0.0)).astype(BF)
        z = lax.dot_general(m_ref[...], w, NT, preferred_element_type=F32)
        acc[i] = z if first else acc[i] + z

    @pl.when(step == 0)
    def _():
        lax.fori_loop(0, 8, lambda i, c: (part(i, True), c)[1], 0)

    @pl.when(step > 0)
    def _():
        lax.fori_loop(0, 8, lambda i, c: (part(i, False), c)[1], 0)

    @pl.when(step == pl.num_programs(0) - 1)
    def _():
        def store(p, carry):
            row = pl.multiple_of((p // 8) * 64, 64)
            for h in range(2):
                o_ref[p // 8 * 16 + p % 8 * 2 + h] = acc[p % 8, pl.ds(row, 64), h * 128 : h * 128 + 128].astype(BF)
            return carry

        lax.fori_loop(0, 128, store, 0, unroll=4)


def deposit(mb, nb, fy, fx, am, width=1024):
    blk = pl.BlockSpec((1, width), lambda i: (0, i))
    return pl.pallas_call(
        deposit_kernel,
        grid=(8192 // width,),
        out_shape=jax.ShapeDtypeStruct((256, 64, 128), BF),
        in_specs=[blk] * 5,
        out_specs=pl.BlockSpec((256, 64, 128), lambda i: (0, 0, 0)),
        scratch_shapes=[pltpu.VMEM((1024, width), BF), pltpu.VMEM((8, 1024, 256), F32)],
        compiler_params=pltpu.CompilerParams(vmem_limit_bytes=VLIM),
        cost_estimate=pl.CostEstimate(flops=int(34e9), bytes_accessed=4 << 20, transcendentals=0),
        name="deposit",
    )(mb, nb, fy, fx, am)


def gather_kernel(base_ref, a_ref, b_ref, col_ref, fy_ref, fx_ref, o_ref, st, g):
    def load(i, carry):
        at = pl.multiple_of(i * 128, 128)
        st[pl.ds(at, 128), :] = a_ref[i].astype(F32)
        st[pl.ds(at + 16384, 128), :] = b_ref[i].astype(F32)
        return carry

    lax.fori_loop(0, 128, load, 0, unroll=2)
    sub = lax.broadcasted_iota(jnp.int32, (8, 128), 0)
    off = lax.broadcasted_iota(jnp.int32, (8, 128), 1) - sub // 4
    upper = sub % 4 >= 2
    odd = sub % 2 == 1
    xs = lax.broadcasted_iota(jnp.int32, (128, 128), 0)

    def chunk(n, carry):
        for f in range(128):
            g[f * 4 : f * 4 + 4, :] = st[pl.ds(base_ref[n, f], 4), :]
        at = pl.ds(pl.multiple_of(n * 128, 128), 128)
        col = col_ref[:, at]
        fy = fy_ref[:, at]
        fx = fx_ref[:, at]
        d = xs - col
        w = jnp.where(d == 0, 1.0 - fx, jnp.where(d == 1, fx, 0.0))
        hi = w.astype(BF)
        lo = (w - hi.astype(F32)).astype(BF)
        rows = g[...].astype(BF)
        z = jnp.dot(rows, hi, preferred_element_type=F32) + jnp.dot(rows, lo, preferred_element_type=F32)
        total = jnp.zeros((8, 128), F32)
        for i in range(64):
            total = total + jnp.where(off == 2 * i, z[8 * i : 8 * i + 8], 0.0)
        total = total * jnp.where(upper, fy, 1.0 - fy)
        o_ref[0:1, at] = jnp.sum(jnp.where(odd, 0.0, total), axis=0, keepdims=True)
        o_ref[1:2, at] = jnp.sum(jnp.where(odd, total, 0.0), axis=0, keepdims=True)
        return carry

    lax.fori_loop(0, 64, chunk, 0)


def gather(base, a, b, col, fy, fx):
    return call(
        gather_kernel,
        jax.ShapeDtypeStruct((2, 8192), F32),
        [SM] + [VM] * 5,
        [pltpu.VMEM((32768, 128), F32), pltpu.VMEM((512, 128), F32)],
        int(2e10), "gather",
        base, a, b, col, fy, fx,
    )


AXES = ("wide", "narrow")


def spread(blocks):
    return lax.all_to_all(blocks, AXES, split_axis=0, concat_axis=0, tiled=True)


def swap_cores(x):
    n = lax.axis_size("narrow")
    return lax.ppermute(x, "narrow", [(i, i ^ 1) for i in range(n)])


def shards(stream_hat, dye, float_slot, float_row, float_col, float_frac, float_dye, tile_lists):
    device = lax.axis_index(AXES)
    group = lax.axis_index("wide")
    core = lax.axis_index("narrow") % 2
    wave = device * 64 + jnp.arange(64)
    wave = jnp.where(wave >= 4096, wave - 8192, wave).astype(F32)[None]
    slot = float_slot.reshape(64, 128)
    row = float_row.reshape(64, 128)
    col = float_col.reshape(64, 128)

    mine = (tile_lists >= 0) & (tile_lists // 64 == device)
    place = jnp.cumsum(mine.astype(jnp.int32), axis=1) - 1
    local = tile_lists % 64 + 1
    send_index = jnp.stack(
        [jnp.sum(jnp.where(mine & (place == e), local, 0), axis=1) for e in range(CAPO)], axis=1
    ) - 1

    own_list = lax.dynamic_index_in_dim(tile_lists, group, 0, keepdims=False)
    holder = own_list // 64
    before = jnp.arange(256)[:, None] > jnp.arange(256)[None, :]
    rank = jnp.sum((before & (holder[:, None] == holder[None, :])).astype(jnp.int32), axis=1)
    position = jnp.where(own_list >= 0, jnp.where(rank == core, 0, 128) + holder, 0)
    pos = jnp.sum(
        jnp.where(jnp.arange(256)[:, None, None] == slot[None], position[:, None, None], 0), axis=0
    )

    flat = lambda x: x.reshape(1, 8192)
    fy = float_frac[0:1]
    fx = float_frac[1:2]
    dep = deposit(
        flat(pos // 16 * 64 + row), flat(pos % 16 * 128 + col), fy, fx, flat(float_dye)
    )
    dep = (dep[:128].astype(F32) + swap_cores(dep[128:]).astype(F32)).astype(BF)
    returned = spread(dep)

    spec = stream_send(stream_hat, wave)
    spec = spread(spec.reshape(128, 2, 64, 128)).reshape(256, 64, 128)
    tiles = stream_recv(spec)
    outgoing = tiles[jnp.maximum(send_index, 0)]
    outgoing = jnp.broadcast_to(outgoing[:, None], (16, 4, 2, 128, 128)).reshape(128, 128, 128)
    own = spread(outgoing)
    other = swap_cores(own)

    front = dye_send(send_index.reshape(1, 32), dye, returned)
    front = spread(front.reshape(128, 2, 32, 128)).reshape(256, 32, 128)
    dye_hat = dye_recv(front)

    velocity = gather(pos * 128 + 2 * row, own, other, flat(float_col), fy, fx)
    return (velocity, dye_hat)


def solution(mesh):
    return jax.shard_map(
        shards,
        mesh=mesh,
        in_specs=(
            P(None, AXES, None),
            P(AXES, None),
            P(AXES),
            P(AXES),
            P(AXES),
            P(None, AXES),
            P(AXES),
            P(),
        ),
        out_specs=(P(None, AXES), P(None, AXES, None)),
        check_vma=False,
    )
```

time: 671 us -> 339 us (0.51); the launches traced: 659 us -> 338 us
  local copies, waits for them, and re-layouts: 259 us -> 11.7 us
  Pallas kernels: 0 us -> 175 us
  other arithmetic: 165 us -> 6.28 us
  matrix products: 135 us -> 0 us
  waiting for transfers between devices: 52.6 us -> 111 us
  starting transfers between devices: 45.6 us -> 33.4 us
    pallas_call x0 -> x6, Pallas kernels: none -> 175 us  [the longest x5 113 us: call(): pl.pallas_call(kernel, out_shape=outs, in_specs=specs, out_specs=jax.tree...]
    dot_general x25 -> x0, matrix products: 127 us -> none  [the longest x6 28.1 us: complex_product(): product(pattern, part_re, sine_table)]
    scatter-add x2 -> x0, other arithmetic: 120 us -> none  [the longest x1 93.6 us: sample_store(): jax.ops.segment_sum(jnp.concatenate([lower_part, upper_part]), jnp.concat...]
    slice x4 -> x3, local copies, waits for them, and re-layouts: 78.8 us -> 2.77 us  [the longest x1 1.91 us: shards(): dep = (dep[:128].astype(F32) + swap_cores(dep[128:]).astype(F32)).astype(BF)]
    gather x3 -> x1, local copies, waits for them, and re-layouts: 59.6 us -> 2.34 us  [shards(): outgoing = tiles[jnp.maximum(send_index, 0)]]
    all_to_all x4, waiting for transfers between devices: 52.6 us -> 107 us  [spread(): return lax.all_to_all(blocks, AXES, split_axis=0, concat_axis=0, tiled=True)]
    reshape x6 -> x0, local copies, waits for them, and re-layouts: 50.7 us -> none  [the longest x1 17 us: shards(): turned = pencil_turn(packed).reshape(length, 2, 2, slab_rows)]
    another operation x9 -> x2, local copies, waits for them, and re-layouts: 33.4 us -> 0.01 us  [the longest x2 13.1 us: along_first(): shaped_im = part_im.reshape(first, second, -1)]
  transfers between devices with their start and end apart: 4 -> 6, of which waited for: 2 -> 4; matrix products, arithmetic and copies ran while one was open for 55% -> 3% of each run, Pallas kernels for 0% -> 28%
where the time goes in v1:
time: 339 us; the launch traced here: 338 us
  Pallas kernels  175 us (52%)
  waiting for transfers between devices  111 us (33%)
  starting transfers between devices  33.4 us (10%)
  local copies, waits for them, and re-layouts  11.7 us (3%)
  other arithmetic  6.28 us (2%)
    pallas_call x5, Pallas kernels, call(): pl.pallas_call(kernel, out_shape=outs, in_specs=specs, out_specs=jax.tree...  113 us
    all_to_all x4, waiting for transfers between devices, spread(): return lax.all_to_all(blocks, AXES, split_axis=0, concat_axis=0, tiled=True)  107 us
    pallas_call x1, Pallas kernels, deposit(): pl.pallas_call(deposit_kernel, grid=(8192 // width,), out_shape=jax.Shape...  61.4 us
    all_to_all x4, starting transfers between devices, spread(): return lax.all_to_all(blocks, AXES, split_axis=0, concat_axis=0, tiled=True)  30.9 us
  transfers between devices with their start and end apart: 6, of which 4 were waited for; matrix products, arithmetic and copies ran while one was open for 3% of the time, Pallas kernels for 28%

profile of v1, /device:TPU:1, one launch (start us, length us, event | category | flops | bytes accessed | tf_op | source)
XLA Modules:
  0.0 338.1 jit_solution(12671127937136631437)
XLA Ops:
  0.6 0.5 fusion.14.wa_ref
  1.2 26.8 %stream_send.1 = bf16[256,64,128]{2,1,0:T(8,128)(2,1)} custom-call(f32[1,64]{1,0:T(1,128)} %fusion.14.wa_ref, bf16[2,64,8192]{2,1,0:T(8,128)(2,1)} %s_ref.1, bf16[256,128]{1,0:T(8,128)(2,1)} %constant.139.clone.g_ref, f32[64,128]{1,0:T(8,128)} %constant.140.clone.tc_ref, f32[64,128]{1,0:T(8,128)} %constant.141.clone.ts_ref, ...), custom_call_target="tpu_custom_call" | custom-call | flops 6000000000 | bytes 1048576 | tf_op jit(solution)/shard_map/stream_send/pallas_call | solution.py:120
  27.9 0.0 copy-start.4
  27.9 0.0 copy-start.7
  27.9 0.0 copy-start.3
  27.9 0.0 copy-start.6
  27.9 0.0 copy-start.5
  27.9 12.0 %all-to-all-start = ((bf16[128,2,64,128]{3,2,1,0:T(8,128)(2,1)}), bf16[128,2,64,128]{3,2,1,0:T(8,128)(2,1)}, u32[]{:S(2)}, u32[]{:S(2)}) async-start(bf16[128,2,64,128]{3,2,1,0:T(8,128)(2,1)} %bitcast.70), calls=%async_computation | async-start | bytes 8388608 | tf_op jit(solution)/shard_map/all_to_all | solution.py:410
  39.9 0.0 copy-done.4
  40.0 0.6 reduce-window.6
  40.6 0.2 slice_reduce_fusion
  40.8 0.1 compare_bitcast_fusion
  40.9 0.1 select_reduce_fusion.2
  41.0 0.1 copy.44
  41.1 0.1 reshape.235
  41.3 0.2 convert_reduce_fusion
  41.5 0.0 copy-done.7
  41.5 1.1 select_reduce_fusion
  42.6 0.0 copy-done.3
  42.6 0.0 copy-done.6
  42.6 0.7 fusion.4
  43.2 0.0 copy-done.5
  43.2 0.7 fusion.15
  43.9 48.6 %all-to-all-done = bf16[128,2,64,128]{3,2,1,0:T(8,128)(2,1)} async-done(((bf16[128,2,64,128]{3,2,1,0:T(8,128)(2,1)}), bf16[128,2,64,128]{3,2,1,0:T(8,128)(2,1)}, u32[]{:S(2)}, u32[]{:S(2)}) %all-to-all-start) | async-done | bytes 4194336 | tf_op jit(solution)/shard_map/all_to_all | solution.py:410
  92.6 30.7 %stream_recv.1 = bf16[64,128,128]{2,1,0:T(8,128)(2,1)} custom-call(bf16[256,64,128]{2,1,0:T(8,128)(2,1)} %bitcast.5.x_ref, bf16[256,256]{1,0:T(8,128)(2,1)} %constant.143.clone.w1_ref, f32[128,128]{1,0:T(8,128)} %constant.144.clone.tc_ref, f32[128,128]{1,0:T(8,128)} %constant.145.clone.ts_ref, bf16[128,256]{1,0:T(8,128)(2,1)} %constant.146.clone.v_ref), custom_call_target="tpu_custom_call" | custom-call | flops 6000000000 | bytes 1048576 | tf_op jit(solution)/shard_map/stream_recv/pallas_call | solution.py:120
  123.2 2.3 gather_fusion
  125.6 3.1 broadcast_in_dim.40
  128.6 5.5 %all-to-all-start.1 = ((bf16[128,128,128]{2,1,0:T(8,128)(2,1)}), bf16[128,128,128]{2,1,0:T(8,128)(2,1)}, u32[]{:S(2)}, u32[]{:S(2)}) async-start(bf16[128,128,128]{2,1,0:T(8,128)(2,1)} %bitcast.68), calls=%async_computation.1 | async-start | bytes 8388608 | tf_op jit(solution)/shard_map/all_to_all | solution.py:410
  134.1 61.4 %deposit.1 = bf16[256,64,128]{2,1,0:T(8,128)(2,1)} custom-call(s32[1,8192]{1,0:T(1,128)} %bitcast.76, s32[1,8192]{1,0:T(1,128)} %bitcast.75, f32[1,8192]{1,0:T(1,128)} %get-tuple-element.9.fy_ref, f32[1,8192]{1,0:T(1,128)} %get-tuple-element.8.fx_ref, f32[1,8192]{1,0:T(1,128)} %bitcast.85), custom_call_target="tpu_custom_call" | custom-call | flops 33999998976 | bytes 4194304 | tf_op jit(solution)/shard_map/deposit/pallas_call | solution.py:344
  195.6 0.0 copy-start
  195.6 1.9 slice.28
  197.5 1.4 collective-permute-start.1
  198.8 3.8 %collective-permute-done.1 = bf16[128,64,128]{2,1,0:T(8,128)(2,1)S(1)} collective-permute-done((bf16[128,64,128]{2,1,0:T(8,128)(2,1)S(1)}, bf16[128,64,128]{2,1,0:T(8,128)(2,1)S(1)}, u32[]{:S(2)}, u32[]{:S(2)}) %collective-permute-start.1) | collective-permute-done | bytes 2097184 | tf_op jit(solution)/shard_map/ppermute | solution.py:415
  202.6 0.0 copy-done
  202.6 2.3 add_convert_fusion
  204.9 0.0 all-to-all-done.1.a_ref
  204.9 9.0 %all-to-all-start.2 = ((bf16[128,64,128]{2,1,0:T(8,128)(2,1)}), bf16[128,64,128]{2,1,0:T(8,128)(2,1)S(1)}, u32[]{:S(2)}, u32[]{:S(2)}) async-start(bf16[128,64,128]{2,1,0:T(8,128)(2,1)} %add_convert_fusion), calls=%async_computation.2 | async-start | bytes 4194304 | tf_op jit(solution)/shard_map/all_to_all | solution.py:410
  213.9 1.1 collective-permute-start
  215.1 0.1 copy.45
  215.2 0.6 sub.42.idx_ref
  215.8 28.7 %all-to-all-done.2.ret_ref = bf16[128,64,128]{2,1,0:T(8,128)(2,1)S(1)} async-done(((bf16[128,64,128]{2,1,0:T(8,128)(2,1)}), bf16[128,64,128]{2,1,0:T(8,128)(2,1)S(1)}, u32[]{:S(2)}, u32[]{:S(2)}) %all-to-all-start.2) | async-done | bytes 2097184 | tf_op jit(solution)/shard_map/all_to_all | solution.py:410
  244.5 0.0 copy-start.1
  244.5 1.3 copy-done.1
  245.8 17.5 %dye_send.1 = bf16[256,32,128]{2,1,0:T(8,128)(2,1)} custom-call(s32[1,32]{1,0:T(1,128)} %sub.42.idx_ref, bf16[64,8192]{1,0:T(8,128)(2,1)} %dye_ref.1, bf16[128,64,128]{2,1,0:T(8,128)(2,1)} %copy-done.1, bf16[128,64]{1,0:T(8,128)(2,1)} %constant.147.clone.g_ref, f32[64,128]{1,0:T(8,128)} %constant.140.clone.tc_ref, f32[64,128]{1,0:T(8,128)} %constant.148.clone.ts_ref, ...), custom_call_target="tpu_custom_call" | custom-call | flops 4000000000 | bytes 1048576 | tf_op jit(solution)/shard_map/dye_send/pallas_call | solution.py:120
  263.2 4.4 %all-to-all-start.3 = ((bf16[128,2,32,128]{3,2,1,0:T(8,128)(2,1)}), bf16[128,2,32,128]{3,2,1,0:T(8,128)(2,1)S(1)}, u32[]{:S(2)}, u32[]{:S(2)}) async-start(bf16[128,2,32,128]{3,2,1,0:T(8,128)(2,1)} %bitcast.72), calls=%async_computation.3 | async-start | bytes 4194304 | tf_op jit(solution)/shard_map/all_to_all | solution.py:410
  267.7 0.6 bitcast_add_fusion.base_ref
  268.3 29.9 %all-to-all-done.3 = bf16[128,2,32,128]{3,2,1,0:T(8,128)(2,1)S(1)} async-done(((bf16[128,2,32,128]{3,2,1,0:T(8,128)(2,1)}), bf16[128,2,32,128]{3,2,1,0:T(8,128)(2,1)S(1)}, u32[]{:S(2)}, u32[]{:S(2)}) %all-to-all-start.3) | async-done | bytes 2097184 | tf_op jit(solution)/shard_map/all_to_all | solution.py:410
  298.2 0.0 copy-start.2
  298.2 1.4 copy-done.2
  299.6 14.7 %dye_recv.1 = f32[2,64,8192]{2,1,0:T(8,128)} custom-call(bf16[256,32,128]{2,1,0:T(8,128)(2,1)} %bitcast.71, bf16[256,256]{1,0:T(8,128)(2,1)} %constant.150.clone.w1_ref, f32[128,128]{1,0:T(8,128)} %constant.144.clone.tc_ref, f32[128,128]{1,0:T(8,128)} %constant.151.clone.ts_ref, bf16[256,256]{1,0:T(8,128)(2,1)} %constant.152.clone.v_ref), custom_call_target="tpu_custom_call" | custom-call | flops 4000000000 | bytes 1048576 | tf_op jit(solution)/shard_map/dye_recv/pallas_call | solution.py:120
  314.3 0.0 collective-permute-done.b_ref
  314.3 23.8 %gather.7 = f32[2,8192]{1,0:T(2,128)} custom-call(s32[64,128]{1,0:T(8,128)} %bitcast_add_fusion.base_ref, bf16[128,128,128]{2,1,0:T(8,128)(2,1)} %all-to-all-done.1.a_ref, bf16[128,128,128]{2,1,0:T(8,128)(2,1)} %collective-permute-done.b_ref, s32[1,8192]{1,0:T(1,128)} %bitcast.74, f32[1,8192]{1,0:T(1,128)} %get-tuple-element.9.fy_ref, ...), custom_call_target="tpu_custom_call" | custom-call | flops 20000000000 | bytes 1048576 | tf_op jit(solution)/shard_map/gather/pallas_call | solution.py:120
  (10 shorter events, 0.1 us)
Async XLA Ops:
  27.9 12.0 %copy-start.4 = (s32[16,256]{1,0:T(8,128)S(1)}, s32[16,256]{1,0:T(8,128)}, u32[]{:S(2)}) copy-start(s32[16,256]{1,0:T(8,128)} %param.31) | copy-start | bytes 49156
  27.9 13.5 %copy-start.7 = (s32[8192]{0:T(1024)S(1)}, s32[8192]{0:T(1024)}, u32[]{:S(2)}) copy-start(s32[8192]{0:T(1024)} %param.26) | copy-start | bytes 98308
  27.9 14.6 %copy-start.3 = (s32[8192]{0:T(1024)S(1)}, s32[8192]{0:T(1024)}, u32[]{:S(2)}) copy-start(s32[8192]{0:T(1024)} %param.27) | copy-start | bytes 98308
  27.9 14.7 %copy-start.6 = (s32[8192]{0:T(1024)S(1)}, s32[8192]{0:T(1024)}, u32[]{:S(2)}) copy-start(s32[8192]{0:T(1024)} %param.28) | copy-start | bytes 98308
  27.9 15.3 %copy-start.5 = (f32[2,8192]{1,0:T(2,128)S(1)}, f32[2,8192]{1,0:T(2,128)}, u32[]{:S(2)}) copy-start(f32[2,8192]{1,0:T(2,128)} %param.29) | copy-start | bytes 196612
  27.9 64.6 %all-to-all-start = ((bf16[128,2,64,128]{3,2,1,0:T(8,128)(2,1)}), bf16[128,2,64,128]{3,2,1,0:T(8,128)(2,1)}, u32[]{:S(2)}, u32[]{:S(2)}) async-start(bf16[128,2,64,128]{3,2,1,0:T(8,128)(2,1)} %bitcast.70), calls=%async_computation | async-start | bytes 8388608 | tf_op jit(solution)/shard_map/all_to_all | solution.py:410
  128.6 76.3 %all-to-all-start.1 = ((bf16[128,128,128]{2,1,0:T(8,128)(2,1)}), bf16[128,128,128]{2,1,0:T(8,128)(2,1)}, u32[]{:S(2)}, u32[]{:S(2)}) async-start(bf16[128,128,128]{2,1,0:T(8,128)(2,1)} %bitcast.68), calls=%async_computation.1 | async-start | bytes 8388608 | tf_op jit(solution)/shard_map/all_to_all | solution.py:410
  195.6 7.1 %copy-start = (bf16[256,64,128]{2,1,0:T(8,128)(2,1)S(1)}, bf16[256,64,128]{2,1,0:T(8,128)(2,1)}, u32[]{:S(2)}) copy-start(bf16[256,64,128]{2,1,0:T(8,128)(2,1)} %deposit.1) | copy-start | bytes 12582916
  197.5 5.1 %collective-permute-start.1 = (bf16[128,64,128]{2,1,0:T(8,128)(2,1)S(1)}, bf16[128,64,128]{2,1,0:T(8,128)(2,1)S(1)}, u32[]{:S(2)}, u32[]{:S(2)}) collective-permute-start(bf16[128,64,128]{2,1,0:T(8,128)(2,1)S(1)} %slice.28), channel_id=1, source_target_pairs={{0,1},{1,0},{2,3},{3,2},{4,5},{5,4},{6,7},{7,6},{8,9},{9,8},{10,11... | collective-permute-start | bytes 6291464 | tf_op jit(solution)/shard_map/ppermute | solution.py:415
  204.9 39.5 %all-to-all-start.2 = ((bf16[128,64,128]{2,1,0:T(8,128)(2,1)}), bf16[128,64,128]{2,1,0:T(8,128)(2,1)S(1)}, u32[]{:S(2)}, u32[]{:S(2)}) async-start(bf16[128,64,128]{2,1,0:T(8,128)(2,1)} %add_convert_fusion), calls=%async_computation.2 | async-start | bytes 4194304 | tf_op jit(solution)/shard_map/all_to_all | solution.py:410
  213.9 100.3 %collective-permute-start = (bf16[128,128,128]{2,1,0:T(8,128)(2,1)}, bf16[128,128,128]{2,1,0:T(8,128)(2,1)}, u32[]{:S(2)}, u32[]{:S(2)}) collective-permute-start(bf16[128,128,128]{2,1,0:T(8,128)(2,1)} %all-to-all-done.1.a_ref), channel_id=1, source_target_pairs={{0,1},{1,0},{2,3},{3,2},{4,5},{5,4},{6,7},{7,6},{8,9},{9,8},{10,11... | collective-permute-start | bytes 12582920 | tf_op jit(solution)/shard_map/ppermute | solution.py:415
  244.5 1.3 copy-start.1
  263.2 35.0 %all-to-all-start.3 = ((bf16[128,2,32,128]{3,2,1,0:T(8,128)(2,1)}), bf16[128,2,32,128]{3,2,1,0:T(8,128)(2,1)S(1)}, u32[]{:S(2)}, u32[]{:S(2)}) async-start(bf16[128,2,32,128]{3,2,1,0:T(8,128)(2,1)} %bitcast.72), calls=%async_computation.3 | async-start | bytes 4194304 | tf_op jit(solution)/shard_map/all_to_all | solution.py:410
  298.2 1.4 copy-start.2

commit v2 on v1

--- a/solution.py
+++ b/solution.py
@@ -10,6 +10,9 @@
 F32 = jnp.float32
 VLIM = 60 * 1024 * 1024
 NT = (((1,), (1,)), ((), ()))
+PAD = 72
+PAD2 = 136
+PAD3 = 40
 
 
 def cs(num, den, sign):
@@ -67,46 +70,52 @@
     def load(p, carry):
         at = pl.multiple_of(p * 128, 128)
         for c in range(2):
-            row = pl.multiple_of((c * 64 + p) * 64, 64)
+            row = pl.multiple_of((c * 64 + p) * PAD, 8)
             xs[pl.ds(row, 64), :] = s_ref[c, :, pl.ds(at, 128)].astype(F32)
         return carry
 
     lax.fori_loop(0, 64, load, 0, unroll=4)
     q = lax.broadcasted_iota(jnp.int32, (64, 128), 1).astype(F32)
 
-    def rows(r, carry):
-        x = xs[pl.ds(r, 128, stride=64), :].astype(BF)
-        z = jnp.dot(g_ref[...], x, preferred_element_type=F32)
+    def rows(n, carry):
+        x = jnp.concatenate([xs[pl.ds(2 * n + h, 128, stride=PAD), :].astype(BF) for h in range(2)], axis=1)
+        both = jnp.dot(g_ref[...], x, preferred_element_type=F32)
         tc = tc_ref[...]
         ts = ts_ref[...]
-        are, aim, bre, bim = z[:64], z[64:128], z[128:192], z[192:]
-        ure = bre + q * are
-        uim = bim + q * aim
-        wa = wa_ref[0, r]
-        base = pl.multiple_of(r * 128, 128)
-        vre = are * tc - aim * ts
-        vim = are * ts + aim * tc
-        tre[pl.ds(base, 64), :] = ure * ts + uim * tc
-        tim[pl.ds(base, 64), :] = uim * ts - ure * tc
-        tre[pl.ds(base + 64, 64), :] = -wa * vim
-        tim[pl.ds(base + 64, 64), :] = wa * vre
-        return carry
-
-    lax.fori_loop(0, 64, rows, 0, unroll=2)
-
-    def cols(t, carry):
+        for h in range(2):
+            r = 2 * n + h
+            z = both[:, h * 128 : h * 128 + 128]
+            are, aim, bre, bim = z[:64], z[64:128], z[128:192], z[192:]
+            ure = bre + q * are
+            uim = bim + q * aim
+            wa = wa_ref[0, r]
+            base = pl.multiple_of(r * PAD2, 8)
+            vre = are * tc - aim * ts
+            vim = are * ts + aim * tc
+            tre[pl.ds(base, 64), :] = ure * ts + uim * tc
+            tim[pl.ds(base, 64), :] = uim * ts - ure * tc
+            tre[pl.ds(base + 64, 64), :] = -wa * vim
+            tim[pl.ds(base + 64, 64), :] = wa * vre
+        return carry
+
+    lax.fori_loop(0, 32, rows, 0, unroll=2)
+
+    def cols(n, carry):
         parts = []
-        for f in range(2):
-            at = pl.ds(f * 64 + t, 64, stride=128)
-            parts.append(jnp.concatenate([tre[at, :].astype(BF), tim[at, :].astype(BF)], axis=1))
+        for h in range(2):
+            for f in range(2):
+                at = pl.ds(f * 64 + 2 * n + h, 64, stride=PAD2)
+                parts.append(jnp.concatenate([tre[at, :].astype(BF), tim[at, :].astype(BF)], axis=1))
         m = jnp.concatenate(parts, axis=0)
-        of[pl.ds(t, 256, stride=64), :] = lax.dot_general(w2_ref[...], m, NT, preferred_element_type=F32)
-        return carry
-
-    lax.fori_loop(0, 64, cols, 0, unroll=2)
+        out = lax.dot_general(w2_ref[...], m, NT, preferred_element_type=F32)
+        for h in range(2):
+            of[pl.ds(2 * n + h, 256, stride=PAD), :] = out[:, h * 128 : h * 128 + 128]
+        return carry
+
+    lax.fori_loop(0, 32, cols, 0, unroll=2)
 
     def store(i, carry):
-        o_ref[i] = of[pl.ds(pl.multiple_of(i * 64, 64), 64), :].astype(BF)
+        o_ref[i] = of[pl.ds(pl.multiple_of(i * PAD, 8), 64), :].astype(BF)
         return carry
 
     lax.fori_loop(0, 256, store, 0, unroll=8)
@@ -134,7 +143,8 @@
         stream_send_kernel,
         jax.ShapeDtypeStruct((256, 64, 128), BF),
         [SM] + [VM] * 5,
-        [pltpu.VMEM((8192, 128), F32)] * 3 + [pltpu.VMEM((16384, 128), F32)],
+        [pltpu.VMEM((128 * PAD, 128), F32)] + [pltpu.VMEM((64 * PAD2, 128), F32)] * 2
+        + [pltpu.VMEM((256 * PAD, 128), F32)],
         int(6e9), "stream_send",
         wa, stream, *send_tables(1.0, True),
     )
@@ -142,27 +152,34 @@
 
 def stream_recv_kernel(x_ref, w1_ref, tc_ref, ts_ref, v_ref, o_ref, xf, of):
     def load(i, carry):
-        xf[pl.ds(pl.multiple_of(i * 64, 64), 64), :] = x_ref[i].astype(F32)
+        xf[pl.ds(pl.multiple_of(i * PAD, 8), 64), :] = x_ref[i].astype(F32)
         return carry
 
     lax.fori_loop(0, 256, load, 0, unroll=8)
 
-    def step(t, carry):
-        d = xf[pl.ds(t, 256, stride=64), :].astype(BF)
+    def step(n, carry):
+        d = jnp.concatenate([xf[pl.ds(2 * n + h, 256, stride=PAD), :].astype(BF) for h in range(2)], axis=1)
         z = jnp.dot(w1_ref[...], d, preferred_element_type=F32)
-        re, im = z[:128], z[128:]
         tc = tc_ref[...]
         ts = ts_ref[...]
-        m = jnp.concatenate([(re * tc - im * ts).astype(BF), (re * ts + im * tc).astype(BF)], axis=1)
+        parts = []
+        for h in range(2):
+            re = z[:128, h * 128 : h * 128 + 128]
+            im = z[128:, h * 128 : h * 128 + 128]
+            parts.append(
+                jnp.concatenate([(re * tc - im * ts).astype(BF), (re * ts + im * tc).astype(BF)], axis=1)
+            )
+        m = jnp.concatenate(parts, axis=0)
         out = lax.dot_general(v_ref[...], m, NT, preferred_element_type=F32)
-        for f in range(2):
-            of[pl.ds(2 * t + f, 64, stride=128), :] = out[f * 64 : f * 64 + 64]
-        return carry
-
-    lax.fori_loop(0, 64, step, 0, unroll=2)
+        for h in range(2):
+            for f in range(2):
+                of[pl.ds(4 * n + 2 * h + f, 64, stride=PAD2), :] = out[f * 64 : f * 64 + 64, h * 128 : h * 128 + 128]
+        return carry
+
+    lax.fori_loop(0, 32, step, 0, unroll=2)
 
     def store(i, carry):
-        o_ref[i] = of[pl.ds(pl.multiple_of(i * 128, 128), 128), :].astype(BF)
+        o_ref[i] = of[pl.ds(pl.multiple_of(i * PAD2, 8), 128), :].astype(BF)
         return carry
 
     lax.fori_loop(0, 64, store, 0, unroll=4)
@@ -173,7 +190,7 @@
         stream_recv_kernel,
         jax.ShapeDtypeStruct((64, 128, 128), BF),
         [VM] * 5,
-        [pltpu.VMEM((16384, 128), F32), pltpu.VMEM((8192, 128), F32)],
+        [pltpu.VMEM((256 * PAD, 128), F32), pltpu.VMEM((64 * PAD2, 128), F32)],
         int(6e9), "stream_recv",
         x, *recv_tables(1.0, True),
     )
@@ -182,7 +199,7 @@
 def dye_send_kernel(idx_ref, dye_ref, ret_ref, g_ref, tc_ref, ts_ref, w2_ref, o_ref, xs, tre, tim, of):
     def load(p, carry):
         at = pl.multiple_of(p * 128, 128)
-        xs[pl.ds(pl.multiple_of(p * 64, 64), 64), :] = dye_ref[:, pl.ds(at, 128)].astype(F32)
+        xs[pl.ds(pl.multiple_of(p * PAD, 8), 64), :] = dye_ref[:, pl.ds(at, 128)].astype(F32)
         return carry
 
     lax.fori_loop(0, 64, load, 0, unroll=4)
@@ -197,39 +214,43 @@
             total = ret_ref[g * 8 + e].astype(F32)
             for x in range(1, 4):
                 total = total + ret_ref[g * 8 + 2 * x + e].astype(F32)
-            at = pl.ds(pl.multiple_of(tile * 64, 64), 64)
+            at = pl.ds(pl.multiple_of(tile * PAD, 8), 64)
             xs[at, :] = xs[at, :] + total
 
         return carry
 
     lax.fori_loop(0, 32, place, 0)
 
-    def rows(r, carry):
-        x = xs[pl.ds(r, 64, stride=64), :].astype(BF)
+    def rows(n, carry):
+        x = jnp.concatenate([xs[pl.ds(4 * n + h, 64, stride=PAD), :].astype(BF) for h in range(4)], axis=1)
         z = jnp.dot(g_ref[...], x, preferred_element_type=F32)
-        re, im = z[:64], z[64:]
         tc = tc_ref[...]
         ts = ts_ref[...]
-        base = pl.multiple_of(r * 64, 64)
-        tre[pl.ds(base, 64), :] = re * tc - im * ts
-        tim[pl.ds(base, 64), :] = re * ts + im * tc
-        return carry
-
-    lax.fori_loop(0, 64, rows, 0, unroll=2)
-
-    def cols(t, carry):
+        for h in range(4):
+            re = z[:64, h * 128 : h * 128 + 128]
+            im = z[64:, h * 128 : h * 128 + 128]
+            base = pl.multiple_of((4 * n + h) * PAD, 8)
+            tre[pl.ds(base, 64), :] = re * tc - im * ts
+            tim[pl.ds(base, 64), :] = re * ts + im * tc
+        return carry
+
+    lax.fori_loop(0, 16, rows, 0, unroll=2)
+
+    def cols(n, carry):
         parts = []
-        for e in range(2):
-            at = pl.ds(2 * t + e, 64, stride=64)
+        for e in range(4):
+            at = pl.ds(4 * n + e, 64, stride=PAD)
             parts.append(jnp.concatenate([tre[at, :].astype(BF), tim[at, :].astype(BF)], axis=1))
         m = jnp.concatenate(parts, axis=0)
-        of[pl.ds(t, 256, stride=32), :] = lax.dot_general(w2_ref[...], m, NT, preferred_element_type=F32)
-        return carry
-
-    lax.fori_loop(0, 32, cols, 0, unroll=2)
+        out = lax.dot_general(w2_ref[...], m, NT, preferred_element_type=F32)
+        for h in range(2):
+            of[pl.ds(2 * n + h, 256, stride=PAD3), :] = out[:, h * 128 : h * 128 + 128]
+        return carry
+
+    lax.fori_loop(0, 16, cols, 0, unroll=2)
 
     def store(i, carry):
-        o_ref[i] = of[pl.ds(pl.multiple_of(i * 32, 32), 32), :].astype(BF)
+        o_ref[i] = of[pl.ds(pl.multiple_of(i * PAD3, 8), 32), :].astype(BF)
         return carry
 
     lax.fori_loop(0, 256, store, 0, unroll=8)
@@ -240,7 +261,7 @@
         dye_send_kernel,
         jax.ShapeDtypeStruct((256, 32, 128), BF),
         [SM] + [VM] * 6,
-        [pltpu.VMEM((4096, 128), F32)] * 3 + [pltpu.VMEM((8192, 128), F32)],
+        [pltpu.VMEM((64 * PAD, 128), F32)] * 3 + [pltpu.VMEM((256 * PAD3, 128), F32)],
         int(4e9), "dye_send",
         idx, dye, ret, *send_tables(-1.0, False),
     )
@@ -248,26 +269,35 @@
 
 def dye_recv_kernel(x_ref, w1_ref, tc_ref, ts_ref, v_ref, o_ref, xf, of):
     def load(i, carry):
-        xf[pl.ds(pl.multiple_of(i * 32, 32), 32), :] = x_ref[i].astype(F32)
+        xf[pl.ds(pl.multiple_of(i * PAD3, 8), 32), :] = x_ref[i].astype(F32)
         return carry
 
     lax.fori_loop(0, 256, load, 0, unroll=8)
 
-    def step(t, carry):
-        d = xf[pl.ds(t, 256, stride=32), :].astype(BF)
+    def step(n, carry):
+        d = jnp.concatenate([xf[pl.ds(2 * n + h, 256, stride=PAD3), :].astype(BF) for h in range(2)], axis=1)
         z = jnp.dot(w1_ref[...], d, preferred_element_type=F32)
-        re, im = z[:128], z[128:]
         tc = tc_ref[...]
         ts = ts_ref[...]
-        m = jnp.concatenate([(re * tc - im * ts).astype(BF), (re * ts + im * tc).astype(BF)], axis=1)
+        parts = []
+        for h in range(2):
+            re = z[:128, h * 128 : h * 128 + 128]
+            im = z[128:, h * 128 : h * 128 + 128]
+            parts.append(
+                jnp.concatenate([(re * tc - im * ts).astype(BF), (re * ts + im * tc).astype(BF)], axis=1)
+            )
+        m = jnp.concatenate(parts, axis=0)
         out = lax.dot_general(v_ref[...], m, NT, preferred_element_type=F32)
-        for c in range(2):
-            for e in range(2):
-                row = c * 4096 + (t // 4) * 512 + (2 * t + e) % 8
-                of[pl.ds(row, 64, stride=8), :] = out[(2 * c + e) * 64 : (2 * c + e) * 64 + 64]
-        return carry
-
-    lax.fori_loop(0, 32, step, 0, unroll=2)
+        for h in range(2):
+            for c in range(2):
+                for e in range(2):
+                    row = c * 4096 + (n // 2) * 512 + (4 * n + 2 * h + e) % 8
+                    of[pl.ds(row, 64, stride=8), :] = out[
+                        (2 * c + e) * 64 : (2 * c + e) * 64 + 64, h * 128 : h * 128 + 128
+                    ]
+        return carry
+
+    lax.fori_loop(0, 16, step, 0, unroll=2)
 
     def store(n, carry):
         c = n // 8
@@ -286,7 +316,7 @@
         dye_recv_kernel,
         jax.ShapeDtypeStruct((2, 64, 8192), F32),
         [VM] * 5,
-        [pltpu.VMEM((8192, 128), F32)] * 2,
+        [pltpu.VMEM((256 * PAD3, 128), F32), pltpu.VMEM((8192, 128), F32)],
         int(4e9), "dye_recv",
         x, *recv_tables(-1.0, False),
     )
@@ -294,7 +324,7 @@
 CAPO = 2
 
 
-def deposit_kernel(mb_ref, nb_ref, fy_ref, fx_ref, am_ref, o_ref, m_ref, acc):
+def deposit_kernel(mb_ref, nb_ref, fy_ref, fx_ref, am_ref, keep_ref, send_ref, m_ref, acc):
     step = pl.program_id(0)
     width = mb_ref.shape[1]
     am = am_ref[...]
@@ -322,31 +352,34 @@
 
     @pl.when(step == 0)
     def _():
-        lax.fori_loop(0, 8, lambda i, c: (part(i, True), c)[1], 0)
+        lax.fori_loop(0, 8, lambda i, c: (part(i, True), c)[1], 0, unroll=2)
 
     @pl.when(step > 0)
     def _():
-        lax.fori_loop(0, 8, lambda i, c: (part(i, False), c)[1], 0)
+        lax.fori_loop(0, 8, lambda i, c: (part(i, False), c)[1], 0, unroll=2)
 
     @pl.when(step == pl.num_programs(0) - 1)
     def _():
         def store(p, carry):
             row = pl.multiple_of((p // 8) * 64, 64)
             for h in range(2):
-                o_ref[p // 8 * 16 + p % 8 * 2 + h] = acc[p % 8, pl.ds(row, 64), h * 128 : h * 128 + 128].astype(BF)
+                lanes = slice(h * 128, h * 128 + 128)
+                at = p // 8 * 16 + p % 8 * 2 + h
+                keep_ref[at] = acc[p % 8, pl.ds(row, 64), lanes].astype(BF)
+                send_ref[at] = acc[p % 8, pl.ds(row + 512, 64), lanes].astype(BF)
             return carry
 
-        lax.fori_loop(0, 128, store, 0, unroll=4)
-
-
-def deposit(mb, nb, fy, fx, am, width=1024):
+        lax.fori_loop(0, 64, store, 0, unroll=4)
+
+
+def deposit(mb, nb, fy, fx, am, width=2048):
     blk = pl.BlockSpec((1, width), lambda i: (0, i))
     return pl.pallas_call(
         deposit_kernel,
         grid=(8192 // width,),
-        out_shape=jax.ShapeDtypeStruct((256, 64, 128), BF),
+        out_shape=[jax.ShapeDtypeStruct((128, 64, 128), BF)] * 2,
         in_specs=[blk] * 5,
-        out_specs=pl.BlockSpec((256, 64, 128), lambda i: (0, 0, 0)),
+        out_specs=[pl.BlockSpec((128, 64, 128), lambda i: (0, 0, 0))] * 2,
         scratch_shapes=[pltpu.VMEM((1024, width), BF), pltpu.VMEM((8, 1024, 256), F32)],
         compiler_params=pltpu.CompilerParams(vmem_limit_bytes=VLIM),
         cost_estimate=pl.CostEstimate(flops=int(34e9), bytes_accessed=4 << 20, transcendentals=0),
@@ -444,25 +477,29 @@
     flat = lambda x: x.reshape(1, 8192)
     fy = float_frac[0:1]
     fx = float_frac[1:2]
-    dep = deposit(
-        flat(pos // 16 * 64 + row), flat(pos % 16 * 128 + col), fy, fx, flat(float_dye)
-    )
-    dep = (dep[:128].astype(F32) + swap_cores(dep[128:]).astype(F32)).astype(BF)
+    rows = flat(pos // 16 * 64 + row)
+    cols = flat(pos % 16 * 128 + col)
+
+    spec = stream_send(stream_hat, wave)
+    spec, rows, cols = lax.optimization_barrier((spec, rows, cols))
+    spec = spread(spec.reshape(128, 2, 64, 128)).reshape(256, 64, 128)
+    keep, send = deposit(rows, cols, fy, fx, flat(float_dye))
+    dep = (keep.astype(F32) + swap_cores(send).astype(F32)).astype(BF)
+    spec, dep = lax.optimization_barrier((spec, dep))
     returned = spread(dep)
 
-    spec = stream_send(stream_hat, wave)
-    spec = spread(spec.reshape(128, 2, 64, 128)).reshape(256, 64, 128)
     tiles = stream_recv(spec)
     outgoing = tiles[jnp.maximum(send_index, 0)]
     outgoing = jnp.broadcast_to(outgoing[:, None], (16, 4, 2, 128, 128)).reshape(128, 128, 128)
+    outgoing, returned = lax.optimization_barrier((outgoing, returned))
     own = spread(outgoing)
+    front = dye_send(send_index.reshape(1, 32), dye, returned)
+    own, front = lax.optimization_barrier((own, front))
     other = swap_cores(own)
-
-    front = dye_send(send_index.reshape(1, 32), dye, returned)
     front = spread(front.reshape(128, 2, 32, 128)).reshape(256, 32, 128)
+    velocity = gather(pos * 128 + 2 * row, own, other, flat(float_col), fy, fx)
+    velocity, front = lax.optimization_barrier((velocity, front))
     dye_hat = dye_recv(front)
-
-    velocity = gather(pos * 128 + 2 * row, own, other, flat(float_col), fy, fx)
     return (velocity, dye_hat)
 
 

time: 339 us -> 237 us (0.70)
  Pallas kernels: 175 us -> 117 us
  waiting for transfers between devices: 111 us -> 68.1 us
  other arithmetic: 6.28 us -> 10.1 us
    pallas_call x5, Pallas kernels: 113 us -> 67 us  [call(): pl.pallas_call(kernel, out_shape=outs, in_specs=specs, out_specs=jax.tree...]
    all_to_all x4, waiting for transfers between devices: 107 us -> 61.6 us  [spread(): return lax.all_to_all(blocks, AXES, split_axis=0, concat_axis=0, tiled=True)]
    pallas_call x1, Pallas kernels: 61.4 us -> 49.8 us  [deposit(): pl.pallas_call(deposit_kernel, grid=(8192 // width,), out_shape=[jax.Shap...]
  transfers between devices with their start and end apart: 6 -> 6, of which waited for: 4 -> 5; matrix products, arithmetic and copies ran while one was open for 3% -> 4% of each run, Pallas kernels for 28% -> 40%
where the time goes in v2:
time: 237 us
  Pallas kernels  117 us (49%)
  waiting for transfers between devices  68.1 us (29%)
  starting transfers between devices  32.5 us (14%)
  other arithmetic  10.1 us (4%)
  local copies, waits for them, and re-layouts  8.47 us (4%)
    pallas_call x5, Pallas kernels, call(): pl.pallas_call(kernel, out_shape=outs, in_specs=specs, out_specs=jax.tree...  67 us
    all_to_all x4, waiting for transfers between devices, spread(): return lax.all_to_all(blocks, AXES, split_axis=0, concat_axis=0, tiled=True)  61.6 us
    pallas_call x1, Pallas kernels, deposit(): pl.pallas_call(deposit_kernel, grid=(8192 // width,), out_shape=[jax.Shap...  49.8 us
    all_to_all x4, starting transfers between devices, spread(): return lax.all_to_all(blocks, AXES, split_axis=0, concat_axis=0, tiled=True)  30.4 us
    ppermute x2, waiting for transfers between devices, swap_cores(): return lax.ppermute(x, 'narrow', [(i, i ^ 1) for i in range(n)])  6.52 us
  transfers between devices with their start and end apart: 6, of which 5 were waited for; matrix products, arithmetic and copies ran while one was open for 4% of the time, Pallas kernels for 40%

profile of v2, /device:TPU:1, one launch (start us, length us, event | category | flops | bytes accessed | tf_op | source)
XLA Modules:
  0.0 236.7 jit_solution(11785087377676640654)
XLA Ops:
  0.6 0.5 fusion.14.wa_ref
  1.2 0.7 and_select_fusion
  1.9 0.2 convert_reduce_fusion
  2.1 1.8 select_reduce_fusion
  4.0 1.4 fusion.4
  5.4 13.4 %stream_send.1 = bf16[256,64,128]{2,1,0:T(8,128)(2,1)} custom-call(f32[1,64]{1,0:T(1,128)} %fusion.14.wa_ref, bf16[2,64,8192]{2,1,0:T(8,128)(2,1)} %s_ref.1, bf16[256,128]{1,0:T(8,128)(2,1)} %constant.139.clone.g_ref, f32[64,128]{1,0:T(8,128)} %constant.140.clone.tc_ref, f32[64,128]{1,0:T(8,128)} %constant.141.clone.ts_ref, ...), custom_call_target="tpu_custom_call" | custom-call | flops 6000000000 | bytes 1048576 | tf_op jit(solution)/shard_map/stream_send/pallas_call | solution.py:129
  18.8 0.0 copy-start.4
  18.8 12.0 %all-to-all-start = ((bf16[128,2,64,128]{3,2,1,0:T(8,128)(2,1)}), bf16[128,2,64,128]{3,2,1,0:T(8,128)(2,1)}, u32[]{:S(2)}, u32[]{:S(2)}) async-start(bf16[128,2,64,128]{3,2,1,0:T(8,128)(2,1)} %bitcast.70), calls=%async_computation | async-start | bytes 8388608 | tf_op jit(solution)/shard_map/all_to_all | solution.py:443
  30.8 0.0 copy-done.4
  30.8 0.7 fusion.15
  31.4 49.8 %deposit.1 = (bf16[128,64,128]{2,1,0:T(8,128)(2,1)}, bf16[128,64,128]{2,1,0:T(8,128)(2,1)}) custom-call(s32[1,8192]{1,0:T(1,128)} %bitcast.76, s32[1,8192]{1,0:T(1,128)} %bitcast.75, f32[1,8192]{1,0:T(1,128)} %get-tuple-element.35.fy_ref, f32[1,8192]{1,0:T(1,128)} %get-tuple-element.34.fx_ref, f32[1,8192]{1,0:T(1,128)} %bitcast.85), custom_call_target="tpu_custom_call" | custom-call | flops 33999998976 | bytes 4194304 | tf_op jit(solution)/shard_map/deposit/pallas_call | solution.py:377
  81.2 1.1 collective-permute-start
  82.4 4.0 %collective-permute-done = bf16[128,64,128]{2,1,0:T(8,128)(2,1)S(1)} collective-permute-done((bf16[128,64,128]{2,1,0:T(8,128)(2,1)}, bf16[128,64,128]{2,1,0:T(8,128)(2,1)S(1)}, u32[]{:S(2)}, u32[]{:S(2)}) %collective-permute-start) | collective-permute-done | bytes 2097184 | tf_op jit(solution)/shard_map/ppermute | solution.py:448
  86.4 0.0 copy-start.3
  86.4 3.9 %add_convert_fusion = bf16[128,64,128]{2,1,0:T(8,128)(2,1)} fusion(bf16[128,64,128]{2,1,0:T(8,128)(2,1)S(1)} %collective-permute-done, bf16[128,64,128]{2,1,0:T(8,128)(2,1)} %get-tuple-element.18), kind=kLoop, calls=%fused_computation.3 | loop fusion | flops 4194304 | bytes 6291456 | tf_op jit(solution)/shard_map/convert_element_type | solution.py:487
  90.3 0.0 all-to-all-done
  90.3 9.0 %all-to-all-start.1 = ((bf16[128,64,128]{2,1,0:T(8,128)(2,1)}), bf16[128,64,128]{2,1,0:T(8,128)(2,1)S(1)}, u32[]{:S(2)}, u32[]{:S(2)}) async-start(bf16[128,64,128]{2,1,0:T(8,128)(2,1)} %add_convert_fusion), calls=%async_computation.1 | async-start | bytes 4194304 | tf_op jit(solution)/shard_map/all_to_all | solution.py:443
  99.3 0.0 copy-done.3
  99.3 0.6 reduce-window.6
  99.9 0.2 slice_reduce_fusion
  100.1 0.1 compare_bitcast_fusion
  100.2 0.1 select_reduce_fusion.2
  100.4 0.1 copy.44
  100.4 0.1 reshape.235
  100.6 12.2 %stream_recv.1 = bf16[64,128,128]{2,1,0:T(8,128)(2,1)} custom-call(bf16[256,64,128]{2,1,0:T(8,128)(2,1)} %bitcast.8.x_ref, bf16[256,256]{1,0:T(8,128)(2,1)} %constant.143.clone.w1_ref, f32[128,128]{1,0:T(8,128)} %constant.144.clone.tc_ref, f32[128,128]{1,0:T(8,128)} %constant.145.clone.ts_ref, bf16[128,256]{1,0:T(8,128)(2,1)} %constant.146.clone.v_ref), custom_call_target="tpu_custom_call" | custom-call | flops 6000000000 | bytes 1048576 | tf_op jit(solution)/shard_map/stream_recv/pallas_call | solution.py:129
  112.8 2.3 gather_fusion
  115.1 14.7 %all-to-all-done.1.ret_ref = bf16[128,64,128]{2,1,0:T(8,128)(2,1)S(1)} async-done(((bf16[128,64,128]{2,1,0:T(8,128)(2,1)}), bf16[128,64,128]{2,1,0:T(8,128)(2,1)S(1)}, u32[]{:S(2)}, u32[]{:S(2)}) %all-to-all-start.1) | async-done | bytes 2097184 | tf_op jit(solution)/shard_map/all_to_all | solution.py:443
  129.8 0.0 copy-start
  129.8 3.1 %broadcast_in_dim.40 = bf16[16,4,2,128,128]{4,3,2,1,0:T(8,128)(2,1)} broadcast(bf16[16,2,128,128]{3,2,1,0:T(8,128)(2,1)S(1)} %bitcast.69), dimensions={0,2,3,4} | broadcast | bytes 5242880 | tf_op jit(solution)/shard_map/broadcast_in_dim | solution.py:493
  132.8 0.0 copy-done
  132.9 5.5 %all-to-all-start.2 = ((bf16[128,128,128]{2,1,0:T(8,128)(2,1)}), bf16[128,128,128]{2,1,0:T(8,128)(2,1)}, u32[]{:S(2)}, u32[]{:S(2)}) async-start(bf16[128,128,128]{2,1,0:T(8,128)(2,1)} %bitcast.68), calls=%async_computation.2 | async-start | bytes 8388608 | tf_op jit(solution)/shard_map/all_to_all | solution.py:443
  138.4 0.1 copy.45
  138.4 0.6 sub.43.idx_ref
  139.0 8.7 %dye_send.1 = bf16[256,32,128]{2,1,0:T(8,128)(2,1)} custom-call(s32[1,32]{1,0:T(1,128)} %sub.43.idx_ref, bf16[64,8192]{1,0:T(8,128)(2,1)} %dye_ref.1, bf16[128,64,128]{2,1,0:T(8,128)(2,1)} %copy-done, bf16[128,64]{1,0:T(8,128)(2,1)} %constant.147.clone.g_ref, f32[64,128]{1,0:T(8,128)} %constant.140.clone.tc_ref, f32[64,128]{1,0:T(8,128)} %constant.148.clone.ts_ref, ...), custom_call_target="tpu_custom_call" | custom-call | flops 4000000000 | bytes 1048576 | tf_op jit(solution)/shard_map/dye_send/pallas_call | solution.py:129
  147.8 0.0 copy-start.2
  147.8 43.3 %all-to-all-done.2.a_ref = bf16[128,128,128]{2,1,0:T(8,128)(2,1)} async-done(((bf16[128,128,128]{2,1,0:T(8,128)(2,1)}), bf16[128,128,128]{2,1,0:T(8,128)(2,1)}, u32[]{:S(2)}, u32[]{:S(2)}) %all-to-all-start.2) | async-done | bytes 4194336 | tf_op jit(solution)/shard_map/all_to_all | solution.py:443
  191.1 0.9 collective-permute-start.1
  192.0 4.0 %all-to-all-start.3 = ((bf16[128,2,32,128]{3,2,1,0:T(8,128)(2,1)}), bf16[128,2,32,128]{3,2,1,0:T(8,128)(2,1)S(1)}, u32[]{:S(2)}, u32[]{:S(2)}) async-start(bf16[128,2,32,128]{3,2,1,0:T(8,128)(2,1)} %bitcast.71), calls=%async_computation.3 | async-start | bytes 4194304 | tf_op jit(solution)/shard_map/all_to_all | solution.py:443
  196.0 0.0 copy-done.2
  196.0 0.6 bitcast_add_fusion.base_ref
  196.7 2.5 %collective-permute-done.1.b_ref = bf16[128,128,128]{2,1,0:T(8,128)(2,1)} collective-permute-done((bf16[128,128,128]{2,1,0:T(8,128)(2,1)}, bf16[128,128,128]{2,1,0:T(8,128)(2,1)}, u32[]{:S(2)}, u32[]{:S(2)}) %collective-permute-start.1) | collective-permute-done | bytes 4194336 | tf_op jit(solution)/shard_map/ppermute | solution.py:448
  199.2 23.8 %gather.7 = f32[2,8192]{1,0:T(2,128)} custom-call(s32[64,128]{1,0:T(8,128)} %bitcast_add_fusion.base_ref, bf16[128,128,128]{2,1,0:T(8,128)(2,1)} %all-to-all-done.2.a_ref, bf16[128,128,128]{2,1,0:T(8,128)(2,1)} %collective-permute-done.1.b_ref, s32[1,8192]{1,0:T(1,128)} %bitcast.74, f32[1,8192]{1,0:T(1,128)} %get-tuple-element.35.fy_ref, ...), custom_call_target="tpu_custom_call" | custom-call | flops 20000000000 | bytes 1048576 | tf_op jit(solution)/shard_map/gather/pallas_call | solution.py:129
  223.0 3.6 %all-to-all-done.3 = bf16[128,2,32,128]{3,2,1,0:T(8,128)(2,1)S(1)} async-done(((bf16[128,2,32,128]{3,2,1,0:T(8,128)(2,1)}), bf16[128,2,32,128]{3,2,1,0:T(8,128)(2,1)S(1)}, u32[]{:S(2)}, u32[]{:S(2)}) %all-to-all-start.3) | async-done | bytes 2097184 | tf_op jit(solution)/shard_map/all_to_all | solution.py:443
  226.5 0.0 copy-start.1
  226.5 1.3 copy-done.1
  227.9 8.8 %dye_recv.1 = f32[2,64,8192]{2,1,0:T(8,128)} custom-call(bf16[256,32,128]{2,1,0:T(8,128)(2,1)} %bitcast.72, bf16[256,256]{1,0:T(8,128)(2,1)} %constant.150.clone.w1_ref, f32[128,128]{1,0:T(8,128)} %constant.144.clone.tc_ref, f32[128,128]{1,0:T(8,128)} %constant.151.clone.ts_ref, bf16[256,256]{1,0:T(8,128)(2,1)} %constant.152.clone.v_ref), custom_call_target="tpu_custom_call" | custom-call | flops 4000000000 | bytes 1048576 | tf_op jit(solution)/shard_map/dye_recv/pallas_call | solution.py:129
  (9 shorter events, 0.1 us)
Async XLA Ops:
  18.8 12.0 %copy-start.4 = (f32[2,8192]{1,0:T(2,128)S(1)}, f32[2,8192]{1,0:T(2,128)}, u32[]{:S(2)}) copy-start(f32[2,8192]{1,0:T(2,128)} %param.29) | copy-start | bytes 196612
  18.8 71.5 %all-to-all-start = ((bf16[128,2,64,128]{3,2,1,0:T(8,128)(2,1)}), bf16[128,2,64,128]{3,2,1,0:T(8,128)(2,1)}, u32[]{:S(2)}, u32[]{:S(2)}) async-start(bf16[128,2,64,128]{3,2,1,0:T(8,128)(2,1)} %bitcast.70), calls=%async_computation | async-start | bytes 8388608 | tf_op jit(solution)/shard_map/all_to_all | solution.py:443
  81.2 5.1 %collective-permute-start = (bf16[128,64,128]{2,1,0:T(8,128)(2,1)}, bf16[128,64,128]{2,1,0:T(8,128)(2,1)S(1)}, u32[]{:S(2)}, u32[]{:S(2)}) collective-permute-start(bf16[128,64,128]{2,1,0:T(8,128)(2,1)} %get-tuple-element.19), channel_id=1, source_target_pairs={{0,1},{1,0},{2,3},{3,2},{4,5},{5,4},{6,7},{7,6},{8,9},{9,8},{10,11... | collective-permute-start | bytes 6291464 | tf_op jit(solution)/shard_map/ppermute | solution.py:448
  86.4 12.9 %copy-start.3 = (s32[16,256]{1,0:T(8,128)S(1)}, s32[16,256]{1,0:T(8,128)}, u32[]{:S(2)}) copy-start(s32[16,256]{1,0:T(8,128)} %param.31) | copy-start | bytes 49156
  90.3 39.5 %all-to-all-start.1 = ((bf16[128,64,128]{2,1,0:T(8,128)(2,1)}), bf16[128,64,128]{2,1,0:T(8,128)(2,1)S(1)}, u32[]{:S(2)}, u32[]{:S(2)}) async-start(bf16[128,64,128]{2,1,0:T(8,128)(2,1)} %add_convert_fusion), calls=%async_computation.1 | async-start | bytes 4194304 | tf_op jit(solution)/shard_map/all_to_all | solution.py:443
  129.8 3.1 %copy-start = (bf16[128,64,128]{2,1,0:T(8,128)(2,1)}, bf16[128,64,128]{2,1,0:T(8,128)(2,1)S(1)}, u32[]{:S(2)}) copy-start(bf16[128,64,128]{2,1,0:T(8,128)(2,1)S(1)} %all-to-all-done.1.ret_ref) | copy-start | bytes 6291460
  132.9 58.3 %all-to-all-start.2 = ((bf16[128,128,128]{2,1,0:T(8,128)(2,1)}), bf16[128,128,128]{2,1,0:T(8,128)(2,1)}, u32[]{:S(2)}, u32[]{:S(2)}) async-start(bf16[128,128,128]{2,1,0:T(8,128)(2,1)} %bitcast.68), calls=%async_computation.2 | async-start | bytes 8388608 | tf_op jit(solution)/shard_map/all_to_all | solution.py:443
  147.8 48.2 %copy-start.2 = (s32[8192]{0:T(1024)S(1)}, s32[8192]{0:T(1024)}, u32[]{:S(2)}) copy-start(s32[8192]{0:T(1024)} %param.27) | copy-start | bytes 98308
  191.1 8.1 %collective-permute-start.1 = (bf16[128,128,128]{2,1,0:T(8,128)(2,1)}, bf16[128,128,128]{2,1,0:T(8,128)(2,1)}, u32[]{:S(2)}, u32[]{:S(2)}) collective-permute-start(bf16[128,128,128]{2,1,0:T(8,128)(2,1)} %all-to-all-done.2.a_ref), channel_id=1, source_target_pairs={{0,1},{1,0},{2,3},{3,2},{4,5},{5,4},{6,7},{7,6},{8,9},{9,8},{10,11... | collective-permute-start | bytes 12582920 | tf_op jit(solution)/shard_map/ppermute | solution.py:448
  192.0 34.5 %all-to-all-start.3 = ((bf16[128,2,32,128]{3,2,1,0:T(8,128)(2,1)}), bf16[128,2,32,128]{3,2,1,0:T(8,128)(2,1)S(1)}, u32[]{:S(2)}, u32[]{:S(2)}) async-start(bf16[128,2,32,128]{3,2,1,0:T(8,128)(2,1)} %bitcast.71), calls=%async_computation.3 | async-start | bytes 4194304 | tf_op jit(solution)/shard_map/all_to_all | solution.py:443
  226.5 1.3 copy-start.1

commit v3 on v2

--- a/solution.py
+++ b/solution.py
@@ -8,7 +8,6 @@
 
 BF = jnp.bfloat16
 F32 = jnp.float32
-VLIM = 60 * 1024 * 1024
 NT = (((1,), (1,)), ((), ()))
 PAD = 72
 PAD2 = 136
@@ -125,14 +124,14 @@
 SM = pl.BlockSpec(memory_space=pltpu.SMEM)
 
 
-def call(kernel, outs, specs, scratch, cost, name, *args):
+def call(kernel, outs, specs, scratch, cost, mib, name, *args):
     return pl.pallas_call(
         kernel,
         out_shape=outs,
         in_specs=specs,
         out_specs=jax.tree.map(lambda _: VM, outs),
         scratch_shapes=scratch,
-        compiler_params=pltpu.CompilerParams(vmem_limit_bytes=VLIM),
+        compiler_params=pltpu.CompilerParams(vmem_limit_bytes=mib << 20),
         cost_estimate=pl.CostEstimate(flops=cost, bytes_accessed=1 << 20, transcendentals=0),
         name=name,
     )(*args)
@@ -145,12 +144,12 @@
         [SM] + [VM] * 5,
         [pltpu.VMEM((128 * PAD, 128), F32)] + [pltpu.VMEM((64 * PAD2, 128), F32)] * 2
         + [pltpu.VMEM((256 * PAD, 128), F32)],
-        int(6e9), "stream_send",
+        int(6e9), 36, "stream_send",
         wa, stream, *send_tables(1.0, True),
     )
 
 
-def stream_recv_kernel(x_ref, w1_ref, tc_ref, ts_ref, v_ref, o_ref, xf, of):
+def stream_recv_kernel(idx_ref, x_ref, w1_ref, tc_ref, ts_ref, v_ref, o_ref, xf, of):
     def load(i, carry):
         xf[pl.ds(pl.multiple_of(i * PAD, 8), 64), :] = x_ref[i].astype(F32)
         return carry
@@ -178,21 +177,24 @@
 
     lax.fori_loop(0, 32, step, 0, unroll=2)
 
-    def store(i, carry):
-        o_ref[i] = of[pl.ds(pl.multiple_of(i * PAD2, 8), 128), :].astype(BF)
-        return carry
-
-    lax.fori_loop(0, 64, store, 0, unroll=4)
-
-
-def stream_recv(x):
+    def store(n, carry):
+        tile = jnp.maximum(idx_ref[0, n], 0)
+        data = of[pl.ds(pl.multiple_of(tile * PAD2, 8), 128), :].astype(BF)
+        for x in range(4):
+            o_ref[n // 2 * 8 + 2 * x + n % 2] = data
+        return carry
+
+    lax.fori_loop(0, 32, store, 0, unroll=2)
+
+
+def stream_recv(idx, x):
     return call(
         stream_recv_kernel,
-        jax.ShapeDtypeStruct((64, 128, 128), BF),
-        [VM] * 5,
+        jax.ShapeDtypeStruct((128, 128, 128), BF),
+        [SM] + [VM] * 5,
         [pltpu.VMEM((256 * PAD, 128), F32), pltpu.VMEM((64 * PAD2, 128), F32)],
-        int(6e9), "stream_recv",
-        x, *recv_tables(1.0, True),
+        int(6e9), 28, "stream_recv",
+        idx, x, *recv_tables(1.0, True),
     )
 
 
@@ -262,7 +264,7 @@
         jax.ShapeDtypeStruct((256, 32, 128), BF),
         [SM] + [VM] * 6,
         [pltpu.VMEM((64 * PAD, 128), F32)] * 3 + [pltpu.VMEM((256 * PAD3, 128), F32)],
-        int(4e9), "dye_send",
+        int(4e9), 24, "dye_send",
         idx, dye, ret, *send_tables(-1.0, False),
     )
 
@@ -317,93 +319,98 @@
         jax.ShapeDtypeStruct((2, 64, 8192), F32),
         [VM] * 5,
         [pltpu.VMEM((256 * PAD3, 128), F32), pltpu.VMEM((8192, 128), F32)],
-        int(4e9), "dye_recv",
+        int(4e9), 20, "dye_recv",
         x, *recv_tables(-1.0, False),
     )
 
 CAPO = 2
 
 
-def deposit_kernel(mb_ref, nb_ref, fy_ref, fx_ref, am_ref, keep_ref, send_ref, m_ref, acc):
-    step = pl.program_id(0)
-    width = mb_ref.shape[1]
-    am = am_ref[...]
-    hi = am * fy_ref[...]
-    lo = am - hi
-    mb = mb_ref[...]
-    nb = nb_ref[...]
-    fx = fx_ref[...]
-    gx = 1.0 - fx
-
-    def build_m(i, carry):
-        at = pl.multiple_of(i * 64, 64)
-        d = lax.broadcasted_iota(jnp.int32, (64, width), 0) + (i * 64 - mb)
-        w = jnp.where(d == 0, lo, jnp.where(d == 1, hi, 0.0))
-        m_ref[pl.ds(at, 64), :] = w.astype(BF)
-        return carry
-
-    lax.fori_loop(0, 16, build_m, 0)
-
-    def part(i, first):
-        d = lax.broadcasted_iota(jnp.int32, (256, width), 0) + (i * 256 - nb)
-        w = jnp.where(d == 0, gx, jnp.where(d == 1, fx, 0.0)).astype(BF)
-        z = lax.dot_general(m_ref[...], w, NT, preferred_element_type=F32)
-        acc[i] = z if first else acc[i] + z
-
-    @pl.when(step == 0)
-    def _():
-        lax.fori_loop(0, 8, lambda i, c: (part(i, True), c)[1], 0, unroll=2)
-
-    @pl.when(step > 0)
-    def _():
-        lax.fori_loop(0, 8, lambda i, c: (part(i, False), c)[1], 0, unroll=2)
-
-    @pl.when(step == pl.num_programs(0) - 1)
-    def _():
-        def store(p, carry):
-            row = pl.multiple_of((p // 8) * 64, 64)
-            for h in range(2):
-                lanes = slice(h * 128, h * 128 + 128)
-                at = p // 8 * 16 + p % 8 * 2 + h
-                keep_ref[at] = acc[p % 8, pl.ds(row, 64), lanes].astype(BF)
-                send_ref[at] = acc[p % 8, pl.ds(row + 512, 64), lanes].astype(BF)
-            return carry
-
-        lax.fori_loop(0, 64, store, 0, unroll=4)
-
-
-def deposit(mb, nb, fy, fx, am, width=2048):
-    blk = pl.BlockSpec((1, width), lambda i: (0, i))
-    return pl.pallas_call(
+def deposit_kernel(idx_ref, col_ref, fy_ref, fx_ref, am_ref, keep_ref, send_ref, wa, wb, *accs):
+    ways = len(accs)
+
+    def clear(i, carry):
+        for acc in accs:
+            acc[pl.ds(pl.multiple_of(i * 64, 64), 64), :] = jnp.zeros((64, 128), F32)
+        return carry
+
+    lax.fori_loop(0, 256, clear, 0, unroll=2)
+
+    def weights(n, dst):
+        xs = lax.broadcasted_iota(jnp.int32, (128, 128), 0)
+        rows = lax.broadcasted_iota(jnp.int32, (256, 128), 0)
+        off = rows // 2 - lax.broadcasted_iota(jnp.int32, (256, 128), 1)
+        odd = rows % 2 == 1
+        at = pl.ds(pl.multiple_of(n * 128, 128), 128)
+        fx = fx_ref[:, at]
+        am = am_ref[:, at]
+        hi = am * fy_ref[:, at]
+        lo = am - hi
+        d = xs - col_ref[:, at]
+        w = jnp.where(d == 0, 1.0 - fx, jnp.where(d == 1, fx, 0.0)).astype(BF)
+        e = jnp.where(off == 0, jnp.where(odd, hi, lo), 0.0).astype(BF)
+        dst[...] = lax.dot_general(e, w, NT, preferred_element_type=F32)
+
+    def add(n, src):
+        for f in range(0, 128, ways):
+            at = [pl.ds(idx_ref[n, f + k], 2) for k in range(ways)]
+            new = [accs[k][at[k], :] + src[2 * (f + k) : 2 * (f + k) + 2, :] for k in range(ways)]
+            for k in range(ways):
+                accs[k][at[k], :] = new[k]
+
+    weights(0, wa)
+
+    def chunk(n, carry):
+        weights(2 * n + 1, wb)
+        add(2 * n, wa)
+        weights(jnp.minimum(2 * n + 2, 63), wa)
+        add(2 * n + 1, wb)
+        return carry
+
+    lax.fori_loop(0, 32, chunk, 0)
+
+    def store(i, carry):
+        for ref, base in ((keep_ref, 0), (send_ref, 8192)):
+            at = pl.ds(pl.multiple_of(i * 64 + base, 64), 64)
+            total = accs[0][at, :]
+            for acc in accs[1:]:
+                total = total + acc[at, :]
+            ref[i] = total.astype(BF)
+        return carry
+
+    lax.fori_loop(0, 128, store, 0, unroll=2)
+
+
+def deposit(idx, col, fy, fx, am):
+    return call(
         deposit_kernel,
-        grid=(8192 // width,),
-        out_shape=[jax.ShapeDtypeStruct((128, 64, 128), BF)] * 2,
-        in_specs=[blk] * 5,
-        out_specs=[pl.BlockSpec((128, 64, 128), lambda i: (0, 0, 0))] * 2,
-        scratch_shapes=[pltpu.VMEM((1024, width), BF), pltpu.VMEM((8, 1024, 256), F32)],
-        compiler_params=pltpu.CompilerParams(vmem_limit_bytes=VLIM),
-        cost_estimate=pl.CostEstimate(flops=int(34e9), bytes_accessed=4 << 20, transcendentals=0),
-        name="deposit",
-    )(mb, nb, fy, fx, am)
-
-
-def gather_kernel(base_ref, a_ref, b_ref, col_ref, fy_ref, fx_ref, o_ref, st, g):
+        [jax.ShapeDtypeStruct((128, 64, 128), BF)] * 2,
+        [SM] + [VM] * 4,
+        [pltpu.VMEM((256, 128), F32)] * 2 + [pltpu.VMEM((16384, 128), F32)] * 4,
+        int(1.2e10), 44, "deposit",
+        idx, col, fy, fx, am,
+    )
+
+
+def gather_kernel(base_ref, a_ref, b_ref, col_ref, fy_ref, fx_ref, o_ref, st, ga, gb):
     def load(i, carry):
         at = pl.multiple_of(i * 128, 128)
         st[pl.ds(at, 128), :] = a_ref[i].astype(F32)
         st[pl.ds(at + 16384, 128), :] = b_ref[i].astype(F32)
         return carry
 
-    lax.fori_loop(0, 128, load, 0, unroll=2)
-    sub = lax.broadcasted_iota(jnp.int32, (8, 128), 0)
-    off = lax.broadcasted_iota(jnp.int32, (8, 128), 1) - sub // 4
-    upper = sub % 4 >= 2
-    odd = sub % 2 == 1
-    xs = lax.broadcasted_iota(jnp.int32, (128, 128), 0)
-
-    def chunk(n, carry):
+    lax.fori_loop(0, 128, load, 0, unroll=4)
+
+    def fetch(n, g):
         for f in range(128):
             g[f * 4 : f * 4 + 4, :] = st[pl.ds(base_ref[n, f], 4), :]
+
+    def mix(n, g):
+        sub = lax.broadcasted_iota(jnp.int32, (8, 128), 0)
+        off = lax.broadcasted_iota(jnp.int32, (8, 128), 1) - sub // 4
+        upper = sub % 4 >= 2
+        odd = sub % 2 == 1
+        xs = lax.broadcasted_iota(jnp.int32, (128, 128), 0)
         at = pl.ds(pl.multiple_of(n * 128, 128), 128)
         col = col_ref[:, at]
         fy = fy_ref[:, at]
@@ -412,17 +419,27 @@
         w = jnp.where(d == 0, 1.0 - fx, jnp.where(d == 1, fx, 0.0))
         hi = w.astype(BF)
         lo = (w - hi.astype(F32)).astype(BF)
-        rows = g[...].astype(BF)
-        z = jnp.dot(rows, hi, preferred_element_type=F32) + jnp.dot(rows, lo, preferred_element_type=F32)
-        total = jnp.zeros((8, 128), F32)
+        z = jnp.dot(g[...].astype(BF), jnp.concatenate([hi, lo], axis=1), preferred_element_type=F32)
+        parts = [jnp.zeros((8, 128), F32) for _ in range(4)]
         for i in range(64):
-            total = total + jnp.where(off == 2 * i, z[8 * i : 8 * i + 8], 0.0)
-        total = total * jnp.where(upper, fy, 1.0 - fy)
+            keep = off == 2 * i
+            for h in range(2):
+                k = 2 * h + i % 2
+                parts[k] = parts[k] + jnp.where(keep, z[8 * i : 8 * i + 8, h * 128 : h * 128 + 128], 0.0)
+        total = (parts[0] + parts[1] + (parts[2] + parts[3])) * jnp.where(upper, fy, 1.0 - fy)
         o_ref[0:1, at] = jnp.sum(jnp.where(odd, 0.0, total), axis=0, keepdims=True)
         o_ref[1:2, at] = jnp.sum(jnp.where(odd, total, 0.0), axis=0, keepdims=True)
-        return carry
-
-    lax.fori_loop(0, 64, chunk, 0)
+
+    fetch(0, ga)
+
+    def chunk(n, carry):
+        fetch(2 * n + 1, gb)
+        mix(2 * n, ga)
+        fetch(jnp.minimum(2 * n + 2, 63), ga)
+        mix(2 * n + 1, gb)
+        return carry
+
+    lax.fori_loop(0, 32, chunk, 0)
 
 
 def gather(base, a, b, col, fy, fx):
@@ -430,8 +447,8 @@
         gather_kernel,
         jax.ShapeDtypeStruct((2, 8192), F32),
         [SM] + [VM] * 5,
-        [pltpu.VMEM((32768, 128), F32), pltpu.VMEM((512, 128), F32)],
-        int(2e10), "gather",
+        [pltpu.VMEM((32768, 128), F32)] + [pltpu.VMEM((512, 128), F32)] * 2,
+        int(1e10), 30, "gather",
         base, a, b, col, fy, fx,
     )
 
@@ -454,16 +471,15 @@
     core = lax.axis_index("narrow") % 2
     wave = device * 64 + jnp.arange(64)
     wave = jnp.where(wave >= 4096, wave - 8192, wave).astype(F32)[None]
+    spec = stream_send(stream_hat, wave)
+    spec, float_slot, tile_lists = lax.optimization_barrier((spec, float_slot, tile_lists))
+    spec = spread(spec.reshape(128, 2, 64, 128)).reshape(256, 64, 128)
+
     slot = float_slot.reshape(64, 128)
     row = float_row.reshape(64, 128)
-    col = float_col.reshape(64, 128)
-
-    mine = (tile_lists >= 0) & (tile_lists // 64 == device)
-    place = jnp.cumsum(mine.astype(jnp.int32), axis=1) - 1
-    local = tile_lists % 64 + 1
-    send_index = jnp.stack(
-        [jnp.sum(jnp.where(mine & (place == e), local, 0), axis=1) for e in range(CAPO)], axis=1
-    ) - 1
+    col = float_col.reshape(1, 8192)
+    fy = float_frac[0:1]
+    fx = float_frac[1:2]
 
     own_list = lax.dynamic_index_in_dim(tile_lists, group, 0, keepdims=False)
     holder = own_list // 64
@@ -474,30 +490,26 @@
         jnp.where(jnp.arange(256)[:, None, None] == slot[None], position[:, None, None], 0), axis=0
     )
 
-    flat = lambda x: x.reshape(1, 8192)
-    fy = float_frac[0:1]
-    fx = float_frac[1:2]
-    rows = flat(pos // 16 * 64 + row)
-    cols = flat(pos % 16 * 128 + col)
-
-    spec = stream_send(stream_hat, wave)
-    spec, rows, cols = lax.optimization_barrier((spec, rows, cols))
-    spec = spread(spec.reshape(128, 2, 64, 128)).reshape(256, 64, 128)
-    keep, send = deposit(rows, cols, fy, fx, flat(float_dye))
+    mine = (tile_lists >= 0) & (tile_lists // 64 == device)
+    place = jnp.cumsum(mine.astype(jnp.int32), axis=1) - 1
+    local = tile_lists % 64 + 1
+    entries = jnp.stack(
+        [jnp.sum(jnp.where(mine & (place == e), local, 0), axis=1) for e in range(CAPO)], axis=1
+    ).reshape(1, 32) - 1
+
+    keep, send = deposit(pos * 64 + row, col, fy, fx, float_dye.reshape(1, 8192))
     dep = (keep.astype(F32) + swap_cores(send).astype(F32)).astype(BF)
+    returned = spread(dep)
     spec, dep = lax.optimization_barrier((spec, dep))
-    returned = spread(dep)
-
-    tiles = stream_recv(spec)
-    outgoing = tiles[jnp.maximum(send_index, 0)]
-    outgoing = jnp.broadcast_to(outgoing[:, None], (16, 4, 2, 128, 128)).reshape(128, 128, 128)
-    outgoing, returned = lax.optimization_barrier((outgoing, returned))
+
+    outgoing = stream_recv(entries, spec)
+    outgoing, dye = lax.optimization_barrier((outgoing, dye))
     own = spread(outgoing)
-    front = dye_send(send_index.reshape(1, 32), dye, returned)
+    front = dye_send(entries, dye, returned)
     own, front = lax.optimization_barrier((own, front))
     other = swap_cores(own)
     front = spread(front.reshape(128, 2, 32, 128)).reshape(256, 32, 128)
-    velocity = gather(pos * 128 + 2 * row, own, other, flat(float_col), fy, fx)
+    velocity = gather(pos * 128 + 2 * row, own, other, col, fy, fx)
     velocity, front = lax.optimization_barrier((velocity, front))
     dye_hat = dye_recv(front)
     return (velocity, dye_hat)

time: 237 us -> 219 us (0.924)
  Pallas kernels: 117 us -> 74.1 us
  waiting for transfers between devices: 68.1 us -> 99.1 us
  other arithmetic: 10.1 us -> 4.5 us
  starting transfers between devices: 32.5 us -> 28.3 us
  local copies, waits for them, and re-layouts: 8.47 us -> 11.5 us
    pallas_call x1 -> x0, Pallas kernels: 49.8 us -> none  [deposit(): pl.pallas_call(deposit_kernel, grid=(8192 // width,), out_shape=[jax.Shap...]
    all_to_all x4, waiting for transfers between devices: 61.6 us -> 92.1 us  [spread(): return lax.all_to_all(blocks, AXES, split_axis=0, concat_axis=0, tiled=True)]
    unnamed x10 -> x52, local copies, waits for them, and re-layouts: 1.36 us -> 11.1 us
    pallas_call x5 -> x6, Pallas kernels: 67 us -> 74.1 us  [call(): pl.pallas_call(kernel, out_shape=outs, in_specs=specs, out_specs=jax.tree...]
    all_to_all x4, starting transfers between devices: 30.4 us -> 26.2 us  [spread(): return lax.all_to_all(blocks, AXES, split_axis=0, concat_axis=0, tiled=True)]
    broadcast_in_dim x1 -> x0, local copies, waits for them, and re-layouts: 3.06 us -> none  [shards(): jnp.broadcast_to(outgoing[:, None], (16, 4, 2, 128, 128))]
  transfers between devices with their start and end apart: 6 -> 6, of which waited for: 5 -> 6; matrix products, arithmetic and copies ran while one was open for 4% -> 2% of each run, Pallas kernels for 40% -> 26%
where the time goes in v3:
time: 219 us; the launch traced here: 218 us
  waiting for transfers between devices  99.1 us (45%)
  Pallas kernels  74.1 us (34%)
  starting transfers between devices  28.3 us (13%)
  local copies, waits for them, and re-layouts  11.5 us (5%)
  other arithmetic  4.5 us (2%)
    all_to_all x4, waiting for transfers between devices, spread(): return lax.all_to_all(blocks, AXES, split_axis=0, concat_axis=0, tiled=True)  92.1 us
    pallas_call x6, Pallas kernels, call(): pl.pallas_call(kernel, out_shape=outs, in_specs=specs, out_specs=jax.tree...  74.1 us
    all_to_all x4, starting transfers between devices, spread(): return lax.all_to_all(blocks, AXES, split_axis=0, concat_axis=0, tiled=True)  26.2 us
    unnamed x52, local copies, waits for them, and re-layouts  11.1 us
    ppermute x2, waiting for transfers between devices, swap_cores(): return lax.ppermute(x, 'narrow', [(i, i ^ 1) for i in range(n)])  6.94 us
  transfers between devices with their start and end apart: 6, of which 6 were waited for; matrix products, arithmetic and copies ran while one was open for 2% of the time, Pallas kernels for 26%

profile of v3, /device:TPU:1, one launch (start us, length us, event | category | flops | bytes accessed | tf_op | source)
XLA Modules:
  0.0 218.5 jit_solution(1689633618467671543)
XLA Ops:
  0.7 0.0 copy-start.3
  0.7 1.6 copy-done.3
  2.2 0.0 copy-start.11
  2.2 0.9 copy-done.11
  3.1 0.0 copy-start.16
  3.2 0.8 copy-done.16
  4.0 0.0 copy-start.17
  4.0 0.8 copy-done.17
  4.8 0.8 copy-done.21
  5.5 10.2 %stream_send.1 = bf16[256,64,128]{2,1,0:T(8,128)(2,1)S(1)} custom-call(f32[1,64]{1,0:T(1,128)S(1)} %fusion.7.wa_ref, bf16[2,64,8192]{2,1,0:T(8,128)(2,1)S(1)} %copy-done.3, bf16[256,128]{1,0:T(8,128)(2,1)S(1)} %copy-done.16, f32[64,128]{1,0:T(8,128)S(1)} %copy-done.17, f32[64,128]{1,0:T(8,128)S(1)} %copy-done.21, bf16[256,256]{1,0:T(8,128)(2,1)S(1)} %copy-done.11), custom_call_target="tpu_custom_call" | custom-call | flops 6000000000 | bytes 1048576 | tf_op jit(solution)/shard_map/stream_send/pallas_call | solution.py:128
  15.7 0.0 copy-start
  15.7 2.0 copy-done
  17.8 0.0 copy-start.5
  17.8 0.0 copy-start.6
  17.8 12.0 %all-to-all-start = ((bf16[128,2,64,128]{3,2,1,0:T(8,128)(2,1)}), bf16[128,2,64,128]{3,2,1,0:T(8,128)(2,1)}, u32[]{:S(2)}, u32[]{:S(2)}) async-start(bf16[128,2,64,128]{3,2,1,0:T(8,128)(2,1)} %bitcast.33), calls=%async_computation | async-start | bytes 8388608 | tf_op jit(solution)/shard_map/all_to_all | solution.py:460
  29.7 0.0 copy-done.23
  29.8 0.1 fusion.8
  29.8 0.0 copy-done.22
  29.9 0.2 convert_reduce_fusion
  30.1 0.0 copy-done.24
  30.1 1.1 select_reduce_fusion
  31.2 0.0 copy-done.25
  31.2 0.0 copy-done.5
  31.2 0.0 copy-done.6
  31.2 21.0 %deposit.1 = (bf16[128,64,128]{2,1,0:T(8,128)(2,1)S(1)}, bf16[128,64,128]{2,1,0:T(8,128)(2,1)S(1)}) custom-call(s32[64,128]{1,0:T(8,128)S(1)} %get-tuple-element.34.idx_ref, s32[1,8192]{1,0:T(1,128)S(1)} %bitcast.37, f32[1,8192]{1,0:T(1,128)S(1)} %get-tuple-element.33.fy_ref, f32[1,8192]{1,0:T(1,128)S(1)} %get-tuple-element.32.fx_ref, f32[1,8192]{1,0:T(1,128)S(1)} %bitcast.36), custom_call_target="tpu_custom_call" | custom-call | flops 12000000000 | bytes 1048576 | tf_op jit(solution)/shard_map/deposit/pallas_call | solution.py:128
  52.2 1.2 collective-permute-start
  53.4 3.8 %collective-permute-done = bf16[128,64,128]{2,1,0:T(8,128)(2,1)S(1)} collective-permute-done((bf16[128,64,128]{2,1,0:T(8,128)(2,1)S(1)}, bf16[128,64,128]{2,1,0:T(8,128)(2,1)S(1)}, u32[]{:S(2)}, u32[]{:S(2)}) %collective-permute-start) | collective-permute-done | bytes 2097184 | tf_op jit(solution)/shard_map/ppermute | solution.py:465
  57.2 2.3 %add_convert_fusion = bf16[128,64,128]{2,1,0:T(8,128)(2,1)} fusion(bf16[128,64,128]{2,1,0:T(8,128)(2,1)S(1)} %collective-permute-done, bf16[128,64,128]{2,1,0:T(8,128)(2,1)S(1)} %get-tuple-element.17), kind=kLoop, calls=%fused_computation.2 | loop fusion | flops 4194304 | bytes 6291456 | tf_op jit(solution)/shard_map/convert_element_type | solution.py:501
  59.5 22.8 %all-to-all-done = bf16[128,2,64,128]{3,2,1,0:T(8,128)(2,1)} async-done(((bf16[128,2,64,128]{3,2,1,0:T(8,128)(2,1)}), bf16[128,2,64,128]{3,2,1,0:T(8,128)(2,1)}, u32[]{:S(2)}, u32[]{:S(2)}) %all-to-all-start) | async-done | bytes 4194336 | tf_op jit(solution)/shard_map/all_to_all | solution.py:460
  82.4 4.8 %all-to-all-start.2 = ((bf16[128,64,128]{2,1,0:T(8,128)(2,1)}), bf16[128,64,128]{2,1,0:T(8,128)(2,1)S(1)}, u32[]{:S(2)}, u32[]{:S(2)}) async-start(bf16[128,64,128]{2,1,0:T(8,128)(2,1)} %add_convert_fusion), calls=%async_computation.2 | async-start | bytes 4194304 | tf_op jit(solution)/shard_map/all_to_all | solution.py:460
  87.2 0.6 reduce-window.6
  87.8 0.2 slice_reduce_fusion
  88.0 0.1 compare_bitcast_fusion
  88.1 0.1 select_reduce_fusion.2
  88.2 0.1 copy.35
  88.3 0.1 sub.33.idx_ref
  88.4 0.0 copy-done.10
  88.4 0.0 copy-done.12
  88.5 0.0 copy-done.14
  88.5 0.0 copy-done.15
  88.5 10.9 %stream_recv.1 = bf16[128,128,128]{2,1,0:T(8,128)(2,1)S(1)} custom-call(s32[1,32]{1,0:T(1,128)S(1)} %sub.33.idx_ref, bf16[256,64,128]{2,1,0:T(8,128)(2,1)} %bitcast.7.x_ref, bf16[256,256]{1,0:T(8,128)(2,1)S(1)} %copy-done.10, f32[128,128]{1,0:T(8,128)S(1)} %copy-done.12, f32[128,128]{1,0:T(8,128)S(1)} %copy-done.15, bf16[128,256]{1,0:T(8,128)(2,1)S(1)} %copy-done.14), custom_call_target="tpu_custom_call" | custom-call | flops 6000000000 | bytes 1048576 | tf_op jit(solution)/shard_map/stream_recv/pallas_call | solution.py:128
  99.4 0.0 copy-start.1
  99.4 2.0 copy-done.1
  101.4 16.2 %all-to-all-done.2.ret_ref = bf16[128,64,128]{2,1,0:T(8,128)(2,1)S(1)} async-done(((bf16[128,64,128]{2,1,0:T(8,128)(2,1)}), bf16[128,64,128]{2,1,0:T(8,128)(2,1)S(1)}, u32[]{:S(2)}, u32[]{:S(2)}) %all-to-all-start.2) | async-done | bytes 2097184 | tf_op jit(solution)/shard_map/all_to_all | solution.py:460
  117.7 5.5 %all-to-all-start.1 = ((bf16[128,128,128]{2,1,0:T(8,128)(2,1)}), bf16[128,128,128]{2,1,0:T(8,128)(2,1)}, u32[]{:S(2)}, u32[]{:S(2)}) async-start(bf16[128,128,128]{2,1,0:T(8,128)(2,1)} %copy-done.1), calls=%async_computation.1 | async-start | bytes 8388608 | tf_op jit(solution)/shard_map/all_to_all | solution.py:460
  123.2 0.0 copy-done.4
  123.2 0.0 copy-done.9
  123.2 0.0 copy-done.18
  123.2 0.0 copy-done.19
  123.2 0.0 copy-start.20
  123.2 0.7 copy-done.20
  124.0 6.0 %dye_send.1 = bf16[256,32,128]{2,1,0:T(8,128)(2,1)S(1)} custom-call(s32[1,32]{1,0:T(1,128)S(1)} %sub.33.idx_ref, bf16[64,8192]{1,0:T(8,128)(2,1)S(1)} %copy-done.4, bf16[128,64,128]{2,1,0:T(8,128)(2,1)S(1)} %all-to-all-done.2.ret_ref, bf16[128,64]{1,0:T(8,128)(2,1)S(1)} %copy-done.20, f32[64,128]{1,0:T(8,128)S(1)} %copy-done.18, f32[64,128]{1,0:T(8,128)S(1)} %copy-done.19, ...), custom_call_target="tpu_custom_call" | custom-call | flops 4000000000 | bytes 1048576 | tf_op jit(solution)/shard_map/dye_send/pallas_call | solution.py:128
  130.0 0.0 copy-start.2
  130.0 1.4 copy-done.2
  131.4 44.6 %all-to-all-done.1.a_ref = bf16[128,128,128]{2,1,0:T(8,128)(2,1)} async-done(((bf16[128,128,128]{2,1,0:T(8,128)(2,1)}), bf16[128,128,128]{2,1,0:T(8,128)(2,1)}, u32[]{:S(2)}, u32[]{:S(2)}) %all-to-all-start.1) | async-done | bytes 4194336 | tf_op jit(solution)/shard_map/all_to_all | solution.py:460
  176.0 0.9 collective-permute-start.1
  176.9 4.0 %all-to-all-start.3 = ((bf16[128,2,32,128]{3,2,1,0:T(8,128)(2,1)}), bf16[128,2,32,128]{3,2,1,0:T(8,128)(2,1)S(1)}, u32[]{:S(2)}, u32[]{:S(2)}) async-start(bf16[128,2,32,128]{3,2,1,0:T(8,128)(2,1)} %bitcast.34), calls=%async_computation.3 | async-start | bytes 4194304 | tf_op jit(solution)/shard_map/all_to_all | solution.py:460
  180.9 3.2 %collective-permute-done.1.b_ref = bf16[128,128,128]{2,1,0:T(8,128)(2,1)} collective-permute-done((bf16[128,128,128]{2,1,0:T(8,128)(2,1)}, bf16[128,128,128]{2,1,0:T(8,128)(2,1)}, u32[]{:S(2)}, u32[]{:S(2)}) %collective-permute-start.1) | collective-permute-done | bytes 4194336 | tf_op jit(solution)/shard_map/ppermute | solution.py:465
  184.0 18.9 %gather.1 = f32[2,8192]{1,0:T(2,128)} custom-call(s32[64,128]{1,0:T(8,128)S(1)} %get-tuple-element.35.base_ref, bf16[128,128,128]{2,1,0:T(8,128)(2,1)} %all-to-all-done.1.a_ref, bf16[128,128,128]{2,1,0:T(8,128)(2,1)} %collective-permute-done.1.b_ref, s32[1,8192]{1,0:T(1,128)S(1)} %bitcast.38, f32[1,8192]{1,0:T(1,128)S(1)} %get-tuple-element.33.fy_ref, ...), custom_call_target="tpu_custom_call" | custom-call | flops 10000000000 | bytes 1048576 | tf_op jit(solution)/shard_map/gather/pallas_call | solution.py:128
  202.9 8.5 %all-to-all-done.3 = bf16[128,2,32,128]{3,2,1,0:T(8,128)(2,1)S(1)} async-done(((bf16[128,2,32,128]{3,2,1,0:T(8,128)(2,1)}), bf16[128,2,32,128]{3,2,1,0:T(8,128)(2,1)S(1)}, u32[]{:S(2)}, u32[]{:S(2)}) %all-to-all-start.3) | async-done | bytes 2097184 | tf_op jit(solution)/shard_map/all_to_all | solution.py:460
  211.4 0.0 copy-done.7
  211.4 0.0 copy-done.8
  211.4 0.0 copy-done.13
  211.4 7.1 %dye_recv.1 = f32[2,64,8192]{2,1,0:T(8,128)} custom-call(bf16[256,32,128]{2,1,0:T(8,128)(2,1)S(1)} %bitcast.35, bf16[256,256]{1,0:T(8,128)(2,1)S(1)} %copy-done.8, f32[128,128]{1,0:T(8,128)S(1)} %copy-done.12, f32[128,128]{1,0:T(8,128)S(1)} %copy-done.13, bf16[256,256]{1,0:T(8,128)(2,1)S(1)} %copy-done.7), custom_call_target="tpu_custom_call" | custom-call | flops 4000000000 | bytes 1048576 | tf_op jit(solution)/shard_map/dye_recv/pallas_call | solution.py:128
  (26 shorter events, 0.2 us)
Async XLA Ops:
  0.7 1.6 copy-start.3
  2.2 0.9 copy-start.11
  3.1 0.8 copy-start.16
  4.0 0.8 copy-start.17
  4.7 0.8 copy-start.21
  15.7 2.0 copy-start
  17.7 12.0 %copy-start.23 = (f32[2,8192]{1,0:T(2,128)S(1)}, f32[2,8192]{1,0:T(2,128)}, u32[]{:S(2)}) copy-start(f32[2,8192]{1,0:T(2,128)} %param.29) | copy-start | bytes 196612
  17.7 12.1 %copy-start.22 = (s32[16,256]{1,0:T(8,128)S(1)}, s32[16,256]{1,0:T(8,128)}, u32[]{:S(2)}) copy-start(s32[16,256]{1,0:T(8,128)} %param.31) | copy-start | bytes 49156
  17.7 12.3 %copy-start.24 = (s32[8192]{0:T(1024)S(1)}, s32[8192]{0:T(1024)}, u32[]{:S(2)}) copy-start(s32[8192]{0:T(1024)} %param.26) | copy-start | bytes 98308
  17.7 13.4 %copy-start.25 = (s32[8192]{0:T(1024)S(1)}, s32[8192]{0:T(1024)}, u32[]{:S(2)}) copy-start(s32[8192]{0:T(1024)} %param.27) | copy-start | bytes 98308
  17.8 13.5 %copy-start.5 = (f32[8192]{0:T(1024)S(1)}, f32[8192]{0:T(1024)}, u32[]{:S(2)}) copy-start(f32[8192]{0:T(1024)} %param.30) | copy-start | bytes 98308
  17.8 13.5 %copy-start.6 = (s32[8192]{0:T(1024)S(1)}, s32[8192]{0:T(1024)}, u32[]{:S(2)}) copy-start(s32[8192]{0:T(1024)} %param.28) | copy-start | bytes 98308
  17.8 64.6 %all-to-all-start = ((bf16[128,2,64,128]{3,2,1,0:T(8,128)(2,1)}), bf16[128,2,64,128]{3,2,1,0:T(8,128)(2,1)}, u32[]{:S(2)}, u32[]{:S(2)}) async-start(bf16[128,2,64,128]{3,2,1,0:T(8,128)(2,1)} %bitcast.33), calls=%async_computation | async-start | bytes 8388608 | tf_op jit(solution)/shard_map/all_to_all | solution.py:460
  52.2 5.0 %collective-permute-start = (bf16[128,64,128]{2,1,0:T(8,128)(2,1)S(1)}, bf16[128,64,128]{2,1,0:T(8,128)(2,1)S(1)}, u32[]{:S(2)}, u32[]{:S(2)}) collective-permute-start(bf16[128,64,128]{2,1,0:T(8,128)(2,1)S(1)} %get-tuple-element.18), channel_id=1, source_target_pairs={{0,1},{1,0},{2,3},{3,2},{4,5},{5,4},{6,7},{7,6},{8,9},{9,8},{10,11... | collective-permute-start | bytes 6291464 | tf_op jit(solution)/shard_map/ppermute | solution.py:465
  57.2 31.2 %copy-start.10 = (bf16[256,256]{1,0:T(8,128)(2,1)S(1)}, bf16[256,256]{1,0:T(8,128)(2,1)}, u32[]{:S(2)}) copy-start(bf16[256,256]{1,0:T(8,128)(2,1)} %constant.116.clone.w1_ref) | copy-start | bytes 393220
  57.2 31.2 %copy-start.12 = (f32[128,128]{1,0:T(8,128)S(1)}, f32[128,128]{1,0:T(8,128)}, u32[]{:S(2)}) copy-start(f32[128,128]{1,0:T(8,128)} %constant.117.clone.tc_ref) | copy-start | bytes 196612
  57.2 31.2 %copy-start.14 = (bf16[128,256]{1,0:T(8,128)(2,1)S(1)}, bf16[128,256]{1,0:T(8,128)(2,1)}, u32[]{:S(2)}) copy-start(bf16[128,256]{1,0:T(8,128)(2,1)} %constant.119.clone.v_ref) | copy-start | bytes 196612
  57.2 31.2 %copy-start.15 = (f32[128,128]{1,0:T(8,128)S(1)}, f32[128,128]{1,0:T(8,128)}, u32[]{:S(2)}) copy-start(f32[128,128]{1,0:T(8,128)} %constant.118.clone.ts_ref) | copy-start | bytes 196612
  82.4 35.3 %all-to-all-start.2 = ((bf16[128,64,128]{2,1,0:T(8,128)(2,1)}), bf16[128,64,128]{2,1,0:T(8,128)(2,1)S(1)}, u32[]{:S(2)}, u32[]{:S(2)}) async-start(bf16[128,64,128]{2,1,0:T(8,128)(2,1)} %add_convert_fusion), calls=%async_computation.2 | async-start | bytes 4194304 | tf_op jit(solution)/shard_map/all_to_all | solution.py:460
  99.4 2.0 copy-start.1
  101.4 21.8 %copy-start.4 = (bf16[64,8192]{1,0:T(8,128)(2,1)S(1)}, bf16[64,8192]{1,0:T(8,128)(2,1)}, u32[]{:S(2)}) copy-start(bf16[64,8192]{1,0:T(8,128)(2,1)} %dye_ref) | copy-start | bytes 3145732
  101.4 21.8 %copy-start.9 = (bf16[256,256]{1,0:T(8,128)(2,1)S(1)}, bf16[256,256]{1,0:T(8,128)(2,1)}, u32[]{:S(2)}) copy-start(bf16[256,256]{1,0:T(8,128)(2,1)} %constant.122.clone.w2_ref) | copy-start | bytes 393220
  101.4 21.8 %copy-start.18 = (f32[64,128]{1,0:T(8,128)S(1)}, f32[64,128]{1,0:T(8,128)}, u32[]{:S(2)}) copy-start(f32[64,128]{1,0:T(8,128)} %constant.113.clone.tc_ref) | copy-start | bytes 98308
  101.4 21.8 %copy-start.19 = (f32[64,128]{1,0:T(8,128)S(1)}, f32[64,128]{1,0:T(8,128)}, u32[]{:S(2)}) copy-start(f32[64,128]{1,0:T(8,128)} %constant.121.clone.ts_ref) | copy-start | bytes 98308
  117.7 58.3 %all-to-all-start.1 = ((bf16[128,128,128]{2,1,0:T(8,128)(2,1)}), bf16[128,128,128]{2,1,0:T(8,128)(2,1)}, u32[]{:S(2)}, u32[]{:S(2)}) async-start(bf16[128,128,128]{2,1,0:T(8,128)(2,1)} %copy-done.1), calls=%async_computation.1 | async-start | bytes 8388608 | tf_op jit(solution)/shard_map/all_to_all | solution.py:460
  123.2 0.8 copy-start.20
  130.0 1.4 copy-start.2
  176.0 8.1 %collective-permute-start.1 = (bf16[128,128,128]{2,1,0:T(8,128)(2,1)}, bf16[128,128,128]{2,1,0:T(8,128)(2,1)}, u32[]{:S(2)}, u32[]{:S(2)}) collective-permute-start(bf16[128,128,128]{2,1,0:T(8,128)(2,1)} %all-to-all-done.1.a_ref), channel_id=1, source_target_pairs={{0,1},{1,0},{2,3},{3,2},{4,5},{5,4},{6,7},{7,6},{8,9},{9,8},{10,11... | collective-permute-start | bytes 12582920 | tf_op jit(solution)/shard_map/ppermute | solution.py:465
  176.9 34.5 %all-to-all-start.3 = ((bf16[128,2,32,128]{3,2,1,0:T(8,128)(2,1)}), bf16[128,2,32,128]{3,2,1,0:T(8,128)(2,1)S(1)}, u32[]{:S(2)}, u32[]{:S(2)}) async-start(bf16[128,2,32,128]{3,2,1,0:T(8,128)(2,1)} %bitcast.34), calls=%async_computation.3 | async-start | bytes 4194304 | tf_op jit(solution)/shard_map/all_to_all | solution.py:460
  184.0 27.4 %copy-start.7 = (bf16[256,256]{1,0:T(8,128)(2,1)S(1)}, bf16[256,256]{1,0:T(8,128)(2,1)}, u32[]{:S(2)}) copy-start(bf16[256,256]{1,0:T(8,128)(2,1)} %constant.125.clone.v_ref) | copy-start | bytes 393220
  184.0 27.4 %copy-start.8 = (bf16[256,256]{1,0:T(8,128)(2,1)S(1)}, bf16[256,256]{1,0:T(8,128)(2,1)}, u32[]{:S(2)}) copy-start(bf16[256,256]{1,0:T(8,128)(2,1)} %constant.123.clone.w1_ref) | copy-start | bytes 393220
  184.0 27.4 %copy-start.13 = (f32[128,128]{1,0:T(8,128)S(1)}, f32[128,128]{1,0:T(8,128)}, u32[]{:S(2)}) copy-start(f32[128,128]{1,0:T(8,128)} %constant.124.clone.ts_ref) | copy-start | bytes 196612

commit v4 on v3

--- a/solution.py
+++ b/solution.py
@@ -144,7 +144,7 @@
         [SM] + [VM] * 5,
         [pltpu.VMEM((128 * PAD, 128), F32)] + [pltpu.VMEM((64 * PAD2, 128), F32)] * 2
         + [pltpu.VMEM((256 * PAD, 128), F32)],
-        int(6e9), 36, "stream_send",
+        int(6e9), 60, "stream_send",
         wa, stream, *send_tables(1.0, True),
     )
 
@@ -179,9 +179,7 @@
 
     def store(n, carry):
         tile = jnp.maximum(idx_ref[0, n], 0)
-        data = of[pl.ds(pl.multiple_of(tile * PAD2, 8), 128), :].astype(BF)
-        for x in range(4):
-            o_ref[n // 2 * 8 + 2 * x + n % 2] = data
+        o_ref[n] = of[pl.ds(pl.multiple_of(tile * PAD2, 8), 128), :].astype(BF)
         return carry
 
     lax.fori_loop(0, 32, store, 0, unroll=2)
@@ -190,7 +188,7 @@
 def stream_recv(idx, x):
     return call(
         stream_recv_kernel,
-        jax.ShapeDtypeStruct((128, 128, 128), BF),
+        jax.ShapeDtypeStruct((32, 128, 128), BF),
         [SM] + [VM] * 5,
         [pltpu.VMEM((256 * PAD, 128), F32), pltpu.VMEM((64 * PAD2, 128), F32)],
         int(6e9), 28, "stream_recv",
@@ -211,13 +209,8 @@
 
         @pl.when(tile >= 0)
         def _():
-            g = n // 2
-            e = n % 2
-            total = ret_ref[g * 8 + e].astype(F32)
-            for x in range(1, 4):
-                total = total + ret_ref[g * 8 + 2 * x + e].astype(F32)
             at = pl.ds(pl.multiple_of(tile * PAD, 8), 64)
-            xs[at, :] = xs[at, :] + total
+            xs[at, :] = xs[at, :] + ret_ref[n].astype(F32)
 
         return carry
 
@@ -392,14 +385,17 @@
     )
 
 
-def gather_kernel(base_ref, a_ref, b_ref, col_ref, fy_ref, fx_ref, o_ref, st, ga, gb):
-    def load(i, carry):
-        at = pl.multiple_of(i * 128, 128)
-        st[pl.ds(at, 128), :] = a_ref[i].astype(F32)
-        st[pl.ds(at + 16384, 128), :] = b_ref[i].astype(F32)
-        return carry
-
-    lax.fori_loop(0, 128, load, 0, unroll=4)
+def gather_kernel(base_ref, col_ref, fy_ref, fx_ref, *refs):
+    o_ref, st, ga, gb = refs[-4:]
+    row = 0
+    for ref in refs[:-4]:
+
+        def load(i, carry, ref=ref, row=row):
+            st[pl.ds(pl.multiple_of(row + i * 128, 128), 128), :] = ref[i].astype(F32)
+            return carry
+
+        lax.fori_loop(0, ref.shape[0], load, 0, unroll=4)
+        row += ref.shape[0] * 128
 
     def fetch(n, g):
         for f in range(128):
@@ -442,22 +438,22 @@
     lax.fori_loop(0, 32, chunk, 0)
 
 
-def gather(base, a, b, col, fy, fx):
+def gather(base, col, fy, fx, pieces):
     return call(
         gather_kernel,
         jax.ShapeDtypeStruct((2, 8192), F32),
-        [SM] + [VM] * 5,
+        [SM] + [VM] * (3 + len(pieces)),
         [pltpu.VMEM((32768, 128), F32)] + [pltpu.VMEM((512, 128), F32)] * 2,
         int(1e10), 30, "gather",
-        base, a, b, col, fy, fx,
+        base, col, fy, fx, *pieces,
     )
 
 
 AXES = ("wide", "narrow")
 
 
-def spread(blocks):
-    return lax.all_to_all(blocks, AXES, split_axis=0, concat_axis=0, tiled=True)
+def spread(blocks, axes=AXES):
+    return lax.all_to_all(blocks, axes, split_axis=0, concat_axis=0, tiled=True)
 
 
 def swap_cores(x):
@@ -465,9 +461,38 @@
     return lax.ppermute(x, "narrow", [(i, i ^ 1) for i in range(n)])
 
 
+def shift(x, chips):
+    n = lax.axis_size("narrow")
+    return lax.ppermute(x, "narrow", [(i, (i + 2 * chips) % n) for i in range(n)])
+
+
+def add(*parts):
+    return sum(part.astype(F32) for part in parts).astype(BF)
+
+
+def chip_sum(keep, send):
+    part = add(keep, swap_cores(send)).reshape(4, 2, 16, 64, 128)
+    up = shift(part[2, 0], 1)
+    down = shift(part[2, 1], -1)
+    up_hi = shift(part[1, 1], 1)
+    down_lo = shift(part[3, 0], -1)
+    up_lo = shift(add(part[1, 0], up), 1)
+    down_hi = shift(add(part[3, 1], down), -1)
+    return jnp.concatenate([add(part[0, 0], up_lo, down_lo), add(part[0, 1], up_hi, down_hi)])
+
+
+def chip_gather(own):
+    down = shift(own, 1)
+    up = shift(own, -1)
+    far = [shift(down[:16], 1), shift(up[16:], -1)]
+    mine = [own, up] + far + [down]
+    return mine + [swap_cores(x) for x in mine]
+
+
 def shards(stream_hat, dye, float_slot, float_row, float_col, float_frac, float_dye, tile_lists):
     device = lax.axis_index(AXES)
     group = lax.axis_index("wide")
+    chip = lax.axis_index("narrow") // 2
     core = lax.axis_index("narrow") % 2
     wave = device * 64 + jnp.arange(64)
     wave = jnp.where(wave >= 4096, wave - 8192, wave).astype(F32)[None]
@@ -485,7 +510,9 @@
     holder = own_list // 64
     before = jnp.arange(256)[:, None] > jnp.arange(256)[None, :]
     rank = jnp.sum((before & (holder[:, None] == holder[None, :])).astype(jnp.int32), axis=1)
-    position = jnp.where(own_list >= 0, jnp.where(rank == core, 0, 128) + holder, 0)
+    away = (holder % 8 // 2 - chip) % 4
+    other = (holder % 2 + core) % 2
+    position = jnp.where(own_list >= 0, (other * 4 + away) * 32 + holder // 8 * 2 + rank, 0)
     pos = jnp.sum(
         jnp.where(jnp.arange(256)[:, None, None] == slot[None], position[:, None, None], 0), axis=0
     )
@@ -498,18 +525,18 @@
     ).reshape(1, 32) - 1
 
     keep, send = deposit(pos * 64 + row, col, fy, fx, float_dye.reshape(1, 8192))
-    dep = (keep.astype(F32) + swap_cores(send).astype(F32)).astype(BF)
-    returned = spread(dep)
+    dep = chip_sum(keep, send)
+    returned = spread(dep.reshape(16, 2, 64, 128), "wide").reshape(32, 64, 128)
     spec, dep = lax.optimization_barrier((spec, dep))
 
     outgoing = stream_recv(entries, spec)
     outgoing, dye = lax.optimization_barrier((outgoing, dye))
-    own = spread(outgoing)
+    own = spread(outgoing.reshape(16, 2, 128, 128), "wide").reshape(32, 128, 128)
     front = dye_send(entries, dye, returned)
     own, front = lax.optimization_barrier((own, front))
-    other = swap_cores(own)
+    pieces = chip_gather(own)
     front = spread(front.reshape(128, 2, 32, 128)).reshape(256, 32, 128)
-    velocity = gather(pos * 128 + 2 * row, own, other, col, fy, fx)
+    velocity = gather(pos * 128 + 2 * row, col, fy, fx, pieces)
     velocity, front = lax.optimization_barrier((velocity, front))
     dye_hat = dye_recv(front)
     return (velocity, dye_hat)

time: 219 us -> 249 us (1.14)
  starting transfers between devices: 28.3 us -> 76.5 us
  waiting for transfers between devices: 99.1 us -> 77.5 us
  local copies, waits for them, and re-layouts: 11.5 us -> 5.33 us
  Pallas kernels: 74.1 us -> 78.8 us
  other arithmetic: 4.5 us -> 8.49 us
    all_to_all x4, waiting for transfers between devices: 92.1 us -> 4.84 us  [spread(): return lax.all_to_all(blocks, axes, split_axis=0, concat_axis=0, tiled=True)]
    ppermute x0 -> x10, waiting for transfers between devices: none -> 70.4 us  [shift(): lax.ppermute(x, 'narrow', [(i, (i + 2 * chips) % n) for i in range(n)])]
    ppermute x2 -> x6, starting transfers between devices: 2.15 us -> 31.8 us  [swap_cores(): return lax.ppermute(x, 'narrow', [(i, i ^ 1) for i in range(n)])]
    ppermute x0 -> x10, starting transfers between devices: none -> 10.3 us  [shift(): lax.ppermute(x, 'narrow', [(i, (i + 2 * chips) % n) for i in range(n)])]
    unnamed x52 -> x38, local copies, waits for them, and re-layouts: 11.1 us -> 1.76 us
    all_to_all x4, starting transfers between devices: 26.2 us -> 34.5 us  [spread(): return lax.all_to_all(blocks, axes, split_axis=0, concat_axis=0, tiled=True)]
    pallas_call x6, Pallas kernels: 74.1 us -> 78.8 us  [call(): pl.pallas_call(kernel, out_shape=outs, in_specs=specs, out_specs=jax.tree...]
    ppermute x2 -> x6, waiting for transfers between devices: 6.94 us -> 2.26 us  [swap_cores(): return lax.ppermute(x, 'narrow', [(i, i ^ 1) for i in range(n)])]
  transfers between devices with their start and end apart: 6 -> 20, of which waited for: 6 -> 10; matrix products, arithmetic and copies ran while one was open for 2% -> 4% of each run, Pallas kernels for 26% -> 15%
where the time goes in v4:
time: 249 us; the launch traced here: 248 us
  Pallas kernels  78.8 us (32%)
  waiting for transfers between devices  77.5 us (31%)
  starting transfers between devices  76.5 us (31%)
  other arithmetic  8.49 us (3%)
  local copies, waits for them, and re-layouts  5.33 us (2%)
    pallas_call x6, Pallas kernels, call(): pl.pallas_call(kernel, out_shape=outs, in_specs=specs, out_specs=jax.tree...  78.8 us
    ppermute x10, waiting for transfers between devices, shift(): lax.ppermute(x, 'narrow', [(i, (i + 2 * chips) % n) for i in range(n)])  70.4 us
    all_to_all x4, starting transfers between devices, spread(): return lax.all_to_all(blocks, axes, split_axis=0, concat_axis=0, tiled=True)  34.5 us
    ppermute x6, starting transfers between devices, swap_cores(): return lax.ppermute(x, 'narrow', [(i, i ^ 1) for i in range(n)])  31.8 us
    ppermute x10, starting transfers between devices, shift(): lax.ppermute(x, 'narrow', [(i, (i + 2 * chips) % n) for i in range(n)])  10.3 us
  transfers between devices with their start and end apart: 20, of which 10 were waited for; matrix products, arithmetic and copies ran while one was open for 4% of the time, Pallas kernels for 15%

profile of v4, /device:TPU:1, one launch (start us, length us, event | category | flops | bytes accessed | tf_op | source)
XLA Modules:
  0.0 247.7 jit_solution(12007947013944521423)
XLA Ops:
  0.6 0.5 fusion.16.wa_ref
  1.2 1.0 fusion.17
  2.1 0.0 copy-start.16
  2.2 0.0 copy-start.17
  2.2 0.0 copy-start.18
  2.2 0.0 copy-start.1
  2.2 0.0 copy-start.2
  2.2 13.4 %stream_send.1 = bf16[256,64,128]{2,1,0:T(8,128)(2,1)} custom-call(f32[1,64]{1,0:T(1,128)} %fusion.16.wa_ref, bf16[2,64,8192]{2,1,0:T(8,128)(2,1)} %s_ref.1, bf16[256,128]{1,0:T(8,128)(2,1)} %constant.173.clone.g_ref, f32[64,128]{1,0:T(8,128)} %constant.174.clone.tc_ref, f32[64,128]{1,0:T(8,128)} %constant.175.clone.ts_ref, ...), custom_call_target="tpu_custom_call" | custom-call | flops 6000000000 | bytes 1048576 | tf_op jit(solution)/shard_map/stream_send/pallas_call | solution.py:128
  15.7 0.2 convert_reduce_fusion
  15.9 1.1 select_reduce_fusion
  17.0 22.4 %deposit.1 = (bf16[128,64,128]{2,1,0:T(8,128)(2,1)S(1)}, bf16[128,64,128]{2,1,0:T(8,128)(2,1)}) custom-call(s32[64,128]{1,0:T(8,128)S(1)} %get-tuple-element.38.idx_ref, s32[1,8192]{1,0:T(1,128)S(1)} %bitcast.73, f32[1,8192]{1,0:T(1,128)S(1)} %get-tuple-element.41.fy_ref, f32[1,8192]{1,0:T(1,128)S(1)} %get-tuple-element.40.fx_ref, f32[1,8192]{1,0:T(1,128)S(1)} %bitcast.72), custom_call_target="tpu_custom_call" | custom-call | flops 12000000000 | bytes 1048576 | tf_op jit(solution)/shard_map/deposit/pallas_call | solution.py:128
  39.4 1.4 collective-permute-start
  40.9 10.7 %all-to-all-start = ((bf16[128,2,64,128]{3,2,1,0:T(8,128)(2,1)}), bf16[128,2,64,128]{3,2,1,0:T(8,128)(2,1)}, u32[]{:S(2)}, u32[]{:S(2)}) async-start(bf16[128,2,64,128]{3,2,1,0:T(8,128)(2,1)} %bitcast.79), calls=%async_computation | async-start | bytes 8388608 | tf_op jit(solution)/shard_map/all_to_all | solution.py:456
  51.5 2.5 %add_convert_fusion = bf16[128,64,128]{2,1,0:T(8,128)(2,1)S(1)} fusion(bf16[128,64,128]{2,1,0:T(8,128)(2,1)} %collective-permute-done, bf16[128,64,128]{2,1,0:T(8,128)(2,1)S(1)} %get-tuple-element.17), kind=kLoop, calls=%fused_computation.2 | loop fusion | flops 4194304 | bytes 6291456 | tf_op jit(solution)/shard_map/convert_element_type | solution.py:470
  54.1 0.1 slice_bitcast_fusion.5
  54.2 1.5 collective-permute-start.1
  55.6 1.3 collective-permute-start.5
  56.9 1.4 collective-permute-start.3
  58.3 46.1 %collective-permute-done.1 = bf16[16,64,128]{2,1,0:T(8,128)(2,1)S(1)} collective-permute-done((bf16[16,64,128]{2,1,0:T(8,128)(2,1)S(1)}, bf16[16,64,128]{2,1,0:T(8,128)(2,1)S(1)}, u32[]{:S(2)}, u32[]{:S(2)}) %collective-permute-start.1) | collective-permute-done | bytes 262176 | tf_op jit(solution)/shard_map/ppermute | solution.py:466
  104.4 0.1 fusion.3
  104.5 0.1 collective-permute-start.2
  104.6 0.6 reduce-window.6
  105.2 0.2 slice_reduce_fusion
  105.5 0.0 copy-start.10
  105.5 0.0 copy-start.11
  105.5 0.3 collective-permute-start.4
  105.8 2.9 %collective-permute-done.3 = bf16[16,64,128]{2,1,0:T(8,128)(2,1)S(1)} collective-permute-done((bf16[16,64,128]{2,1,0:T(8,128)(2,1)S(1)}, bf16[16,64,128]{2,1,0:T(8,128)(2,1)S(1)}, u32[]{:S(2)}, u32[]{:S(2)}) %collective-permute-start.3) | collective-permute-done | bytes 262176 | tf_op jit(solution)/shard_map/ppermute | solution.py:466
  108.7 4.1 %collective-permute-done.2 = bf16[16,64,128]{2,1,0:T(8,128)(2,1)S(1)} collective-permute-done((bf16[16,64,128]{2,1,0:T(8,128)(2,1)S(1)}, bf16[16,64,128]{2,1,0:T(8,128)(2,1)S(1)}, u32[]{:S(2)}, u32[]{:S(2)}) %collective-permute-start.2) | collective-permute-done | bytes 262176 | tf_op jit(solution)/shard_map/ppermute | solution.py:466
  112.9 1.3 fusion.5
  114.1 0.1 collective-permute-start.6
  114.2 0.1 compare_bitcast_fusion
  114.3 0.1 select_reduce_fusion.2
  114.4 0.1 copy.35
  114.5 0.1 sub.60.idx_ref
  114.6 3.9 %collective-permute-done.4 = bf16[16,64,128]{2,1,0:T(8,128)(2,1)S(1)} collective-permute-done((bf16[16,64,128]{2,1,0:T(8,128)(2,1)S(1)}, bf16[16,64,128]{2,1,0:T(8,128)(2,1)S(1)}, u32[]{:S(2)}, u32[]{:S(2)}) %collective-permute-start.4) | collective-permute-done | bytes 262176 | tf_op jit(solution)/shard_map/ppermute | solution.py:466
  118.5 1.2 collective-permute-done.6
  119.7 1.1 fusion.2
  120.8 0.9 pad_maximum_fusion
  121.6 6.8 %all-to-all-start.2 = ((bf16[16,2,64,128]{3,2,1,0:T(8,128)(2,1)}), bf16[16,2,64,128]{3,2,1,0:T(8,128)(2,1)S(1)}, u32[]{:S(2)}, u32[]{:S(2)}) async-start(bf16[16,2,64,128]{3,2,1,0:T(8,128)(2,1)} %bitcast.21), calls=%async_computation.2 | async-start | bytes 1048576 | tf_op jit(solution)/shard_map/all_to_all | solution.py:456
  128.5 11.8 %stream_recv.1 = bf16[32,128,128]{2,1,0:T(8,128)(2,1)} custom-call(s32[1,32]{1,0:T(1,128)S(1)} %sub.60.idx_ref, bf16[256,64,128]{2,1,0:T(8,128)(2,1)} %bitcast.8.x_ref, bf16[256,256]{1,0:T(8,128)(2,1)S(1)} %copy-done.6, f32[128,128]{1,0:T(8,128)S(1)} %copy-done.7, f32[128,128]{1,0:T(8,128)S(1)} %copy-done.11, bf16[128,256]{1,0:T(8,128)(2,1)S(1)} %copy-done.10), custom_call_target="tpu_custom_call" | custom-call | flops 6000000000 | bytes 1048576 | tf_op jit(solution)/shard_map/stream_recv/pallas_call | solution.py:128
  140.3 0.0 copy-start.14
  140.3 6.8 %all-to-all-start.1 = ((bf16[16,2,128,128]{3,2,1,0:T(8,128)(2,1)}), bf16[16,2,128,128]{3,2,1,0:T(8,128)(2,1)S(1)}, u32[]{:S(2)}, u32[]{:S(2)}) async-start(bf16[16,2,128,128]{3,2,1,0:T(8,128)(2,1)} %bitcast.19), calls=%async_computation.1 | async-start | bytes 2097152 | tf_op jit(solution)/shard_map/all_to_all | solution.py:456
  147.2 7.1 %dye_send.1 = bf16[256,32,128]{2,1,0:T(8,128)(2,1)} custom-call(s32[1,32]{1,0:T(1,128)S(1)} %sub.60.idx_ref, bf16[64,8192]{1,0:T(8,128)(2,1)S(1)} %copy-done, bf16[32,64,128]{2,1,0:T(8,128)(2,1)S(1)} %bitcast.71, bf16[128,64]{1,0:T(8,128)(2,1)S(1)} %copy-done.14, f32[64,128]{1,0:T(8,128)S(1)} %copy-done.12, f32[64,128]{1,0:T(8,128)S(1)} %copy-done.13, ...), custom_call_target="tpu_custom_call" | custom-call | flops 4000000000 | bytes 1048576 | tf_op jit(solution)/shard_map/dye_send/pallas_call | solution.py:128
  154.2 4.8 %all-to-all-done.1 = bf16[16,2,128,128]{3,2,1,0:T(8,128)(2,1)S(1)} async-done(((bf16[16,2,128,128]{3,2,1,0:T(8,128)(2,1)}), bf16[16,2,128,128]{3,2,1,0:T(8,128)(2,1)S(1)}, u32[]{:S(2)}, u32[]{:S(2)}) %all-to-all-start.1) | async-done | bytes 1048608 | tf_op jit(solution)/shard_map/all_to_all | solution.py:456
  159.1 2.7 %collective-permute-start.7 = (bf16[32,128,128]{2,1,0:T(8,128)(2,1)S(1)}, bf16[32,128,128]{2,1,0:T(8,128)(2,1)}, u32[]{:S(2)}, u32[]{:S(2)}) collective-permute-start(bf16[32,128,128]{2,1,0:T(8,128)(2,1)S(1)} %bitcast.68), channel_id=1, source_target_pairs={{0,6},{1,7},{2,0},{3,1},{4,2},{5,3},{6,4},{7,5},{8,14},{9,15},{10,... | collective-permute-start | bytes 3145736 | tf_op jit(solution)/shard_map/ppermute | solution.py:466
  161.8 10.2 %all-to-all-start.3 = ((bf16[128,2,32,128]{3,2,1,0:T(8,128)(2,1)}), bf16[128,2,32,128]{3,2,1,0:T(8,128)(2,1)S(1)}, u32[]{:S(2)}, u32[]{:S(2)}) async-start(bf16[128,2,32,128]{3,2,1,0:T(8,128)(2,1)} %bitcast.23), calls=%async_computation.3 | async-start | bytes 4194304 | tf_op jit(solution)/shard_map/all_to_all | solution.py:456
  172.0 1.3 collective-permute-start.11
  173.3 5.6 %collective-permute-done.8.refs_4_ = bf16[32,128,128]{2,1,0:T(8,128)(2,1)} collective-permute-done((bf16[32,128,128]{2,1,0:T(8,128)(2,1)S(1)}, bf16[32,128,128]{2,1,0:T(8,128)(2,1)}, u32[]{:S(2)}, u32[]{:S(2)}) %collective-permute-start.8) | collective-permute-done | bytes 1048608 | tf_op jit(solution)/shard_map/ppermute | solution.py:466
  178.8 1.1 slice.65
  179.9 0.1 collective-permute-start.9
  180.0 21.2 %collective-permute-start.15 = (bf16[32,128,128]{2,1,0:T(8,128)(2,1)}, bf16[32,128,128]{2,1,0:T(8,128)(2,1)S(1)}, u32[]{:S(2)}, u32[]{:S(2)}) collective-permute-start(bf16[32,128,128]{2,1,0:T(8,128)(2,1)} %collective-permute-done.8.refs_4_), channel_id=1, source_target_pairs={{0,1},{1,0},{2,3},{3,2},{4,5},{5,4},{6,7},{7,6},{8,9},{9,8},{10,11... | collective-permute-start | bytes 3145736 | tf_op jit(solution)/shard_map/ppermute | solution.py:461
  201.2 1.1 slice.66
  202.2 0.1 collective-permute-start.12
  202.3 2.9 %collective-permute-start.10 = (bf16[16,128,128]{2,1,0:T(8,128)(2,1)S(1)}, bf16[16,128,128]{2,1,0:T(8,128)(2,1)S(1)}, u32[]{:S(2)}, u32[]{:S(2)}) collective-permute-start(bf16[16,128,128]{2,1,0:T(8,128)(2,1)S(1)} %slice.66), channel_id=1, source_target_pairs={{0,6},{1,7},{2,0},{3,1},{4,2},{5,3},{6,4},{7,5},{8,14},{9,15},{10,... | collective-permute-start | bytes 1572872 | tf_op jit(solution)/shard_map/ppermute | solution.py:466
  205.3 6.5 %collective-permute-done.9.refs_2_ = bf16[16,128,128]{2,1,0:T(8,128)(2,1)S(1)} collective-permute-done((bf16[16,128,128]{2,1,0:T(8,128)(2,1)S(1)}, bf16[16,128,128]{2,1,0:T(8,128)(2,1)S(1)}, u32[]{:S(2)}, u32[]{:S(2)}) %collective-permute-start.9) | collective-permute-done | bytes 524320 | tf_op jit(solution)/shard_map/ppermute | solution.py:466
  211.8 7.8 %collective-permute-start.13 = (bf16[16,128,128]{2,1,0:T(8,128)(2,1)S(1)}, bf16[16,128,128]{2,1,0:T(8,128)(2,1)S(1)}, u32[]{:S(2)}, u32[]{:S(2)}) collective-permute-start(bf16[16,128,128]{2,1,0:T(8,128)(2,1)S(1)} %collective-permute-done.9.refs_2_), channel_id=1, source_target_pairs={{0,1},{1,0},{2,3},{3,2},{4,5},{5,4},{6,7},{7,6},{8,9},{9,8},{10,11... | collective-permute-start | bytes 1572872 | tf_op jit(solution)/shard_map/ppermute | solution.py:461
  219.6 0.0 collective-permute-start.14
  219.6 1.5 collective-permute-done.13.refs_7_
  221.1 0.7 collective-permute-done.14.refs_8_
  221.9 17.1 %gather.1 = f32[2,8192]{1,0:T(2,128)} custom-call(s32[64,128]{1,0:T(8,128)S(1)} %get-tuple-element.39.base_ref, s32[1,8192]{1,0:T(1,128)S(1)} %bitcast.74, f32[1,8192]{1,0:T(1,128)S(1)} %get-tuple-element.41.fy_ref, f32[1,8192]{1,0:T(1,128)S(1)} %get-tuple-element.40.fx_ref, bf16[32,128,128]{2,1,0:T(8,128)(2,1)S(1)} %bitcast.70, ...), custom_call_target="tpu_custom_call" | custom-call | flops 10000000000 | bytes 1048576 | tf_op jit(solution)/shard_map/gather/pallas_call | solution.py:128
  238.9 0.0 copy-start.8
  239.0 0.8 copy-done.8
  239.8 0.8 copy-done.9
  240.6 7.1 %dye_recv.1 = f32[2,64,8192]{2,1,0:T(8,128)} custom-call(bf16[256,32,128]{2,1,0:T(8,128)(2,1)S(1)} %bitcast.66, bf16[256,256]{1,0:T(8,128)(2,1)S(1)} %copy-done.4, f32[128,128]{1,0:T(8,128)S(1)} %copy-done.8, f32[128,128]{1,0:T(8,128)S(1)} %copy-done.9, bf16[256,256]{1,0:T(8,128)(2,1)S(1)} %copy-done.3), custom_call_target="tpu_custom_call" | custom-call | flops 4000000000 | bytes 1048576 | tf_op jit(solution)/shard_map/dye_recv/pallas_call | solution.py:128
  (47 shorter events, 0.2 us)
Async XLA Ops:
  2.1 13.5 %copy-start.16 = (s32[16,256]{1,0:T(8,128)S(1)}, s32[16,256]{1,0:T(8,128)}, u32[]{:S(2)}) copy-start(s32[16,256]{1,0:T(8,128)} %param.31) | copy-start | bytes 49156
  2.2 13.7 %copy-start.17 = (s32[8192]{0:T(1024)S(1)}, s32[8192]{0:T(1024)}, u32[]{:S(2)}) copy-start(s32[8192]{0:T(1024)} %param.26) | copy-start | bytes 98308
  2.2 14.8 %copy-start.18 = (s32[8192]{0:T(1024)S(1)}, s32[8192]{0:T(1024)}, u32[]{:S(2)}) copy-start(s32[8192]{0:T(1024)} %param.27) | copy-start | bytes 98308
  2.2 14.8 %copy-start.1 = (f32[8192]{0:T(1024)S(1)}, f32[8192]{0:T(1024)}, u32[]{:S(2)}) copy-start(f32[8192]{0:T(1024)} %param.30) | copy-start | bytes 98308
  2.2 14.8 %copy-start.2 = (s32[8192]{0:T(1024)S(1)}, s32[8192]{0:T(1024)}, u32[]{:S(2)}) copy-start(s32[8192]{0:T(1024)} %param.28) | copy-start | bytes 98308
  39.4 12.1 %collective-permute-start = (bf16[128,64,128]{2,1,0:T(8,128)(2,1)}, bf16[128,64,128]{2,1,0:T(8,128)(2,1)}, u32[]{:S(2)}, u32[]{:S(2)}) collective-permute-start(bf16[128,64,128]{2,1,0:T(8,128)(2,1)} %get-tuple-element.18), channel_id=1, source_target_pairs={{0,1},{1,0},{2,3},{3,2},{4,5},{5,4},{6,7},{7,6},{8,9},{9,8},{10,11... | collective-permute-start | bytes 6291464 | tf_op jit(solution)/shard_map/ppermute | solution.py:461
  40.9 80.8 %all-to-all-start = ((bf16[128,2,64,128]{3,2,1,0:T(8,128)(2,1)}), bf16[128,2,64,128]{3,2,1,0:T(8,128)(2,1)}, u32[]{:S(2)}, u32[]{:S(2)}) async-start(bf16[128,2,64,128]{3,2,1,0:T(8,128)(2,1)} %bitcast.79), calls=%async_computation | async-start | bytes 8388608 | tf_op jit(solution)/shard_map/all_to_all | solution.py:456
  54.1 50.4 %copy-start.15 = (bf16[128,64,128]{2,1,0:T(8,128)(2,1)}, bf16[128,64,128]{2,1,0:T(8,128)(2,1)S(1)}, u32[]{:S(2)}) copy-start(bf16[128,64,128]{2,1,0:T(8,128)(2,1)S(1)} %add_convert_fusion) | copy-start | bytes 6291460
  54.2 50.3 %collective-permute-start.1 = (bf16[16,64,128]{2,1,0:T(8,128)(2,1)S(1)}, bf16[16,64,128]{2,1,0:T(8,128)(2,1)S(1)}, u32[]{:S(2)}, u32[]{:S(2)}) collective-permute-start(bf16[16,64,128]{2,1,0:T(8,128)(2,1)S(1)} %get-tuple-element.34), channel_id=1, source_target_pairs={{0,2},{1,3},{2,4},{3,5},{4,6},{5,7},{6,0},{7,1},{8,10},{9,11},{10,... | collective-permute-start | bytes 786440 | tf_op jit(solution)/shard_map/ppermute | solution.py:466
  55.6 50.2 %collective-permute-start.5 = (bf16[16,64,128]{2,1,0:T(8,128)(2,1)S(1)}, bf16[16,64,128]{2,1,0:T(8,128)(2,1)S(1)}, u32[]{:S(2)}, u32[]{:S(2)}) collective-permute-start(bf16[16,64,128]{2,1,0:T(8,128)(2,1)S(1)} %get-tuple-element.35), channel_id=1, source_target_pairs={{0,6},{1,7},{2,0},{3,1},{4,2},{5,3},{6,4},{7,5},{8,14},{9,15},{10,... | collective-permute-start | bytes 786440 | tf_op jit(solution)/shard_map/ppermute | solution.py:466
  56.9 51.8 %collective-permute-start.3 = (bf16[16,64,128]{2,1,0:T(8,128)(2,1)S(1)}, bf16[16,64,128]{2,1,0:T(8,128)(2,1)S(1)}, u32[]{:S(2)}, u32[]{:S(2)}) collective-permute-start(bf16[16,64,128]{2,1,0:T(8,128)(2,1)S(1)} %get-tuple-element.37), channel_id=1, source_target_pairs={{0,6},{1,7},{2,0},{3,1},{4,2},{5,3},{6,4},{7,5},{8,14},{9,15},{10,... | collective-permute-start | bytes 786440 | tf_op jit(solution)/shard_map/ppermute | solution.py:466
  104.5 8.3 %collective-permute-start.2 = (bf16[16,64,128]{2,1,0:T(8,128)(2,1)S(1)}, bf16[16,64,128]{2,1,0:T(8,128)(2,1)S(1)}, u32[]{:S(2)}, u32[]{:S(2)}) collective-permute-start(bf16[16,64,128]{2,1,0:T(8,128)(2,1)S(1)} %fusion.3), channel_id=1, source_target_pairs={{0,2},{1,3},{2,4},{3,5},{4,6},{5,7},{6,0},{7,1},{8,10},{9,11},{10,... | collective-permute-start | bytes 786440 | tf_op jit(solution)/shard_map/ppermute | solution.py:466
  105.5 23.0 %copy-start.6 = (bf16[256,256]{1,0:T(8,128)(2,1)S(1)}, bf16[256,256]{1,0:T(8,128)(2,1)}, u32[]{:S(2)}) copy-start(bf16[256,256]{1,0:T(8,128)(2,1)} %constant.177.clone.w1_ref) | copy-start | bytes 393220
  105.5 23.0 %copy-start.7 = (f32[128,128]{1,0:T(8,128)S(1)}, f32[128,128]{1,0:T(8,128)}, u32[]{:S(2)}) copy-start(f32[128,128]{1,0:T(8,128)} %constant.178.clone.tc_ref) | copy-start | bytes 196612
  105.5 23.0 %copy-start.10 = (bf16[128,256]{1,0:T(8,128)(2,1)S(1)}, bf16[128,256]{1,0:T(8,128)(2,1)}, u32[]{:S(2)}) copy-start(bf16[128,256]{1,0:T(8,128)(2,1)} %constant.180.clone.v_ref) | copy-start | bytes 196612
  105.5 23.0 %copy-start.11 = (f32[128,128]{1,0:T(8,128)S(1)}, f32[128,128]{1,0:T(8,128)}, u32[]{:S(2)}) copy-start(f32[128,128]{1,0:T(8,128)} %constant.179.clone.ts_ref) | copy-start | bytes 196612
  105.5 13.0 %collective-permute-start.4 = (bf16[16,64,128]{2,1,0:T(8,128)(2,1)S(1)}, bf16[16,64,128]{2,1,0:T(8,128)(2,1)S(1)}, u32[]{:S(2)}, u32[]{:S(2)}) collective-permute-start(bf16[16,64,128]{2,1,0:T(8,128)(2,1)S(1)} %get-tuple-element.36), channel_id=1, source_target_pairs={{0,2},{1,3},{2,4},{3,5},{4,6},{5,7},{6,0},{7,1},{8,10},{9,11},{10,... | collective-permute-start | bytes 786440 | tf_op jit(solution)/shard_map/ppermute | solution.py:466
  114.1 5.6 %collective-permute-start.6 = (bf16[16,64,128]{2,1,0:T(8,128)(2,1)S(1)}, bf16[16,64,128]{2,1,0:T(8,128)(2,1)S(1)}, u32[]{:S(2)}, u32[]{:S(2)}) collective-permute-start(bf16[16,64,128]{2,1,0:T(8,128)(2,1)S(1)} %get-tuple-element.33), channel_id=1, source_target_pairs={{0,6},{1,7},{2,0},{3,1},{4,2},{5,3},{6,4},{7,5},{8,14},{9,15},{10,... | collective-permute-start | bytes 786440 | tf_op jit(solution)/shard_map/ppermute | solution.py:466
  121.6 18.7 %all-to-all-start.2 = ((bf16[16,2,64,128]{3,2,1,0:T(8,128)(2,1)}), bf16[16,2,64,128]{3,2,1,0:T(8,128)(2,1)S(1)}, u32[]{:S(2)}, u32[]{:S(2)}) async-start(bf16[16,2,64,128]{3,2,1,0:T(8,128)(2,1)} %bitcast.21), calls=%async_computation.2 | async-start | bytes 1048576 | tf_op jit(solution)/shard_map/all_to_all | solution.py:456
  140.3 6.8 %copy-start = (bf16[64,8192]{1,0:T(8,128)(2,1)S(1)}, bf16[64,8192]{1,0:T(8,128)(2,1)}, u32[]{:S(2)}) copy-start(bf16[64,8192]{1,0:T(8,128)(2,1)} %dye_ref) | copy-start | bytes 3145732
  140.3 6.9 %copy-start.5 = (bf16[256,256]{1,0:T(8,128)(2,1)S(1)}, bf16[256,256]{1,0:T(8,128)(2,1)}, u32[]{:S(2)}) copy-start(bf16[256,256]{1,0:T(8,128)(2,1)} %constant.183.clone.w2_ref) | copy-start | bytes 393220
  140.3 6.9 %copy-start.12 = (f32[64,128]{1,0:T(8,128)S(1)}, f32[64,128]{1,0:T(8,128)}, u32[]{:S(2)}) copy-start(f32[64,128]{1,0:T(8,128)} %constant.174.clone.tc_ref) | copy-start | bytes 98308
  140.3 6.9 %copy-start.13 = (f32[64,128]{1,0:T(8,128)S(1)}, f32[64,128]{1,0:T(8,128)}, u32[]{:S(2)}) copy-start(f32[64,128]{1,0:T(8,128)} %constant.182.clone.ts_ref) | copy-start | bytes 98308
  140.3 6.9 %copy-start.14 = (bf16[128,64]{1,0:T(8,128)(2,1)S(1)}, bf16[128,64]{1,0:T(8,128)(2,1)}, u32[]{:S(2)}) copy-start(bf16[128,64]{1,0:T(8,128)(2,1)} %constant.181.clone.g_ref) | copy-start | bytes 49156
  140.3 18.8 %all-to-all-start.1 = ((bf16[16,2,128,128]{3,2,1,0:T(8,128)(2,1)}), bf16[16,2,128,128]{3,2,1,0:T(8,128)(2,1)S(1)}, u32[]{:S(2)}, u32[]{:S(2)}) async-start(bf16[16,2,128,128]{3,2,1,0:T(8,128)(2,1)} %bitcast.19), calls=%async_computation.1 | async-start | bytes 2097152 | tf_op jit(solution)/shard_map/all_to_all | solution.py:456
  159.1 19.7 %collective-permute-start.8 = (bf16[32,128,128]{2,1,0:T(8,128)(2,1)S(1)}, bf16[32,128,128]{2,1,0:T(8,128)(2,1)}, u32[]{:S(2)}, u32[]{:S(2)}) collective-permute-start(bf16[32,128,128]{2,1,0:T(8,128)(2,1)S(1)} %bitcast.67), channel_id=1, source_target_pairs={{0,2},{1,3},{2,4},{3,5},{4,6},{5,7},{6,0},{7,1},{8,10},{9,11},{10,... | collective-permute-start | bytes 3145736 | tf_op jit(solution)/shard_map/ppermute | solution.py:466
  159.1 42.1 %collective-permute-start.7 = (bf16[32,128,128]{2,1,0:T(8,128)(2,1)S(1)}, bf16[32,128,128]{2,1,0:T(8,128)(2,1)}, u32[]{:S(2)}, u32[]{:S(2)}) collective-permute-start(bf16[32,128,128]{2,1,0:T(8,128)(2,1)S(1)} %bitcast.68), channel_id=1, source_target_pairs={{0,6},{1,7},{2,0},{3,1},{4,2},{5,3},{6,4},{7,5},{8,14},{9,15},{10,... | collective-permute-start | bytes 3145736 | tf_op jit(solution)/shard_map/ppermute | solution.py:466
  161.8 77.2 %all-to-all-start.3 = ((bf16[128,2,32,128]{3,2,1,0:T(8,128)(2,1)}), bf16[128,2,32,128]{3,2,1,0:T(8,128)(2,1)S(1)}, u32[]{:S(2)}, u32[]{:S(2)}) async-start(bf16[128,2,32,128]{3,2,1,0:T(8,128)(2,1)} %bitcast.23), calls=%async_computation.3 | async-start | bytes 4194304 | tf_op jit(solution)/shard_map/all_to_all | solution.py:456
  172.0 47.6 %collective-permute-start.11 = (bf16[32,128,128]{2,1,0:T(8,128)(2,1)S(1)}, bf16[32,128,128]{2,1,0:T(8,128)(2,1)S(1)}, u32[]{:S(2)}, u32[]{:S(2)}) collective-permute-start(bf16[32,128,128]{2,1,0:T(8,128)(2,1)S(1)} %bitcast.69), channel_id=1, source_target_pairs={{0,1},{1,0},{2,3},{3,2},{4,5},{5,4},{6,7},{7,6},{8,9},{9,8},{10,11... | collective-permute-start | bytes 3145736 | tf_op jit(solution)/shard_map/ppermute | solution.py:461
  179.9 31.9 %collective-permute-start.9 = (bf16[16,128,128]{2,1,0:T(8,128)(2,1)S(1)}, bf16[16,128,128]{2,1,0:T(8,128)(2,1)S(1)}, u32[]{:S(2)}, u32[]{:S(2)}) collective-permute-start(bf16[16,128,128]{2,1,0:T(8,128)(2,1)S(1)} %slice.65), channel_id=1, source_target_pairs={{0,2},{1,3},{2,4},{3,5},{4,6},{5,7},{6,0},{7,1},{8,10},{9,11},{10,... | collective-permute-start | bytes 1572872 | tf_op jit(solution)/shard_map/ppermute | solution.py:466
  180.0 39.6 %collective-permute-start.15 = (bf16[32,128,128]{2,1,0:T(8,128)(2,1)}, bf16[32,128,128]{2,1,0:T(8,128)(2,1)S(1)}, u32[]{:S(2)}, u32[]{:S(2)}) collective-permute-start(bf16[32,128,128]{2,1,0:T(8,128)(2,1)} %collective-permute-done.8.refs_4_), channel_id=1, source_target_pairs={{0,1},{1,0},{2,3},{3,2},{4,5},{5,4},{6,7},{7,6},{8,9},{9,8},{10,11... | collective-permute-start | bytes 3145736 | tf_op jit(solution)/shard_map/ppermute | solution.py:461
  202.2 17.4 %collective-permute-start.12 = (bf16[32,128,128]{2,1,0:T(8,128)(2,1)}, bf16[32,128,128]{2,1,0:T(8,128)(2,1)S(1)}, u32[]{:S(2)}, u32[]{:S(2)}) collective-permute-start(bf16[32,128,128]{2,1,0:T(8,128)(2,1)} %collective-permute-done.7.refs_1_), channel_id=1, source_target_pairs={{0,1},{1,0},{2,3},{3,2},{4,5},{5,4},{6,7},{7,6},{8,9},{9,8},{10,11... | collective-permute-start | bytes 3145736 | tf_op jit(solution)/shard_map/ppermute | solution.py:461
  202.3 17.2 %collective-permute-start.10 = (bf16[16,128,128]{2,1,0:T(8,128)(2,1)S(1)}, bf16[16,128,128]{2,1,0:T(8,128)(2,1)S(1)}, u32[]{:S(2)}, u32[]{:S(2)}) collective-permute-start(bf16[16,128,128]{2,1,0:T(8,128)(2,1)S(1)} %slice.66), channel_id=1, source_target_pairs={{0,6},{1,7},{2,0},{3,1},{4,2},{5,3},{6,4},{7,5},{8,14},{9,15},{10,... | collective-permute-start | bytes 1572872 | tf_op jit(solution)/shard_map/ppermute | solution.py:466
  211.8 9.3 %collective-permute-start.13 = (bf16[16,128,128]{2,1,0:T(8,128)(2,1)S(1)}, bf16[16,128,128]{2,1,0:T(8,128)(2,1)S(1)}, u32[]{:S(2)}, u32[]{:S(2)}) collective-permute-start(bf16[16,128,128]{2,1,0:T(8,128)(2,1)S(1)} %collective-permute-done.9.refs_2_), channel_id=1, source_target_pairs={{0,1},{1,0},{2,3},{3,2},{4,5},{5,4},{6,7},{7,6},{8,9},{9,8},{10,11... | collective-permute-start | bytes 1572872 | tf_op jit(solution)/shard_map/ppermute | solution.py:461
  219.6 2.3 collective-permute-start.14
  221.9 17.1 %copy-start.3 = (bf16[256,256]{1,0:T(8,128)(2,1)S(1)}, bf16[256,256]{1,0:T(8,128)(2,1)}, u32[]{:S(2)}) copy-start(bf16[256,256]{1,0:T(8,128)(2,1)} %constant.186.clone.v_ref) | copy-start | bytes 393220
  221.9 17.1 %copy-start.4 = (bf16[256,256]{1,0:T(8,128)(2,1)S(1)}, bf16[256,256]{1,0:T(8,128)(2,1)}, u32[]{:S(2)}) copy-start(bf16[256,256]{1,0:T(8,128)(2,1)} %constant.184.clone.w1_ref) | copy-start | bytes 393220
  238.9 0.8 copy-start.8
  239.8 0.8 copy-start.9

commit v5 on v3

--- a/solution.py
+++ b/solution.py
@@ -144,7 +144,7 @@
         [SM] + [VM] * 5,
         [pltpu.VMEM((128 * PAD, 128), F32)] + [pltpu.VMEM((64 * PAD2, 128), F32)] * 2
         + [pltpu.VMEM((256 * PAD, 128), F32)],
-        int(6e9), 36, "stream_send",
+        int(6e9), 60, "stream_send",
         wa, stream, *send_tables(1.0, True),
     )
 
@@ -172,16 +172,17 @@
         out = lax.dot_general(v_ref[...], m, NT, preferred_element_type=F32)
         for h in range(2):
             for f in range(2):
-                of[pl.ds(4 * n + 2 * h + f, 64, stride=PAD2), :] = out[f * 64 : f * 64 + 64, h * 128 : h * 128 + 128]
+                of[pl.ds(64 * f + 2 * n + h, 64, stride=PAD2), :] = out[f * 64 : f * 64 + 64, h * 128 : h * 128 + 128]
         return carry
 
     lax.fori_loop(0, 32, step, 0, unroll=2)
 
     def store(n, carry):
         tile = jnp.maximum(idx_ref[0, n], 0)
-        data = of[pl.ds(pl.multiple_of(tile * PAD2, 8), 128), :].astype(BF)
-        for x in range(4):
-            o_ref[n // 2 * 8 + 2 * x + n % 2] = data
+        for f in range(2):
+            data = of[pl.ds(pl.multiple_of(tile * PAD2, 8) + 64 * f, 64), :].astype(BF)
+            for x in range(2):
+                o_ref[n // 2 * 8 + 4 * x + 2 * f + n % 2] = data
         return carry
 
     lax.fori_loop(0, 32, store, 0, unroll=2)
@@ -190,7 +191,7 @@
 def stream_recv(idx, x):
     return call(
         stream_recv_kernel,
-        jax.ShapeDtypeStruct((128, 128, 128), BF),
+        jax.ShapeDtypeStruct((128, 64, 128), BF),
         [SM] + [VM] * 5,
         [pltpu.VMEM((256 * PAD, 128), F32), pltpu.VMEM((64 * PAD2, 128), F32)],
         int(6e9), 28, "stream_recv",
@@ -213,11 +214,12 @@
         def _():
             g = n // 2
             e = n % 2
-            total = ret_ref[g * 8 + e].astype(F32)
-            for x in range(1, 4):
-                total = total + ret_ref[g * 8 + 2 * x + e].astype(F32)
-            at = pl.ds(pl.multiple_of(tile * PAD, 8), 64)
-            xs[at, :] = xs[at, :] + total
+            for half in range(2):
+                at = pl.ds(pl.multiple_of(tile * PAD, 8) + 32 * half, 32)
+                total = xs[at, :]
+                for x in range(2):
+                    total = total + ret_ref[g * 8 + 4 * x + 2 * half + e].astype(F32)
+                xs[at, :] = total
 
         return carry
 
@@ -331,10 +333,10 @@
 
     def clear(i, carry):
         for acc in accs:
-            acc[pl.ds(pl.multiple_of(i * 64, 64), 64), :] = jnp.zeros((64, 128), F32)
-        return carry
-
-    lax.fori_loop(0, 256, clear, 0, unroll=2)
+            acc[pl.ds(pl.multiple_of(i * 40, 8), 40), :] = jnp.zeros((40, 128), F32)
+        return carry
+
+    lax.fori_loop(0, 257, clear, 0)
 
     def weights(n, dst):
         xs = lax.broadcasted_iota(jnp.int32, (128, 128), 0)
@@ -363,15 +365,15 @@
     def chunk(n, carry):
         weights(2 * n + 1, wb)
         add(2 * n, wa)
-        weights(jnp.minimum(2 * n + 2, 63), wa)
+        weights(jnp.minimum(2 * n + 2, 127), wa)
         add(2 * n + 1, wb)
         return carry
 
-    lax.fori_loop(0, 32, chunk, 0)
+    lax.fori_loop(0, 64, chunk, 0)
 
     def store(i, carry):
-        for ref, base in ((keep_ref, 0), (send_ref, 8192)):
-            at = pl.ds(pl.multiple_of(i * 64 + base, 64), 64)
+        for ref, base in ((keep_ref, 8), (send_ref, 128 * 40 + 8)):
+            at = pl.ds(pl.multiple_of(i * 40 + base, 8), 32)
             total = accs[0][at, :]
             for acc in accs[1:]:
                 total = total + acc[at, :]
@@ -384,32 +386,30 @@
 def deposit(idx, col, fy, fx, am):
     return call(
         deposit_kernel,
-        [jax.ShapeDtypeStruct((128, 64, 128), BF)] * 2,
+        [jax.ShapeDtypeStruct((128, 32, 128), BF)] * 2,
         [SM] + [VM] * 4,
-        [pltpu.VMEM((256, 128), F32)] * 2 + [pltpu.VMEM((16384, 128), F32)] * 4,
-        int(1.2e10), 44, "deposit",
+        [pltpu.VMEM((256, 128), F32)] * 2 + [pltpu.VMEM((257 * 40, 128), F32)] * 4,
+        int(2e10), 30, "deposit",
         idx, col, fy, fx, am,
     )
 
 
 def gather_kernel(base_ref, a_ref, b_ref, col_ref, fy_ref, fx_ref, o_ref, st, ga, gb):
     def load(i, carry):
-        at = pl.multiple_of(i * 128, 128)
-        st[pl.ds(at, 128), :] = a_ref[i].astype(F32)
-        st[pl.ds(at + 16384, 128), :] = b_ref[i].astype(F32)
+        at = pl.multiple_of(i * 64, 64)
+        st[pl.ds(at, 64), :] = a_ref[i].astype(F32)
+        st[pl.ds(at + 8192, 64), :] = b_ref[i].astype(F32)
         return carry
 
     lax.fori_loop(0, 128, load, 0, unroll=4)
 
     def fetch(n, g):
         for f in range(128):
-            g[f * 4 : f * 4 + 4, :] = st[pl.ds(base_ref[n, f], 4), :]
+            g[f * 2 : f * 2 + 2, :] = st[pl.ds(base_ref[n, f], 2), :]
 
     def mix(n, g):
         sub = lax.broadcasted_iota(jnp.int32, (8, 128), 0)
-        off = lax.broadcasted_iota(jnp.int32, (8, 128), 1) - sub // 4
-        upper = sub % 4 >= 2
-        odd = sub % 2 == 1
+        off = lax.broadcasted_iota(jnp.int32, (8, 128), 1) - sub // 2
         xs = lax.broadcasted_iota(jnp.int32, (128, 128), 0)
         at = pl.ds(pl.multiple_of(n * 128, 128), 128)
         col = col_ref[:, at]
@@ -421,34 +421,33 @@
         lo = (w - hi.astype(F32)).astype(BF)
         z = jnp.dot(g[...].astype(BF), jnp.concatenate([hi, lo], axis=1), preferred_element_type=F32)
         parts = [jnp.zeros((8, 128), F32) for _ in range(4)]
-        for i in range(64):
-            keep = off == 2 * i
+        for i in range(32):
+            keep = off == 4 * i
             for h in range(2):
                 k = 2 * h + i % 2
                 parts[k] = parts[k] + jnp.where(keep, z[8 * i : 8 * i + 8, h * 128 : h * 128 + 128], 0.0)
-        total = (parts[0] + parts[1] + (parts[2] + parts[3])) * jnp.where(upper, fy, 1.0 - fy)
-        o_ref[0:1, at] = jnp.sum(jnp.where(odd, 0.0, total), axis=0, keepdims=True)
-        o_ref[1:2, at] = jnp.sum(jnp.where(odd, total, 0.0), axis=0, keepdims=True)
+        total = (parts[0] + parts[1] + (parts[2] + parts[3])) * jnp.where(sub % 2 == 1, fy, 1.0 - fy)
+        o_ref[:, at] = jnp.sum(total, axis=0, keepdims=True)
 
     fetch(0, ga)
 
     def chunk(n, carry):
         fetch(2 * n + 1, gb)
         mix(2 * n, ga)
-        fetch(jnp.minimum(2 * n + 2, 63), ga)
+        fetch(jnp.minimum(2 * n + 2, 127), ga)
         mix(2 * n + 1, gb)
         return carry
 
-    lax.fori_loop(0, 32, chunk, 0)
+    lax.fori_loop(0, 64, chunk, 0)
 
 
 def gather(base, a, b, col, fy, fx):
     return call(
         gather_kernel,
-        jax.ShapeDtypeStruct((2, 8192), F32),
+        jax.ShapeDtypeStruct((1, 16384), F32),
         [SM] + [VM] * 5,
-        [pltpu.VMEM((32768, 128), F32)] + [pltpu.VMEM((512, 128), F32)] * 2,
-        int(1e10), 30, "gather",
+        [pltpu.VMEM((16384, 128), F32)] + [pltpu.VMEM((256, 128), F32)] * 2,
+        int(1e10), 20, "gather",
         base, a, b, col, fy, fx,
     )
 
@@ -463,23 +462,34 @@
 def swap_cores(x):
     n = lax.axis_size("narrow")
     return lax.ppermute(x, "narrow", [(i, i ^ 1) for i in range(n)])
+
+
+def swap_chips(x):
+    n = lax.axis_size("narrow")
+    return lax.ppermute(x, "narrow", [(i, i ^ 2) for i in range(n)])
 
 
 def shards(stream_hat, dye, float_slot, float_row, float_col, float_frac, float_dye, tile_lists):
     device = lax.axis_index(AXES)
     group = lax.axis_index("wide")
     core = lax.axis_index("narrow") % 2
+    side = lax.axis_index("narrow") // 2 % 2
     wave = device * 64 + jnp.arange(64)
     wave = jnp.where(wave >= 4096, wave - 8192, wave).astype(F32)[None]
+
+    floats = (float_slot, float_row, float_col, float_frac, float_dye)
+    theirs = [swap_chips(x) for x in floats]
     spec = stream_send(stream_hat, wave)
-    spec, float_slot, tile_lists = lax.optimization_barrier((spec, float_slot, tile_lists))
+    spec, theirs, tile_lists = lax.optimization_barrier((spec, theirs, tile_lists))
     spec = spread(spec.reshape(128, 2, 64, 128)).reshape(256, 64, 128)
-
-    slot = float_slot.reshape(64, 128)
-    row = float_row.reshape(64, 128)
-    col = float_col.reshape(1, 8192)
-    fy = float_frac[0:1]
-    fx = float_frac[1:2]
+    slot, row, col, frac, amount = [
+        jnp.concatenate([x, y], axis=-1) for x, y in zip(floats, theirs)
+    ]
+    slot = slot.reshape(128, 128)
+    row = row.reshape(128, 128)
+    col = col.reshape(1, 16384)
+    fy = frac[0:1]
+    fx = frac[1:2]
 
     own_list = lax.dynamic_index_in_dim(tile_lists, group, 0, keepdims=False)
     holder = own_list // 64
@@ -497,7 +507,9 @@
         [jnp.sum(jnp.where(mine & (place == e), local, 0), axis=1) for e in range(CAPO)], axis=1
     ).reshape(1, 32) - 1
 
-    keep, send = deposit(pos * 64 + row, col, fy, fx, float_dye.reshape(1, 8192))
+    level = row - 32 * side
+    base = jnp.where((level >= -1) & (level <= 31), pos * 40 + 8 + level, 0)
+    keep, send = deposit(base, col, fy, fx, amount.reshape(1, 16384))
     dep = (keep.astype(F32) + swap_cores(send).astype(F32)).astype(BF)
     returned = spread(dep)
     spec, dep = lax.optimization_barrier((spec, dep))
@@ -509,8 +521,12 @@
     own, front = lax.optimization_barrier((own, front))
     other = swap_cores(own)
     front = spread(front.reshape(128, 2, 32, 128)).reshape(256, 32, 128)
-    velocity = gather(pos * 128 + 2 * row, own, other, col, fy, fx)
-    velocity, front = lax.optimization_barrier((velocity, front))
+
+    speed = gather(pos * 64 + row, own, other, col, fy, fx).reshape(2, 8192)
+    speed, front = lax.optimization_barrier((speed, front))
+    mine = speed[0]
+    back = swap_chips(speed[1])
+    velocity = jnp.stack([jnp.where(side == 0, mine, back), jnp.where(side == 0, back, mine)])
     dye_hat = dye_recv(front)
     return (velocity, dye_hat)
 

time: 219 us -> 189 us (0.86)
  waiting for transfers between devices: 99.1 us -> 37.1 us
  Pallas kernels: 74.1 us -> 106 us
  local copies, waits for them, and re-layouts: 11.5 us -> 3.35 us
  starting transfers between devices: 28.3 us -> 33.4 us
  other arithmetic: 4.5 us -> 7.31 us
    all_to_all x4, waiting for transfers between devices: 92.1 us -> 34.7 us  [spread(): return lax.all_to_all(blocks, AXES, split_axis=0, concat_axis=0, tiled=True)]
    pallas_call x6, Pallas kernels: 74.1 us -> 106 us  [call(): pl.pallas_call(kernel, out_shape=outs, in_specs=specs, out_specs=jax.tree...]
    unnamed x52 -> x37, local copies, waits for them, and re-layouts: 11.1 us -> 2.26 us
    ppermute x0 -> x6, starting transfers between devices: none -> 5.22 us  [swap_chips(): return lax.ppermute(x, 'narrow', [(i, i ^ 2) for i in range(n)])]
    ppermute x2, waiting for transfers between devices: 6.94 us -> 2.32 us  [swap_cores(): return lax.ppermute(x, 'narrow', [(i, i ^ 1) for i in range(n)])]
  transfers between devices with their start and end apart: 6 -> 12, of which waited for: 6 -> 6; matrix products, arithmetic and copies ran while one was open for 2% -> 4% of each run, Pallas kernels for 26% -> 56%
where the time goes in v5:
time: 189 us
  Pallas kernels  106 us (56%)
  waiting for transfers between devices  37.1 us (20%)
  starting transfers between devices  33.4 us (18%)
  other arithmetic  7.31 us (4%)
  local copies, waits for them, and re-layouts  3.35 us (2%)
    pallas_call x6, Pallas kernels, call(): pl.pallas_call(kernel, out_shape=outs, in_specs=specs, out_specs=jax.tree...  106 us
    all_to_all x4, waiting for transfers between devices, spread(): return lax.all_to_all(blocks, AXES, split_axis=0, concat_axis=0, tiled=True)  34.7 us
    all_to_all x4, starting transfers between devices, spread(): return lax.all_to_all(blocks, AXES, split_axis=0, concat_axis=0, tiled=True)  26.1 us
    ppermute x6, starting transfers between devices, swap_chips(): return lax.ppermute(x, 'narrow', [(i, i ^ 2) for i in range(n)])  5.22 us
  transfers between devices with their start and end apart: 12, of which 6 were waited for; matrix products, arithmetic and copies ran while one was open for 4% of the time, Pallas kernels for 56%

profile of v5, /device:TPU:1, one launch (start us, length us, event | category | flops | bytes accessed | tf_op | source)
XLA Modules:
  0.0 188.5 jit_solution(16191211642760342282)
XLA Ops:
  0.6 2.1 %collective-permute-start = (s32[8192]{0:T(1024)}, s32[8192]{0:T(1024)S(1)}, u32[]{:S(2)}, u32[]{:S(2)}) collective-permute-start(s32[8192]{0:T(1024)} %param.26), channel_id=1, source_target_pairs={{0,2},{1,3},{2,0},{3,1},{4,6},{5,7},{6,4},{7,5},{8,10},{9,11},{10,... | collective-permute-start | bytes 98312 | tf_op jit(solution)/shard_map/ppermute | solution.py:469
  2.7 0.1 collective-permute-start.1
  2.8 1.4 collective-permute-start.2
  4.2 0.1 collective-permute-start.3
  4.3 1.4 collective-permute-start.4
  5.7 0.8 constant_dynamic-update-slice_fusion.1
  6.5 0.5 fusion.6.wa_ref
  7.0 13.4 %stream_send.1 = bf16[256,64,128]{2,1,0:T(8,128)(2,1)} custom-call(f32[1,64]{1,0:T(1,128)} %fusion.6.wa_ref, bf16[2,64,8192]{2,1,0:T(8,128)(2,1)} %s_ref.1, bf16[256,128]{1,0:T(8,128)(2,1)} %constant.132.clone.g_ref, f32[64,128]{1,0:T(8,128)} %constant.133.clone.tc_ref, f32[64,128]{1,0:T(8,128)} %constant.134.clone.ts_ref, ...), custom_call_target="tpu_custom_call" | custom-call | flops 6000000000 | bytes 1048576 | tf_op jit(solution)/shard_map/stream_send/pallas_call | solution.py:128
  20.5 0.0 collective-permute-done
  20.5 0.0 collective-permute-done.1
  20.5 0.0 collective-permute-done.2
  20.5 0.0 collective-permute-done.4
  20.5 0.0 collective-permute-done.3
  20.5 0.0 copy-done.13
  20.6 0.0 copy-start.14
  20.6 0.0 copy-start.15
  20.6 0.0 copy-start.16
  20.6 0.0 copy-start.17
  20.6 12.2 %all-to-all-start = ((bf16[128,2,64,128]{3,2,1,0:T(8,128)(2,1)}), bf16[128,2,64,128]{3,2,1,0:T(8,128)(2,1)}, u32[]{:S(2)}, u32[]{:S(2)}) async-start(bf16[128,2,64,128]{3,2,1,0:T(8,128)(2,1)} %bitcast.40), calls=%async_computation | async-start | bytes 8388608 | tf_op jit(solution)/shard_map/all_to_all | solution.py:459
  32.9 0.0 copy-done.14
  32.9 0.1 fusion.7
  33.0 0.0 copy-done.15
  33.0 0.2 convert_reduce_fusion
  33.2 0.0 copy-done.16
  33.3 1.7 select_reduce_fusion
  35.0 0.0 copy-done.17
  35.0 40.1 %deposit.1 = (bf16[128,32,128]{2,1,0:T(8,128)(2,1)S(1)}, bf16[128,32,128]{2,1,0:T(8,128)(2,1)S(1)}) custom-call(s32[128,128]{1,0:T(8,128)S(1)} %get-tuple-element.42.idx_ref, s32[1,16384]{1,0:T(1,128)S(1)} %bitcast.37, f32[1,16384]{1,0:T(1,128)S(1)} %get-tuple-element.41.fy_ref, f32[1,16384]{1,0:T(1,128)S(1)} %get-tuple-element.40.fx_ref, ...), custom_call_target="tpu_custom_call" | custom-call | flops 20000000000 | bytes 1048576 | tf_op jit(solution)/shard_map/deposit/pallas_call | solution.py:128
  75.1 0.0 copy-start.6
  75.2 0.0 copy-start.8
  75.2 0.0 copy-start.9
  75.2 1.1 collective-permute-start.5
  76.4 0.6 reduce-window.6
  76.9 1.8 collective-permute-done.5
  78.7 2.5 %add_convert_fusion = bf16[128,32,128]{2,1,0:T(8,128)(2,1)} fusion(bf16[128,32,128]{2,1,0:T(8,128)(2,1)} %collective-permute-done.5, bf16[128,32,128]{2,1,0:T(8,128)(2,1)S(1)} %get-tuple-element.25), kind=kLoop, calls=%fused_computation.2 | loop fusion | flops 2097152 | bytes 3145728 | tf_op jit(solution)/shard_map/convert_element_type | solution.py:513
  81.2 4.3 %all-to-all-done = bf16[128,2,64,128]{3,2,1,0:T(8,128)(2,1)} async-done(((bf16[128,2,64,128]{3,2,1,0:T(8,128)(2,1)}), bf16[128,2,64,128]{3,2,1,0:T(8,128)(2,1)}, u32[]{:S(2)}, u32[]{:S(2)}) %all-to-all-start) | async-done | bytes 4194336 | tf_op jit(solution)/shard_map/all_to_all | solution.py:459
  85.5 4.9 %all-to-all-start.2 = ((bf16[128,32,128]{2,1,0:T(8,128)(2,1)}), bf16[128,32,128]{2,1,0:T(8,128)(2,1)S(1)}, u32[]{:S(2)}, u32[]{:S(2)}) async-start(bf16[128,32,128]{2,1,0:T(8,128)(2,1)} %add_convert_fusion), calls=%async_computation.2 | async-start | bytes 2097152 | tf_op jit(solution)/shard_map/all_to_all | solution.py:459
  90.4 0.2 slice_reduce_fusion
  90.6 0.1 compare_bitcast_fusion
  90.7 0.1 select_reduce_fusion.2
  90.9 0.1 copy.35
  91.0 0.1 sub.44.idx_ref
  91.1 0.0 copy-done.5
  91.1 0.0 copy-done.6
  91.1 12.2 %stream_recv.1 = bf16[128,64,128]{2,1,0:T(8,128)(2,1)} custom-call(s32[1,32]{1,0:T(1,128)S(1)} %sub.44.idx_ref, bf16[256,64,128]{2,1,0:T(8,128)(2,1)} %bitcast.9.x_ref, bf16[256,256]{1,0:T(8,128)(2,1)S(1)} %copy-done.5, f32[128,128]{1,0:T(8,128)S(1)} %copy-done.6, f32[128,128]{1,0:T(8,128)S(1)} %copy-done.8, bf16[128,256]{1,0:T(8,128)(2,1)S(1)} %copy-done.9), custom_call_target="tpu_custom_call" | custom-call | flops 6000000000 | bytes 1048576 | tf_op jit(solution)/shard_map/stream_recv/pallas_call | solution.py:128
  103.3 0.0 copy-start.12
  103.3 6.5 %all-to-all-done.2.ret_ref = bf16[128,32,128]{2,1,0:T(8,128)(2,1)S(1)} async-done(((bf16[128,32,128]{2,1,0:T(8,128)(2,1)}), bf16[128,32,128]{2,1,0:T(8,128)(2,1)S(1)}, u32[]{:S(2)}, u32[]{:S(2)}) %all-to-all-start.2) | async-done | bytes 1048608 | tf_op jit(solution)/shard_map/all_to_all | solution.py:459
  109.8 5.4 %all-to-all-start.1 = ((bf16[128,64,128]{2,1,0:T(8,128)(2,1)}), bf16[128,64,128]{2,1,0:T(8,128)(2,1)}, u32[]{:S(2)}, u32[]{:S(2)}) async-start(bf16[128,64,128]{2,1,0:T(8,128)(2,1)} %stream_recv.1), calls=%async_computation.1 | async-start | bytes 4194304 | tf_op jit(solution)/shard_map/all_to_all | solution.py:459
  115.2 5.8 %dye_send.1 = bf16[256,32,128]{2,1,0:T(8,128)(2,1)S(1)} custom-call(s32[1,32]{1,0:T(1,128)S(1)} %sub.44.idx_ref, bf16[64,8192]{1,0:T(8,128)(2,1)S(1)} %copy-done.1, bf16[128,32,128]{2,1,0:T(8,128)(2,1)S(1)} %all-to-all-done.2.ret_ref, bf16[128,64]{1,0:T(8,128)(2,1)S(1)} %copy-done.11, f32[64,128]{1,0:T(8,128)S(1)} %copy-done.10, f32[64,128]{1,0:T(8,128)S(1)} %copy-done.12, ...), custom_call_target="tpu_custom_call" | custom-call | flops 4000000000 | bytes 1048576 | tf_op jit(solution)/shard_map/dye_send/pallas_call | solution.py:128
  121.0 0.0 copy-start
  121.0 1.3 copy-done
  122.3 23.1 %all-to-all-done.1.a_ref = bf16[128,64,128]{2,1,0:T(8,128)(2,1)} async-done(((bf16[128,64,128]{2,1,0:T(8,128)(2,1)}), bf16[128,64,128]{2,1,0:T(8,128)(2,1)}, u32[]{:S(2)}, u32[]{:S(2)}) %all-to-all-start.1) | async-done | bytes 2097184 | tf_op jit(solution)/shard_map/all_to_all | solution.py:459
  145.5 0.9 collective-permute-start.6
  146.4 3.6 %all-to-all-start.3 = ((bf16[128,2,32,128]{3,2,1,0:T(8,128)(2,1)}), bf16[128,2,32,128]{3,2,1,0:T(8,128)(2,1)S(1)}, u32[]{:S(2)}, u32[]{:S(2)}) async-start(bf16[128,2,32,128]{3,2,1,0:T(8,128)(2,1)} %bitcast.36), calls=%async_computation.3 | async-start | bytes 4194304 | tf_op jit(solution)/shard_map/all_to_all | solution.py:459
  150.0 0.5 collective-permute-done.6.b_ref
  150.5 27.8 %gather.1 = f32[1,16384]{1,0:T(1,128)S(1)} custom-call(s32[128,128]{1,0:T(8,128)S(1)} %get-tuple-element.43.base_ref, bf16[128,64,128]{2,1,0:T(8,128)(2,1)} %all-to-all-done.1.a_ref, bf16[128,64,128]{2,1,0:T(8,128)(2,1)} %collective-permute-done.6.b_ref, s32[1,16384]{1,0:T(1,128)S(1)} %bitcast.38, f32[1,16384]{1,0:T(1,128)S(1)} %get-tuple-element.41.fy_ref, ...), custom_call_target="tpu_custom_call" | custom-call | flops 10000000000 | bytes 1048576 | tf_op jit(solution)/shard_map/gather/pallas_call | solution.py:128
  178.3 0.5 broadcast.191
  178.8 0.8 reduce.5
  179.7 0.8 all-to-all-done.3
  180.5 0.1 fusion.8
  180.6 0.2 collective-permute-start.7
  180.7 0.0 copy-done.3
  180.7 7.1 %dye_recv.1 = f32[2,64,8192]{2,1,0:T(8,128)} custom-call(bf16[256,32,128]{2,1,0:T(8,128)(2,1)S(1)} %bitcast.35, bf16[256,256]{1,0:T(8,128)(2,1)S(1)} %copy-done.2, f32[128,128]{1,0:T(8,128)S(1)} %copy-done.6, f32[128,128]{1,0:T(8,128)S(1)} %copy-done.7, bf16[256,256]{1,0:T(8,128)(2,1)S(1)} %copy-done.3), custom_call_target="tpu_custom_call" | custom-call | flops 4000000000 | bytes 1048576 | tf_op jit(solution)/shard_map/dye_recv/pallas_call | solution.py:128
  187.8 0.0 collective-permute-done.7
  187.8 0.7 pad_maximum_fusion.1
  (33 shorter events, 0.3 us)
Async XLA Ops:
  0.6 19.8 %collective-permute-start = (s32[8192]{0:T(1024)}, s32[8192]{0:T(1024)S(1)}, u32[]{:S(2)}, u32[]{:S(2)}) collective-permute-start(s32[8192]{0:T(1024)} %param.26), channel_id=1, source_target_pairs={{0,2},{1,3},{2,0},{3,1},{4,6},{5,7},{6,4},{7,5},{8,10},{9,11},{10,... | collective-permute-start | bytes 98312 | tf_op jit(solution)/shard_map/ppermute | solution.py:469
  2.7 17.7 %collective-permute-start.1 = (s32[8192]{0:T(1024)}, s32[8192]{0:T(1024)S(1)}, u32[]{:S(2)}, u32[]{:S(2)}) collective-permute-start(s32[8192]{0:T(1024)} %param.27), channel_id=1, source_target_pairs={{0,2},{1,3},{2,0},{3,1},{4,6},{5,7},{6,4},{7,5},{8,10},{9,11},{10,... | collective-permute-start | bytes 98312 | tf_op jit(solution)/shard_map/ppermute | solution.py:469
  2.8 17.6 %collective-permute-start.2 = (s32[8192]{0:T(1024)}, s32[8192]{0:T(1024)S(1)}, u32[]{:S(2)}, u32[]{:S(2)}) collective-permute-start(s32[8192]{0:T(1024)} %param.28), channel_id=1, source_target_pairs={{0,2},{1,3},{2,0},{3,1},{4,6},{5,7},{6,4},{7,5},{8,10},{9,11},{10,... | collective-permute-start | bytes 98312 | tf_op jit(solution)/shard_map/ppermute | solution.py:469
  4.2 16.3 %collective-permute-start.3 = (f32[2,8192]{1,0:T(2,128)}, f32[2,8192]{1,0:T(2,128)S(1)}, u32[]{:S(2)}, u32[]{:S(2)}) collective-permute-start(f32[2,8192]{1,0:T(2,128)} %param.29), channel_id=1, source_target_pairs={{0,2},{1,3},{2,0},{3,1},{4,6},{5,7},{6,4},{7,5},{8,10},{9,11},{10,... | collective-permute-start | bytes 196616 | tf_op jit(solution)/shard_map/ppermute | solution.py:469
  4.3 16.2 %collective-permute-start.4 = (f32[8192]{0:T(1024)}, f32[8192]{0:T(1024)S(1)}, u32[]{:S(2)}, u32[]{:S(2)}) collective-permute-start(f32[8192]{0:T(1024)} %param.30), channel_id=1, source_target_pairs={{0,2},{1,3},{2,0},{3,1},{4,6},{5,7},{6,4},{7,5},{8,10},{9,11},{10,... | collective-permute-start | bytes 98312 | tf_op jit(solution)/shard_map/ppermute | solution.py:469
  7.0 13.5 %copy-start.13 = (s32[16,256]{1,0:T(8,128)S(1)}, s32[16,256]{1,0:T(8,128)}, u32[]{:S(2)}) copy-start(s32[16,256]{1,0:T(8,128)} %param.31) | copy-start | bytes 49156
  20.6 12.3 %copy-start.14 = (s32[8192]{0:T(1024)S(1)}, s32[8192]{0:T(1024)}, u32[]{:S(2)}) copy-start(s32[8192]{0:T(1024)} %param.28) | copy-start | bytes 98308
  20.6 12.4 %copy-start.15 = (f32[8192]{0:T(1024)S(1)}, f32[8192]{0:T(1024)}, u32[]{:S(2)}) copy-start(f32[8192]{0:T(1024)} %param.30) | copy-start | bytes 98308
  20.6 12.6 %copy-start.16 = (s32[8192]{0:T(1024)S(1)}, s32[8192]{0:T(1024)}, u32[]{:S(2)}) copy-start(s32[8192]{0:T(1024)} %param.26) | copy-start | bytes 98308
  20.6 14.4 %copy-start.17 = (s32[8192]{0:T(1024)S(1)}, s32[8192]{0:T(1024)}, u32[]{:S(2)}) copy-start(s32[8192]{0:T(1024)} %param.27) | copy-start | bytes 98308
  20.6 64.9 %all-to-all-start = ((bf16[128,2,64,128]{3,2,1,0:T(8,128)(2,1)}), bf16[128,2,64,128]{3,2,1,0:T(8,128)(2,1)}, u32[]{:S(2)}, u32[]{:S(2)}) async-start(bf16[128,2,64,128]{3,2,1,0:T(8,128)(2,1)} %bitcast.40), calls=%async_computation | async-start | bytes 8388608 | tf_op jit(solution)/shard_map/all_to_all | solution.py:459
  75.1 15.9 %copy-start.5 = (bf16[256,256]{1,0:T(8,128)(2,1)S(1)}, bf16[256,256]{1,0:T(8,128)(2,1)}, u32[]{:S(2)}) copy-start(bf16[256,256]{1,0:T(8,128)(2,1)} %constant.136.clone.w1_ref) | copy-start | bytes 393220
  75.1 15.9 %copy-start.6 = (f32[128,128]{1,0:T(8,128)S(1)}, f32[128,128]{1,0:T(8,128)}, u32[]{:S(2)}) copy-start(f32[128,128]{1,0:T(8,128)} %constant.137.clone.tc_ref) | copy-start | bytes 196612
  75.2 15.9 %copy-start.8 = (f32[128,128]{1,0:T(8,128)S(1)}, f32[128,128]{1,0:T(8,128)}, u32[]{:S(2)}) copy-start(f32[128,128]{1,0:T(8,128)} %constant.138.clone.ts_ref) | copy-start | bytes 196612
  75.2 15.9 %copy-start.9 = (bf16[128,256]{1,0:T(8,128)(2,1)S(1)}, bf16[128,256]{1,0:T(8,128)(2,1)}, u32[]{:S(2)}) copy-start(bf16[128,256]{1,0:T(8,128)(2,1)} %constant.139.clone.v_ref) | copy-start | bytes 196612
  75.2 3.6 %collective-permute-start.5 = (bf16[128,32,128]{2,1,0:T(8,128)(2,1)S(1)}, bf16[128,32,128]{2,1,0:T(8,128)(2,1)}, u32[]{:S(2)}, u32[]{:S(2)}) collective-permute-start(bf16[128,32,128]{2,1,0:T(8,128)(2,1)S(1)} %get-tuple-element.26), channel_id=1, source_target_pairs={{0,1},{1,0},{2,3},{3,2},{4,5},{5,4},{6,7},{7,6},{8,9},{9,8},{10,11... | collective-permute-start | bytes 3145736 | tf_op jit(solution)/shard_map/ppermute | solution.py:464
  85.5 24.3 %all-to-all-start.2 = ((bf16[128,32,128]{2,1,0:T(8,128)(2,1)}), bf16[128,32,128]{2,1,0:T(8,128)(2,1)S(1)}, u32[]{:S(2)}, u32[]{:S(2)}) async-start(bf16[128,32,128]{2,1,0:T(8,128)(2,1)} %add_convert_fusion), calls=%async_computation.2 | async-start | bytes 2097152 | tf_op jit(solution)/shard_map/all_to_all | solution.py:459
  103.3 11.9 %copy-start.1 = (bf16[64,8192]{1,0:T(8,128)(2,1)S(1)}, bf16[64,8192]{1,0:T(8,128)(2,1)}, u32[]{:S(2)}) copy-start(bf16[64,8192]{1,0:T(8,128)(2,1)} %dye_ref) | copy-start | bytes 3145732
  103.3 11.9 %copy-start.4 = (bf16[256,256]{1,0:T(8,128)(2,1)S(1)}, bf16[256,256]{1,0:T(8,128)(2,1)}, u32[]{:S(2)}) copy-start(bf16[256,256]{1,0:T(8,128)(2,1)} %constant.142.clone.w2_ref) | copy-start | bytes 393220
  103.3 11.9 %copy-start.10 = (f32[64,128]{1,0:T(8,128)S(1)}, f32[64,128]{1,0:T(8,128)}, u32[]{:S(2)}) copy-start(f32[64,128]{1,0:T(8,128)} %constant.133.clone.tc_ref) | copy-start | bytes 98308
  103.3 11.9 %copy-start.11 = (bf16[128,64]{1,0:T(8,128)(2,1)S(1)}, bf16[128,64]{1,0:T(8,128)(2,1)}, u32[]{:S(2)}) copy-start(bf16[128,64]{1,0:T(8,128)(2,1)} %constant.140.clone.g_ref) | copy-start | bytes 49156
  103.3 11.9 %copy-start.12 = (f32[64,128]{1,0:T(8,128)S(1)}, f32[64,128]{1,0:T(8,128)}, u32[]{:S(2)}) copy-start(f32[64,128]{1,0:T(8,128)} %constant.141.clone.ts_ref) | copy-start | bytes 98308
  109.8 35.7 %all-to-all-start.1 = ((bf16[128,64,128]{2,1,0:T(8,128)(2,1)}), bf16[128,64,128]{2,1,0:T(8,128)(2,1)}, u32[]{:S(2)}, u32[]{:S(2)}) async-start(bf16[128,64,128]{2,1,0:T(8,128)(2,1)} %stream_recv.1), calls=%async_computation.1 | async-start | bytes 4194304 | tf_op jit(solution)/shard_map/all_to_all | solution.py:459
  121.0 1.3 copy-start
  145.5 5.1 %collective-permute-start.6 = (bf16[128,64,128]{2,1,0:T(8,128)(2,1)}, bf16[128,64,128]{2,1,0:T(8,128)(2,1)}, u32[]{:S(2)}, u32[]{:S(2)}) collective-permute-start(bf16[128,64,128]{2,1,0:T(8,128)(2,1)} %all-to-all-done.1.a_ref), channel_id=1, source_target_pairs={{0,1},{1,0},{2,3},{3,2},{4,5},{5,4},{6,7},{7,6},{8,9},{9,8},{10,11... | collective-permute-start | bytes 6291464 | tf_op jit(solution)/shard_map/ppermute | solution.py:464
  146.4 34.1 %all-to-all-start.3 = ((bf16[128,2,32,128]{3,2,1,0:T(8,128)(2,1)}), bf16[128,2,32,128]{3,2,1,0:T(8,128)(2,1)S(1)}, u32[]{:S(2)}, u32[]{:S(2)}) async-start(bf16[128,2,32,128]{3,2,1,0:T(8,128)(2,1)} %bitcast.36), calls=%async_computation.3 | async-start | bytes 4194304 | tf_op jit(solution)/shard_map/all_to_all | solution.py:459
  150.5 30.2 %copy-start.2 = (bf16[256,256]{1,0:T(8,128)(2,1)S(1)}, bf16[256,256]{1,0:T(8,128)(2,1)}, u32[]{:S(2)}) copy-start(bf16[256,256]{1,0:T(8,128)(2,1)} %constant.143.clone.w1_ref) | copy-start | bytes 393220
  150.5 30.2 %copy-start.3 = (bf16[256,256]{1,0:T(8,128)(2,1)S(1)}, bf16[256,256]{1,0:T(8,128)(2,1)}, u32[]{:S(2)}) copy-start(bf16[256,256]{1,0:T(8,128)(2,1)} %constant.145.clone.v_ref) | copy-start | bytes 393220
  150.5 30.2 %copy-start.7 = (f32[128,128]{1,0:T(8,128)S(1)}, f32[128,128]{1,0:T(8,128)}, u32[]{:S(2)}) copy-start(f32[128,128]{1,0:T(8,128)} %constant.144.clone.ts_ref) | copy-start | bytes 196612
  180.6 7.3 %collective-permute-start.7 = (f32[8192]{0:T(1024)S(1)}, f32[8192]{0:T(1024)S(1)}, u32[]{:S(2)}, u32[]{:S(2)}) collective-permute-start(f32[8192]{0:T(1024)S(1)} %bitcast.47), channel_id=1, source_target_pairs={{0,2},{1,3},{2,0},{3,1},{4,6},{5,7},{6,4},{7,5},{8,10},{9,11},{10,... | collective-permute-start | bytes 98312 | tf_op jit(solution)/shard_map/ppermute | solution.py:469

commit v6 on v5

--- a/solution.py
+++ b/solution.py
@@ -97,7 +97,7 @@
             tim[pl.ds(base + 64, 64), :] = wa * vre
         return carry
 
-    lax.fori_loop(0, 32, rows, 0, unroll=2)
+    lax.fori_loop(0, 32, rows, 0, unroll=8)
 
     def cols(n, carry):
         parts = []
@@ -111,7 +111,7 @@
             of[pl.ds(2 * n + h, 256, stride=PAD), :] = out[:, h * 128 : h * 128 + 128]
         return carry
 
-    lax.fori_loop(0, 32, cols, 0, unroll=2)
+    lax.fori_loop(0, 32, cols, 0, unroll=8)
 
     def store(i, carry):
         o_ref[i] = of[pl.ds(pl.multiple_of(i * PAD, 8), 64), :].astype(BF)
@@ -175,7 +175,7 @@
                 of[pl.ds(64 * f + 2 * n + h, 64, stride=PAD2), :] = out[f * 64 : f * 64 + 64, h * 128 : h * 128 + 128]
         return carry
 
-    lax.fori_loop(0, 32, step, 0, unroll=2)
+    lax.fori_loop(0, 32, step, 0, unroll=8)
 
     def store(n, carry):
         tile = jnp.maximum(idx_ref[0, n], 0)
@@ -238,7 +238,7 @@
             tim[pl.ds(base, 64), :] = re * ts + im * tc
         return carry
 
-    lax.fori_loop(0, 16, rows, 0, unroll=2)
+    lax.fori_loop(0, 16, rows, 0, unroll=8)
 
     def cols(n, carry):
         parts = []
@@ -251,7 +251,7 @@
             of[pl.ds(2 * n + h, 256, stride=PAD3), :] = out[:, h * 128 : h * 128 + 128]
         return carry
 
-    lax.fori_loop(0, 16, cols, 0, unroll=2)
+    lax.fori_loop(0, 16, cols, 0, unroll=8)
 
     def store(i, carry):
         o_ref[i] = of[pl.ds(pl.multiple_of(i * PAD3, 8), 32), :].astype(BF)
@@ -301,7 +301,7 @@
                     ]
         return carry
 
-    lax.fori_loop(0, 16, step, 0, unroll=2)
+    lax.fori_loop(0, 16, step, 0, unroll=8)
 
     def store(n, carry):
         c = n // 8
@@ -328,7 +328,9 @@
 CAPO = 2
 
 
-def deposit_kernel(idx_ref, col_ref, fy_ref, fx_ref, am_ref, keep_ref, send_ref, wa, wb, *accs):
+def deposit_kernel(idx_ref, col_ref, fy_ref, fx_ref, am_ref, keep_ref, send_ref, *refs):
+    bufs = refs[:4]
+    accs = refs[4:]
     ways = len(accs)
 
     def clear(i, carry):
@@ -360,16 +362,15 @@
             for k in range(ways):
                 accs[k][at[k], :] = new[k]
 
-    weights(0, wa)
+    weights(0, bufs[0])
 
     def chunk(n, carry):
-        weights(2 * n + 1, wb)
-        add(2 * n, wa)
-        weights(jnp.minimum(2 * n + 2, 127), wa)
-        add(2 * n + 1, wb)
-        return carry
-
-    lax.fori_loop(0, 64, chunk, 0)
+        for q in range(4):
+            weights(jnp.minimum(4 * n + q + 1, 127), bufs[(q + 1) % 4])
+            add(4 * n + q, bufs[q])
+        return carry
+
+    lax.fori_loop(0, 32, chunk, 0)
 
     def store(i, carry):
         for ref, base in ((keep_ref, 8), (send_ref, 128 * 40 + 8)):
@@ -388,13 +389,13 @@
         deposit_kernel,
         [jax.ShapeDtypeStruct((128, 32, 128), BF)] * 2,
         [SM] + [VM] * 4,
-        [pltpu.VMEM((256, 128), F32)] * 2 + [pltpu.VMEM((257 * 40, 128), F32)] * 4,
+        [pltpu.VMEM((256, 128), F32)] * 4 + [pltpu.VMEM((257 * 40, 128), F32)] * 4,
         int(2e10), 30, "deposit",
         idx, col, fy, fx, am,
     )
 
 
-def gather_kernel(base_ref, a_ref, b_ref, col_ref, fy_ref, fx_ref, o_ref, st, ga, gb):
+def gather_kernel(base_ref, a_ref, b_ref, col_ref, fy_ref, fx_ref, mine_ref, theirs_ref, st, *bufs):
     def load(i, carry):
         at = pl.multiple_of(i * 64, 64)
         st[pl.ds(at, 64), :] = a_ref[i].astype(F32)
@@ -407,7 +408,7 @@
         for f in range(128):
             g[f * 2 : f * 2 + 2, :] = st[pl.ds(base_ref[n, f], 2), :]
 
-    def mix(n, g):
+    def mix(n, g, o_ref, to):
         sub = lax.broadcasted_iota(jnp.int32, (8, 128), 0)
         off = lax.broadcasted_iota(jnp.int32, (8, 128), 1) - sub // 2
         xs = lax.broadcasted_iota(jnp.int32, (128, 128), 0)
@@ -419,34 +420,37 @@
         w = jnp.where(d == 0, 1.0 - fx, jnp.where(d == 1, fx, 0.0))
         hi = w.astype(BF)
         lo = (w - hi.astype(F32)).astype(BF)
-        z = jnp.dot(g[...].astype(BF), jnp.concatenate([hi, lo], axis=1), preferred_element_type=F32)
+        rows = g[...].astype(BF)
+        z = jnp.dot(
+            jnp.concatenate([rows, rows], axis=1),
+            jnp.concatenate([hi, lo], axis=0),
+            preferred_element_type=F32,
+        )
         parts = [jnp.zeros((8, 128), F32) for _ in range(4)]
         for i in range(32):
-            keep = off == 4 * i
-            for h in range(2):
-                k = 2 * h + i % 2
-                parts[k] = parts[k] + jnp.where(keep, z[8 * i : 8 * i + 8, h * 128 : h * 128 + 128], 0.0)
+            parts[i % 4] = jnp.where(off == 4 * i, z[8 * i : 8 * i + 8], parts[i % 4])
         total = (parts[0] + parts[1] + (parts[2] + parts[3])) * jnp.where(sub % 2 == 1, fy, 1.0 - fy)
-        o_ref[:, at] = jnp.sum(total, axis=0, keepdims=True)
-
-    fetch(0, ga)
-
-    def chunk(n, carry):
-        fetch(2 * n + 1, gb)
-        mix(2 * n, ga)
-        fetch(jnp.minimum(2 * n + 2, 127), ga)
-        mix(2 * n + 1, gb)
-        return carry
-
-    lax.fori_loop(0, 64, chunk, 0)
+        o_ref[:, pl.ds(pl.multiple_of(to * 128, 128), 128)] = jnp.sum(total, axis=0, keepdims=True)
+
+    fetch(0, bufs[0])
+    for half, o_ref in enumerate((mine_ref, theirs_ref)):
+
+        def chunk(n, carry, half=half, o_ref=o_ref):
+            for q in range(8):
+                at = half * 64 + 8 * n + q
+                fetch(jnp.minimum(at + 1, 127), bufs[(q + 1) % 8])
+                mix(at, bufs[q], o_ref, 8 * n + q)
+            return carry
+
+        lax.fori_loop(0, 8, chunk, 0)
 
 
 def gather(base, a, b, col, fy, fx):
     return call(
         gather_kernel,
-        jax.ShapeDtypeStruct((1, 16384), F32),
+        [jax.ShapeDtypeStruct((1, 8192), F32)] * 2,
         [SM] + [VM] * 5,
-        [pltpu.VMEM((16384, 128), F32)] + [pltpu.VMEM((256, 128), F32)] * 2,
+        [pltpu.VMEM((16384, 128), F32)] + [pltpu.VMEM((256, 128), F32)] * 8,
         int(1e10), 20, "gather",
         base, a, b, col, fy, fx,
     )
@@ -477,19 +481,22 @@
     wave = device * 64 + jnp.arange(64)
     wave = jnp.where(wave >= 4096, wave - 8192, wave).astype(F32)[None]
 
-    floats = (float_slot, float_row, float_col, float_frac, float_dye)
-    theirs = [swap_chips(x) for x in floats]
+    own_floats = jnp.concatenate(
+        [jnp.stack([float_slot, float_row, float_col]).astype(F32), float_frac, float_dye[None]]
+    )
+    their_floats = swap_chips(own_floats)
     spec = stream_send(stream_hat, wave)
-    spec, theirs, tile_lists = lax.optimization_barrier((spec, theirs, tile_lists))
+    spec, own_floats, their_floats, tile_lists = lax.optimization_barrier(
+        (spec, own_floats, their_floats, tile_lists)
+    )
     spec = spread(spec.reshape(128, 2, 64, 128)).reshape(256, 64, 128)
-    slot, row, col, frac, amount = [
-        jnp.concatenate([x, y], axis=-1) for x, y in zip(floats, theirs)
-    ]
-    slot = slot.reshape(128, 128)
-    row = row.reshape(128, 128)
-    col = col.reshape(1, 16384)
-    fy = frac[0:1]
-    fx = frac[1:2]
+    floats = jnp.concatenate([own_floats, their_floats], axis=1)
+    slot = floats[0].astype(jnp.int32).reshape(128, 128)
+    row = floats[1].astype(jnp.int32).reshape(128, 128)
+    col = floats[2:3].astype(jnp.int32)
+    fy = floats[3:4]
+    fx = floats[4:5]
+    amount = floats[5:6]
 
     own_list = lax.dynamic_index_in_dim(tile_lists, group, 0, keepdims=False)
     holder = own_list // 64
@@ -509,7 +516,7 @@
 
     level = row - 32 * side
     base = jnp.where((level >= -1) & (level <= 31), pos * 40 + 8 + level, 0)
-    keep, send = deposit(base, col, fy, fx, amount.reshape(1, 16384))
+    keep, send = deposit(base, col, fy, fx, amount)
     dep = (keep.astype(F32) + swap_cores(send).astype(F32)).astype(BF)
     returned = spread(dep)
     spec, dep = lax.optimization_barrier((spec, dep))
@@ -522,11 +529,10 @@
     other = swap_cores(own)
     front = spread(front.reshape(128, 2, 32, 128)).reshape(256, 32, 128)
 
-    speed = gather(pos * 64 + row, own, other, col, fy, fx).reshape(2, 8192)
-    speed, front = lax.optimization_barrier((speed, front))
-    mine = speed[0]
-    back = swap_chips(speed[1])
-    velocity = jnp.stack([jnp.where(side == 0, mine, back), jnp.where(side == 0, back, mine)])
+    mine, theirs = gather(pos * 64 + row, own, other, col, fy, fx)
+    mine, theirs, front = lax.optimization_barrier((mine, theirs, front))
+    back = swap_chips(theirs)
+    velocity = jnp.where(side == 0, jnp.concatenate([mine, back]), jnp.concatenate([back, mine]))
     dye_hat = dye_recv(front)
     return (velocity, dye_hat)
 

time: 189 us -> 183 us (0.968)
  Pallas kernels: 106 us -> 81.6 us
  waiting for transfers between devices: 37.1 us -> 51.6 us
  local copies, waits for them, and re-layouts: 3.35 us -> 8.26 us
  starting transfers between devices: 33.4 us -> 29.4 us
  other arithmetic: 7.31 us -> 9.97 us
    pallas_call x6, Pallas kernels: 106 us -> 81.6 us  [call(): pl.pallas_call(kernel, out_shape=outs, in_specs=specs, out_specs=jax.tree...]
    all_to_all x4, waiting for transfers between devices: 34.7 us -> 50.4 us  [spread(): return lax.all_to_all(blocks, AXES, split_axis=0, concat_axis=0, tiled=True)]
    unnamed x37 -> x35, local copies, waits for them, and re-layouts: 2.26 us -> 7.87 us
    ppermute x6 -> x2, starting transfers between devices: 5.22 us -> 2.18 us  [swap_chips(): return lax.ppermute(x, 'narrow', [(i, i ^ 2) for i in range(n)])]
  transfers between devices with their start and end apart: 12 -> 8, of which waited for: 6 -> 5; matrix products, arithmetic and copies ran while one was open for 4% -> 4% of each run, Pallas kernels for 56% -> 45%
where the time goes in v6:
time: 183 us; the launch traced here: 182 us
  Pallas kernels  81.6 us (45%)
  waiting for transfers between devices  51.6 us (28%)
  starting transfers between devices  29.4 us (16%)
  other arithmetic  9.97 us (5%)
  local copies, waits for them, and re-layouts  8.26 us (5%)
    pallas_call x6, Pallas kernels, call(): pl.pallas_call(kernel, out_shape=outs, in_specs=specs, out_specs=jax.tree...  81.6 us
    all_to_all x4, waiting for transfers between devices, spread(): return lax.all_to_all(blocks, AXES, split_axis=0, concat_axis=0, tiled=True)  50.4 us
    all_to_all x4, starting transfers between devices, spread(): return lax.all_to_all(blocks, AXES, split_axis=0, concat_axis=0, tiled=True)  25.1 us
    unnamed x35, local copies, waits for them, and re-layouts  7.87 us
  transfers between devices with their start and end apart: 8, of which 5 were waited for; matrix products, arithmetic and copies ran while one was open for 4% of the time, Pallas kernels for 45%

profile of v6, /device:TPU:1, one launch (start us, length us, event | category | flops | bytes accessed | tf_op | source)
XLA Modules:
  0.0 181.7 jit_solution(4081351723797098730)
XLA Ops:
  0.6 0.9 add_convert_fusion.1
  1.5 1.0 pad_maximum_fusion
  2.5 2.1 %collective-permute-start = (f32[6,8192]{1,0:T(8,128)S(1)}, f32[6,8192]{1,0:T(8,128)S(1)}, u32[]{:S(2)}, u32[]{:S(2)}) collective-permute-start(f32[6,8192]{1,0:T(8,128)S(1)} %pad_maximum_fusion), channel_id=1, source_target_pairs={{0,2},{1,3},{2,0},{3,1},{4,6},{5,7},{6,4},{7,5},{8,10},{9,11},{10,... | collective-permute-start | bytes 589832 | tf_op jit(solution)/shard_map/ppermute | solution.py:473
  4.6 0.5 fusion.6.wa_ref
  5.1 0.0 copy-start.16
  5.1 10.1 %stream_send.1 = bf16[256,64,128]{2,1,0:T(8,128)(2,1)} custom-call(f32[1,64]{1,0:T(1,128)} %fusion.6.wa_ref, bf16[2,64,8192]{2,1,0:T(8,128)(2,1)} %s_ref.1, bf16[256,128]{1,0:T(8,128)(2,1)} %constant.132.clone.g_ref, f32[64,128]{1,0:T(8,128)} %constant.133.clone.tc_ref, f32[64,128]{1,0:T(8,128)} %constant.134.clone.ts_ref, ...), custom_call_target="tpu_custom_call" | custom-call | flops 6000000000 | bytes 1048576 | tf_op jit(solution)/shard_map/stream_send/pallas_call | solution.py:128
  15.2 0.0 collective-permute-done
  15.2 0.0 copy-done.16
  15.3 0.3 fusion.7
  15.6 11.1 %all-to-all-start = ((bf16[128,2,64,128]{3,2,1,0:T(8,128)(2,1)}), bf16[128,2,64,128]{3,2,1,0:T(8,128)(2,1)}, u32[]{:S(2)}, u32[]{:S(2)}) async-start(bf16[128,2,64,128]{3,2,1,0:T(8,128)(2,1)} %bitcast.32), calls=%async_computation | async-start | bytes 8388608 | tf_op jit(solution)/shard_map/all_to_all | solution.py:463
  26.7 0.2 convert_reduce_fusion
  26.9 1.7 select_reduce_fusion
  28.6 32.1 %deposit.1 = (bf16[128,32,128]{2,1,0:T(8,128)(2,1)S(1)}, bf16[128,32,128]{2,1,0:T(8,128)(2,1)S(1)}) custom-call(s32[128,128]{1,0:T(8,128)S(1)} %get-tuple-element.46.idx_ref, s32[1,16384]{1,0:T(1,128)S(1)} %get-tuple-element.43.col_ref, f32[1,16384]{1,0:T(1,128)S(1)} %get-tuple-element.42.fy_ref, f32[1,16384]{1,0:T(1,128)S(1)} %get-tuple-element.41.fx_ref, ...), custom_call_target="tpu_custom_call" | custom-call | flops 20000000000 | bytes 1048576 | tf_op jit(solution)/shard_map/deposit/pallas_call | solution.py:128
  60.7 0.0 copy-start.6
  60.7 0.0 copy-start.7
  60.8 1.2 collective-permute-start.1
  62.0 1.2 reduce-window.6
  63.2 1.2 collective-permute-done.1
  64.4 2.5 %add_convert_fusion = bf16[128,32,128]{2,1,0:T(8,128)(2,1)} fusion(bf16[128,32,128]{2,1,0:T(8,128)(2,1)} %collective-permute-done.1, bf16[128,32,128]{2,1,0:T(8,128)(2,1)S(1)} %get-tuple-element.22), kind=kLoop, calls=%fused_computation.2 | loop fusion | flops 2097152 | bytes 3145728 | tf_op jit(solution)/shard_map/convert_element_type | solution.py:520
  66.9 12.5 %all-to-all-done = bf16[128,2,64,128]{3,2,1,0:T(8,128)(2,1)} async-done(((bf16[128,2,64,128]{3,2,1,0:T(8,128)(2,1)}), bf16[128,2,64,128]{3,2,1,0:T(8,128)(2,1)}, u32[]{:S(2)}, u32[]{:S(2)}) %all-to-all-start) | async-done | bytes 4194336 | tf_op jit(solution)/shard_map/all_to_all | solution.py:463
  79.3 4.8 %all-to-all-start.2 = ((bf16[128,32,128]{2,1,0:T(8,128)(2,1)}), bf16[128,32,128]{2,1,0:T(8,128)(2,1)S(1)}, u32[]{:S(2)}, u32[]{:S(2)}) async-start(bf16[128,32,128]{2,1,0:T(8,128)(2,1)} %add_convert_fusion), calls=%async_computation.2 | async-start | bytes 2097152 | tf_op jit(solution)/shard_map/all_to_all | solution.py:463
  84.1 0.0 copy-done.15
  84.1 0.2 slice_reduce_fusion
  84.4 0.1 compare_bitcast_fusion
  84.4 0.8 select_reduce_fusion.2
  85.3 0.1 copy.35
  85.4 0.1 sub.44.idx_ref
  85.5 0.0 copy-done.6
  85.5 0.0 copy-done.7
  85.5 0.0 copy-start.10
  85.5 0.8 copy-done.10
  86.4 0.8 copy-done.11
  87.2 7.2 %stream_recv.1 = bf16[128,64,128]{2,1,0:T(8,128)(2,1)S(1)} custom-call(s32[1,32]{1,0:T(1,128)S(1)} %sub.44.idx_ref, bf16[256,64,128]{2,1,0:T(8,128)(2,1)} %bitcast.11.x_ref, bf16[256,256]{1,0:T(8,128)(2,1)S(1)} %copy-done.6, f32[128,128]{1,0:T(8,128)S(1)} %copy-done.7, f32[128,128]{1,0:T(8,128)S(1)} %copy-done.10, bf16[128,256]{1,0:T(8,128)(2,1)S(1)} %copy-done.11), custom_call_target="tpu_custom_call" | custom-call | flops 6000000000 | bytes 1048576 | tf_op jit(solution)/shard_map/stream_recv/pallas_call | solution.py:128
  94.4 0.0 copy-start.1
  94.4 1.3 copy-done.1
  95.7 7.8 %all-to-all-done.2.ret_ref = bf16[128,32,128]{2,1,0:T(8,128)(2,1)S(1)} async-done(((bf16[128,32,128]{2,1,0:T(8,128)(2,1)}), bf16[128,32,128]{2,1,0:T(8,128)(2,1)S(1)}, u32[]{:S(2)}, u32[]{:S(2)}) %all-to-all-start.2) | async-done | bytes 1048608 | tf_op jit(solution)/shard_map/all_to_all | solution.py:463
  103.5 4.3 %all-to-all-start.1 = ((bf16[128,64,128]{2,1,0:T(8,128)(2,1)}), bf16[128,64,128]{2,1,0:T(8,128)(2,1)S(1)}, u32[]{:S(2)}, u32[]{:S(2)}) async-start(bf16[128,64,128]{2,1,0:T(8,128)(2,1)} %copy-done.1), calls=%async_computation.1 | async-start | bytes 4194304 | tf_op jit(solution)/shard_map/all_to_all | solution.py:463
  107.8 0.0 copy-done.5
  107.8 0.0 copy-start.2
  107.8 1.2 copy-done.2
  109.1 0.8 copy-done.12
  109.8 0.8 copy-done.13
  110.6 0.8 copy-done.14
  111.3 4.2 %dye_send.1 = bf16[256,32,128]{2,1,0:T(8,128)(2,1)S(1)} custom-call(s32[1,32]{1,0:T(1,128)S(1)} %sub.44.idx_ref, bf16[64,8192]{1,0:T(8,128)(2,1)S(1)} %copy-done.2, bf16[128,32,128]{2,1,0:T(8,128)(2,1)S(1)} %all-to-all-done.2.ret_ref, bf16[128,64]{1,0:T(8,128)(2,1)S(1)} %copy-done.13, f32[64,128]{1,0:T(8,128)S(1)} %copy-done.12, f32[64,128]{1,0:T(8,128)S(1)} %copy-done.14, ...), custom_call_target="tpu_custom_call" | custom-call | flops 4000000000 | bytes 1048576 | tf_op jit(solution)/shard_map/dye_send/pallas_call | solution.py:128
  115.5 0.0 copy-start
  115.5 1.3 copy-done
  116.9 21.6 %all-to-all-done.1.a_ref = bf16[128,64,128]{2,1,0:T(8,128)(2,1)S(1)} async-done(((bf16[128,64,128]{2,1,0:T(8,128)(2,1)}), bf16[128,64,128]{2,1,0:T(8,128)(2,1)S(1)}, u32[]{:S(2)}, u32[]{:S(2)}) %all-to-all-start.1) | async-done | bytes 2097184 | tf_op jit(solution)/shard_map/all_to_all | solution.py:463
  138.5 0.9 collective-permute-start.2
  139.4 4.9 %all-to-all-start.3 = ((bf16[128,2,32,128]{3,2,1,0:T(8,128)(2,1)}), bf16[128,2,32,128]{3,2,1,0:T(8,128)(2,1)}, u32[]{:S(2)}, u32[]{:S(2)}) async-start(bf16[128,2,32,128]{3,2,1,0:T(8,128)(2,1)} %bitcast.31), calls=%async_computation.3 | async-start | bytes 4194304 | tf_op jit(solution)/shard_map/all_to_all | solution.py:463
  144.3 0.0 collective-permute-done.2.b_ref
  144.3 0.0 copy-start.3
  144.3 0.0 copy-start.4
  144.3 0.0 copy-start.8
  144.3 0.0 copy-start.9
  144.4 21.3 %gather.1 = (f32[1,8192]{1,0:T(1,128)S(1)}, f32[1,8192]{1,0:T(1,128)S(1)}) custom-call(s32[128,128]{1,0:T(8,128)S(1)} %get-tuple-element.47.base_ref, bf16[128,64,128]{2,1,0:T(8,128)(2,1)S(1)} %all-to-all-done.1.a_ref, bf16[128,64,128]{2,1,0:T(8,128)(2,1)} %collective-permute-done.2.b_ref, s32[1,16384]{1,0:T(1,128)S(1)} %get-tuple-element.43.col_ref, ...), custom_call_target="tpu_custom_call" | custom-call | flops 10000000000 | bytes 1048576 | tf_op jit(solution)/shard_map/gather/pallas_call | solution.py:128
  165.7 8.6 %all-to-all-done.3 = bf16[128,2,32,128]{3,2,1,0:T(8,128)(2,1)} async-done(((bf16[128,2,32,128]{3,2,1,0:T(8,128)(2,1)}), bf16[128,2,32,128]{3,2,1,0:T(8,128)(2,1)}, u32[]{:S(2)}, u32[]{:S(2)}) %all-to-all-start.3) | async-done | bytes 2097184 | tf_op jit(solution)/shard_map/all_to_all | solution.py:463
  174.2 0.1 collective-permute-start.3
  174.3 0.0 copy-done.3
  174.3 0.0 copy-done.4
  174.3 0.0 copy-done.8
  174.3 0.0 copy-done.9
  174.3 6.7 %dye_recv.1 = f32[2,64,8192]{2,1,0:T(8,128)} custom-call(bf16[256,32,128]{2,1,0:T(8,128)(2,1)} %bitcast.13.x_ref, bf16[256,256]{1,0:T(8,128)(2,1)S(1)} %copy-done.3, f32[128,128]{1,0:T(8,128)S(1)} %copy-done.8, f32[128,128]{1,0:T(8,128)S(1)} %copy-done.9, bf16[256,256]{1,0:T(8,128)(2,1)S(1)} %copy-done.4), custom_call_target="tpu_custom_call" | custom-call | flops 4000000000 | bytes 1048576 | tf_op jit(solution)/shard_map/dye_recv/pallas_call | solution.py:128
  181.0 0.0 collective-permute-done.3
  181.0 0.7 maximum_select_fusion
  (17 shorter events, 0.2 us)
Async XLA Ops:
  2.5 12.7 %collective-permute-start = (f32[6,8192]{1,0:T(8,128)S(1)}, f32[6,8192]{1,0:T(8,128)S(1)}, u32[]{:S(2)}, u32[]{:S(2)}) collective-permute-start(f32[6,8192]{1,0:T(8,128)S(1)} %pad_maximum_fusion), channel_id=1, source_target_pairs={{0,2},{1,3},{2,0},{3,1},{4,6},{5,7},{6,4},{7,5},{8,10},{9,11},{10,... | collective-permute-start | bytes 589832 | tf_op jit(solution)/shard_map/ppermute | solution.py:473
  5.1 10.1 %copy-start.16 = (s32[16,256]{1,0:T(8,128)S(1)}, s32[16,256]{1,0:T(8,128)}, u32[]{:S(2)}) copy-start(s32[16,256]{1,0:T(8,128)} %param.31) | copy-start | bytes 49156
  15.6 63.8 %all-to-all-start = ((bf16[128,2,64,128]{3,2,1,0:T(8,128)(2,1)}), bf16[128,2,64,128]{3,2,1,0:T(8,128)(2,1)}, u32[]{:S(2)}, u32[]{:S(2)}) async-start(bf16[128,2,64,128]{3,2,1,0:T(8,128)(2,1)} %bitcast.32), calls=%async_computation | async-start | bytes 8388608 | tf_op jit(solution)/shard_map/all_to_all | solution.py:463
  60.7 24.8 %copy-start.6 = (bf16[256,256]{1,0:T(8,128)(2,1)S(1)}, bf16[256,256]{1,0:T(8,128)(2,1)}, u32[]{:S(2)}) copy-start(bf16[256,256]{1,0:T(8,128)(2,1)} %constant.136.clone.w1_ref) | copy-start | bytes 393220
  60.7 24.8 %copy-start.7 = (f32[128,128]{1,0:T(8,128)S(1)}, f32[128,128]{1,0:T(8,128)}, u32[]{:S(2)}) copy-start(f32[128,128]{1,0:T(8,128)} %constant.137.clone.tc_ref) | copy-start | bytes 196612
  60.8 3.6 %collective-permute-start.1 = (bf16[128,32,128]{2,1,0:T(8,128)(2,1)S(1)}, bf16[128,32,128]{2,1,0:T(8,128)(2,1)}, u32[]{:S(2)}, u32[]{:S(2)}) collective-permute-start(bf16[128,32,128]{2,1,0:T(8,128)(2,1)S(1)} %get-tuple-element.23), channel_id=1, source_target_pairs={{0,1},{1,0},{2,3},{3,2},{4,5},{5,4},{6,7},{7,6},{8,9},{9,8},{10,11... | collective-permute-start | bytes 3145736 | tf_op jit(solution)/shard_map/ppermute | solution.py:468
  64.4 19.8 %copy-start.15 = (s32[16,2,128]{2,0,1:T(8,128)S(1)}, s32[16,2,128]{2,0,1:T(8,128)}, u32[]{:S(2)}) copy-start(s32[16,2,128]{2,0,1:T(8,128)} %reduce-window.6) | copy-start | bytes 49156
  79.3 24.1 %all-to-all-start.2 = ((bf16[128,32,128]{2,1,0:T(8,128)(2,1)}), bf16[128,32,128]{2,1,0:T(8,128)(2,1)S(1)}, u32[]{:S(2)}, u32[]{:S(2)}) async-start(bf16[128,32,128]{2,1,0:T(8,128)(2,1)} %add_convert_fusion), calls=%async_computation.2 | async-start | bytes 2097152 | tf_op jit(solution)/shard_map/all_to_all | solution.py:463
  85.5 0.8 copy-start.10
  86.4 0.8 copy-start.11
  94.4 1.3 copy-start.1
  95.7 12.1 %copy-start.5 = (bf16[256,256]{1,0:T(8,128)(2,1)S(1)}, bf16[256,256]{1,0:T(8,128)(2,1)}, u32[]{:S(2)}) copy-start(bf16[256,256]{1,0:T(8,128)(2,1)} %constant.142.clone.w2_ref) | copy-start | bytes 393220
  103.5 35.0 %all-to-all-start.1 = ((bf16[128,64,128]{2,1,0:T(8,128)(2,1)}), bf16[128,64,128]{2,1,0:T(8,128)(2,1)S(1)}, u32[]{:S(2)}, u32[]{:S(2)}) async-start(bf16[128,64,128]{2,1,0:T(8,128)(2,1)} %copy-done.1), calls=%async_computation.1 | async-start | bytes 4194304 | tf_op jit(solution)/shard_map/all_to_all | solution.py:463
  107.8 1.2 copy-start.2
  109.1 0.8 copy-start.12
  109.8 0.8 copy-start.13
  110.6 0.8 copy-start.14
  115.5 1.3 copy-start
  138.5 5.8 %collective-permute-start.2 = (bf16[128,64,128]{2,1,0:T(8,128)(2,1)S(1)}, bf16[128,64,128]{2,1,0:T(8,128)(2,1)}, u32[]{:S(2)}, u32[]{:S(2)}) collective-permute-start(bf16[128,64,128]{2,1,0:T(8,128)(2,1)S(1)} %all-to-all-done.1.a_ref), channel_id=1, source_target_pairs={{0,1},{1,0},{2,3},{3,2},{4,5},{5,4},{6,7},{7,6},{8,9},{9,8},{10,11... | collective-permute-start | bytes 6291464 | tf_op jit(solution)/shard_map/ppermute | solution.py:468
  139.4 34.8 %all-to-all-start.3 = ((bf16[128,2,32,128]{3,2,1,0:T(8,128)(2,1)}), bf16[128,2,32,128]{3,2,1,0:T(8,128)(2,1)}, u32[]{:S(2)}, u32[]{:S(2)}) async-start(bf16[128,2,32,128]{3,2,1,0:T(8,128)(2,1)} %bitcast.31), calls=%async_computation.3 | async-start | bytes 4194304 | tf_op jit(solution)/shard_map/all_to_all | solution.py:463
  144.3 30.0 %copy-start.3 = (bf16[256,256]{1,0:T(8,128)(2,1)S(1)}, bf16[256,256]{1,0:T(8,128)(2,1)}, u32[]{:S(2)}) copy-start(bf16[256,256]{1,0:T(8,128)(2,1)} %constant.143.clone.w1_ref) | copy-start | bytes 393220
  144.3 30.0 %copy-start.4 = (bf16[256,256]{1,0:T(8,128)(2,1)S(1)}, bf16[256,256]{1,0:T(8,128)(2,1)}, u32[]{:S(2)}) copy-start(bf16[256,256]{1,0:T(8,128)(2,1)} %constant.145.clone.v_ref) | copy-start | bytes 393220
  144.3 30.0 %copy-start.8 = (f32[128,128]{1,0:T(8,128)S(1)}, f32[128,128]{1,0:T(8,128)}, u32[]{:S(2)}) copy-start(f32[128,128]{1,0:T(8,128)} %constant.137.clone.tc_ref) | copy-start | bytes 196612
  144.3 29.9 %copy-start.9 = (f32[128,128]{1,0:T(8,128)S(1)}, f32[128,128]{1,0:T(8,128)}, u32[]{:S(2)}) copy-start(f32[128,128]{1,0:T(8,128)} %constant.144.clone.ts_ref) | copy-start | bytes 196612
  174.2 6.8 %collective-permute-start.3 = (f32[1,8192]{1,0:T(1,128)S(1)}, f32[1,8192]{1,0:T(1,128)S(1)}, u32[]{:S(2)}, u32[]{:S(2)}) collective-permute-start(f32[1,8192]{1,0:T(1,128)S(1)} %get-tuple-element.32), channel_id=1, source_target_pairs={{0,2},{1,3},{2,0},{3,1},{4,6},{5,7},{6,4},{7,5},{8,10},{9,11},{10,... | collective-permute-start | bytes 98312 | tf_op jit(solution)/shard_map/ppermute | solution.py:473

commit v7 on v6

--- a/solution.py
+++ b/solution.py
@@ -65,7 +65,23 @@
     return bf(w1), np.float32(tc), np.float32(ts), bf(v)
 
 
-def stream_send_kernel(wa_ref, s_ref, g_ref, tc_ref, ts_ref, w2_ref, o_ref, xs, tre, tim, of):
+def stream_send_kernel(
+    wa_ref, slot_ref, row_ref, col_ref, frac_ref, amount_ref, g_ref, tc_ref, ts_ref, w2_ref, s_hbm,
+    floats_ref, o_hbm, s_ref, xs, tre, tim, of, o_ref, in_sem, out_sem,
+):
+    reads = []
+    for k in range(4):
+        lanes = pl.ds(2048 * k, 2048)
+        reads.append(
+            pltpu.make_async_copy(s_hbm.at[:, :, lanes], s_ref.at[:, :, lanes], in_sem.at[k])
+        )
+        reads[k].start()
+    floats_ref[0:1, :] = slot_ref[...].astype(F32)
+    floats_ref[1:2, :] = row_ref[...].astype(F32)
+    floats_ref[2:3, :] = col_ref[...].astype(F32)
+    floats_ref[3:5, :] = frac_ref[...]
+    floats_ref[5:6, :] = amount_ref[...]
+
     def load(p, carry):
         at = pl.multiple_of(p * 128, 128)
         for c in range(2):
@@ -73,7 +89,9 @@
             xs[pl.ds(row, 64), :] = s_ref[c, :, pl.ds(at, 128)].astype(F32)
         return carry
 
-    lax.fori_loop(0, 64, load, 0, unroll=4)
+    for k in range(4):
+        reads[k].wait()
+        lax.fori_loop(16 * k, 16 * k + 16, load, 0, unroll=4)
     q = lax.broadcasted_iota(jnp.int32, (64, 128), 1).astype(F32)
 
     def rows(n, carry):
@@ -111,25 +129,33 @@
             of[pl.ds(2 * n + h, 256, stride=PAD), :] = out[:, h * 128 : h * 128 + 128]
         return carry
 
-    lax.fori_loop(0, 32, cols, 0, unroll=8)
-
-    def store(i, carry):
-        o_ref[i] = of[pl.ds(pl.multiple_of(i * PAD, 8), 64), :].astype(BF)
-        return carry
-
-    lax.fori_loop(0, 256, store, 0, unroll=8)
+    writes = []
+    for k in range(4):
+        lax.fori_loop(8 * k, 8 * k + 8, cols, 0, unroll=8)
+
+        def store(i, carry, k=k):
+            o_ref[i, 16 * k : 16 * k + 16] = of[pl.ds(pl.multiple_of(i * PAD + 16 * k, 8), 16), :].astype(BF)
+            return carry
+
+        lax.fori_loop(0, 256, store, 0, unroll=8)
+        levels = pl.ds(16 * k, 16)
+        writes.append(pltpu.make_async_copy(o_ref.at[:, levels, :], o_hbm.at[:, levels, :], out_sem.at[k]))
+        writes[k].start()
+    for write in writes:
+        write.wait()
 
 
 VM = pl.BlockSpec(memory_space=pltpu.VMEM)
 SM = pl.BlockSpec(memory_space=pltpu.SMEM)
-
-
-def call(kernel, outs, specs, scratch, cost, mib, name, *args):
+HB = pl.BlockSpec(memory_space=pl.ANY)
+
+
+def call(kernel, outs, specs, scratch, cost, mib, name, *args, out_specs=None):
     return pl.pallas_call(
         kernel,
         out_shape=outs,
         in_specs=specs,
-        out_specs=jax.tree.map(lambda _: VM, outs),
+        out_specs=out_specs or jax.tree.map(lambda _: VM, outs),
         scratch_shapes=scratch,
         compiler_params=pltpu.CompilerParams(vmem_limit_bytes=mib << 20),
         cost_estimate=pl.CostEstimate(flops=cost, bytes_accessed=1 << 20, transcendentals=0),
@@ -137,15 +163,17 @@
     )(*args)
 
 
-def stream_send(stream, wa):
+def stream_send(stream, wa, floats):
     return call(
         stream_send_kernel,
-        jax.ShapeDtypeStruct((256, 64, 128), BF),
-        [SM] + [VM] * 5,
-        [pltpu.VMEM((128 * PAD, 128), F32)] + [pltpu.VMEM((64 * PAD2, 128), F32)] * 2
-        + [pltpu.VMEM((256 * PAD, 128), F32)],
+        [jax.ShapeDtypeStruct((6, 8192), F32), jax.ShapeDtypeStruct((256, 64, 128), BF)],
+        [SM] + [VM] * 9 + [HB],
+        [pltpu.VMEM((2, 64, 8192), BF), pltpu.VMEM((128 * PAD, 128), F32)]
+        + [pltpu.VMEM((64 * PAD2, 128), F32)] * 2
+        + [pltpu.VMEM((256 * PAD, 128), F32), pltpu.VMEM((256, 64, 128), BF)]
+        + [pltpu.SemaphoreType.DMA((4,))] * 2,
         int(6e9), 60, "stream_send",
-        wa, stream, *send_tables(1.0, True),
+        wa, *floats, *send_tables(1.0, True), stream, out_specs=[VM, HB],
     )
 
 
@@ -271,7 +299,7 @@
     )
 
 
-def dye_recv_kernel(x_ref, w1_ref, tc_ref, ts_ref, v_ref, o_ref, xf, of):
+def dye_recv_kernel(x_ref, w1_ref, tc_ref, ts_ref, v_ref, o_hbm, xf, of, o_ref, out_sem):
     def load(i, carry):
         xf[pl.ds(pl.multiple_of(i * PAD3, 8), 32), :] = x_ref[i].astype(F32)
         return carry
@@ -301,18 +329,18 @@
                     ]
         return carry
 
-    lax.fori_loop(0, 16, step, 0, unroll=8)
-
-    def store(n, carry):
-        c = n // 8
-        t8 = n % 8
-        base = pl.multiple_of(n * 512, 512)
-        at = pl.ds(pl.multiple_of(t8 * 8, 8), 8)
-        for j in range(64):
-            o_ref[c, at, j * 128 : j * 128 + 128] = of[pl.ds(base + j * 8, 8), :]
-        return carry
-
-    lax.fori_loop(0, 16, store, 0)
+    writes = []
+    for k in range(8):
+        for n in range(2 * k, 2 * k + 2):
+            step(n, 0)
+        at = pl.ds(8 * k, 8)
+        for c in range(2):
+            for j in range(64):
+                o_ref[c, at, j * 128 : j * 128 + 128] = of[pl.ds(c * 4096 + k * 512 + j * 8, 8), :]
+        writes.append(pltpu.make_async_copy(o_ref.at[:, at, :], o_hbm.at[:, at, :], out_sem.at[k]))
+        writes[k].start()
+    for write in writes:
+        write.wait()
 
 
 def dye_recv(x):
@@ -320,9 +348,10 @@
         dye_recv_kernel,
         jax.ShapeDtypeStruct((2, 64, 8192), F32),
         [VM] * 5,
-        [pltpu.VMEM((256 * PAD3, 128), F32), pltpu.VMEM((8192, 128), F32)],
+        [pltpu.VMEM((256 * PAD3, 128), F32), pltpu.VMEM((8192, 128), F32)]
+        + [pltpu.VMEM((2, 64, 8192), F32), pltpu.SemaphoreType.DMA((8,))],
         int(4e9), 20, "dye_recv",
-        x, *recv_tables(-1.0, False),
+        x, *recv_tables(-1.0, False), out_specs=HB,
     )
 
 CAPO = 2
@@ -481,14 +510,14 @@
     wave = device * 64 + jnp.arange(64)
     wave = jnp.where(wave >= 4096, wave - 8192, wave).astype(F32)[None]
 
-    own_floats = jnp.concatenate(
-        [jnp.stack([float_slot, float_row, float_col]).astype(F32), float_frac, float_dye[None]]
+    line = lambda x: x.reshape(1, 8192)
+    own_floats, spec = stream_send(
+        stream_hat,
+        wave,
+        (line(float_slot), line(float_row), line(float_col), float_frac, line(float_dye)),
     )
     their_floats = swap_chips(own_floats)
-    spec = stream_send(stream_hat, wave)
-    spec, own_floats, their_floats, tile_lists = lax.optimization_barrier(
-        (spec, own_floats, their_floats, tile_lists)
-    )
+    spec, own_floats, tile_lists = lax.optimization_barrier((spec, own_floats, tile_lists))
     spec = spread(spec.reshape(128, 2, 64, 128)).reshape(256, 64, 128)
     floats = jnp.concatenate([own_floats, their_floats], axis=1)
     slot = floats[0].astype(jnp.int32).reshape(128, 128)

time: 183 us -> 179 us (0.978)
  other arithmetic: 9.97 us -> 6.83 us
    unnamed x35 -> x39, local copies, waits for them, and re-layouts: 7.87 us -> 8.73 us
  transfers between devices with their start and end apart: 8 -> 8, of which waited for: 5 -> 4; matrix products, arithmetic and copies ran while one was open for 4% -> 4% of each run, Pallas kernels for 45% -> 39%
where the time goes in v7:
time: 179 us; the launch traced here: 178 us
  Pallas kernels  80.4 us (45%)
  waiting for transfers between devices  51.1 us (29%)
  starting transfers between devices  29.4 us (16%)
  local copies, waits for them, and re-layouts  9.72 us (5%)
  other arithmetic  6.83 us (4%)
    pallas_call x6, Pallas kernels, call(): pl.pallas_call(kernel, out_shape=outs, in_specs=specs, out_specs=out_spec...  80.4 us
    all_to_all x4, waiting for transfers between devices, spread(): return lax.all_to_all(blocks, AXES, split_axis=0, concat_axis=0, tiled=True)  51.1 us
    all_to_all x4, starting transfers between devices, spread(): return lax.all_to_all(blocks, AXES, split_axis=0, concat_axis=0, tiled=True)  24.9 us
    unnamed x39, local copies, waits for them, and re-layouts  8.73 us
  transfers between devices with their start and end apart: 8, of which 4 were waited for; matrix products, arithmetic and copies ran while one was open for 4% of the time, Pallas kernels for 39%

profile of v7, /device:TPU:1, one launch (start us, length us, event | category | flops | bytes accessed | tf_op | source)
XLA Modules:
  0.0 178.5 jit_solution(9324836817764874697)
XLA Ops:
  0.6 0.5 fusion.6.wa_ref
  1.2 10.8 %stream_send.1 = (f32[6,8192]{1,0:T(8,128)}, bf16[256,64,128]{2,1,0:T(8,128)(2,1)}) custom-call(f32[1,64]{1,0:T(1,128)} %fusion.6.wa_ref, s32[1,8192]{1,0:T(1,128)} %bitcast.41, s32[1,8192]{1,0:T(1,128)} %bitcast.42, s32[1,8192]{1,0:T(1,128)} %bitcast.43, f32[2,8192]{1,0:T(2,128)} %frac_ref.1, f32[1,8192]{1,0:T(1,128)} %bitcast.44, ...), custom_call_target="tpu_custom_call" | custom-call | flops 6000000000 | bytes 1048576 | tf_op jit(solution)/shard_map/stream_send/pallas_call | solution.py:154
  11.9 2.1 %collective-permute-start = (f32[6,8192]{1,0:T(8,128)}, f32[6,8192]{1,0:T(8,128)S(1)}, u32[]{:S(2)}, u32[]{:S(2)}) collective-permute-start(f32[6,8192]{1,0:T(8,128)} %get-tuple-element.21), channel_id=1, source_target_pairs={{0,2},{1,3},{2,0},{3,1},{4,6},{5,7},{6,4},{7,5},{8,10},{9,11},{10,... | collective-permute-start | bytes 589832 | tf_op jit(solution)/shard_map/ppermute | solution.py:502
  14.1 11.1 %all-to-all-start = ((bf16[128,2,64,128]{3,2,1,0:T(8,128)(2,1)}), bf16[128,2,64,128]{3,2,1,0:T(8,128)(2,1)}, u32[]{:S(2)}, u32[]{:S(2)}) async-start(bf16[128,2,64,128]{3,2,1,0:T(8,128)(2,1)} %bitcast.32), calls=%async_computation | async-start | bytes 8388608 | tf_op jit(solution)/shard_map/all_to_all | solution.py:492
  25.2 0.0 copy-done.16
  25.3 0.0 copy-done.15
  25.3 0.2 convert_reduce_fusion
  25.5 0.0 collective-permute-done
  25.6 0.3 fusion.7
  25.8 1.7 select_reduce_fusion
  27.6 32.1 %deposit.1 = (bf16[128,32,128]{2,1,0:T(8,128)(2,1)S(1)}, bf16[128,32,128]{2,1,0:T(8,128)(2,1)S(1)}) custom-call(s32[128,128]{1,0:T(8,128)S(1)} %get-tuple-element.48.idx_ref, s32[1,16384]{1,0:T(1,128)S(1)} %get-tuple-element.45.col_ref, f32[1,16384]{1,0:T(1,128)S(1)} %get-tuple-element.44.fy_ref, f32[1,16384]{1,0:T(1,128)S(1)} %get-tuple-element.43.fx_ref, ...), custom_call_target="tpu_custom_call" | custom-call | flops 20000000000 | bytes 1048576 | tf_op jit(solution)/shard_map/deposit/pallas_call | solution.py:154
  59.6 0.0 copy-start.6
  59.7 1.3 collective-permute-start.1
  61.0 0.6 convert_bitcast_fusion
  61.6 0.6 copy.42
  62.2 1.3 reduce-window.6
  63.4 0.0 collective-permute-done.1
  63.5 1.2 add_convert_fusion
  64.7 13.1 %all-to-all-done = bf16[128,2,64,128]{3,2,1,0:T(8,128)(2,1)} async-done(((bf16[128,2,64,128]{3,2,1,0:T(8,128)(2,1)}), bf16[128,2,64,128]{3,2,1,0:T(8,128)(2,1)}, u32[]{:S(2)}, u32[]{:S(2)}) %all-to-all-start) | async-done | bytes 4194336 | tf_op jit(solution)/shard_map/all_to_all | solution.py:492
  77.8 4.8 %all-to-all-start.2 = ((bf16[128,32,128]{2,1,0:T(8,128)(2,1)}), bf16[128,32,128]{2,1,0:T(8,128)(2,1)S(1)}, u32[]{:S(2)}, u32[]{:S(2)}) async-start(bf16[128,32,128]{2,1,0:T(8,128)(2,1)} %add_convert_fusion), calls=%async_computation.2 | async-start | bytes 2097152 | tf_op jit(solution)/shard_map/all_to_all | solution.py:492
  82.6 0.2 slice_reduce_fusion
  82.8 0.1 compare_bitcast_fusion
  82.9 0.0 copy-done.17
  82.9 0.0 copy-done.18
  82.9 0.1 select_reduce_fusion.2
  83.1 0.1 copy.35
  83.2 0.1 sub.44.idx_ref
  83.3 0.0 copy-done.6
  83.3 0.0 copy-start.7
  83.3 0.8 copy-done.7
  84.1 0.8 copy-done.10
  85.0 0.8 copy-done.11
  85.8 7.1 %stream_recv.1 = bf16[128,64,128]{2,1,0:T(8,128)(2,1)S(1)} custom-call(s32[1,32]{1,0:T(1,128)S(1)} %sub.44.idx_ref, bf16[256,64,128]{2,1,0:T(8,128)(2,1)} %bitcast.11.x_ref, bf16[256,256]{1,0:T(8,128)(2,1)S(1)} %copy-done.6, f32[128,128]{1,0:T(8,128)S(1)} %copy-done.7, f32[128,128]{1,0:T(8,128)S(1)} %copy-done.11, bf16[128,256]{1,0:T(8,128)(2,1)S(1)} %copy-done.10), custom_call_target="tpu_custom_call" | custom-call | flops 6000000000 | bytes 1048576 | tf_op jit(solution)/shard_map/stream_recv/pallas_call | solution.py:154
  92.9 0.0 copy-start.1
  93.0 1.3 copy-done.1
  94.3 7.7 %all-to-all-done.2.ret_ref = bf16[128,32,128]{2,1,0:T(8,128)(2,1)S(1)} async-done(((bf16[128,32,128]{2,1,0:T(8,128)(2,1)}), bf16[128,32,128]{2,1,0:T(8,128)(2,1)S(1)}, u32[]{:S(2)}, u32[]{:S(2)}) %all-to-all-start.2) | async-done | bytes 1048608 | tf_op jit(solution)/shard_map/all_to_all | solution.py:492
  102.0 4.3 %all-to-all-start.1 = ((bf16[128,64,128]{2,1,0:T(8,128)(2,1)}), bf16[128,64,128]{2,1,0:T(8,128)(2,1)S(1)}, u32[]{:S(2)}, u32[]{:S(2)}) async-start(bf16[128,64,128]{2,1,0:T(8,128)(2,1)} %copy-done.1), calls=%async_computation.1 | async-start | bytes 4194304 | tf_op jit(solution)/shard_map/all_to_all | solution.py:492
  106.3 0.0 copy-done.5
  106.3 0.0 copy-start.2
  106.3 1.2 copy-done.2
  107.5 0.8 copy-done.12
  108.3 0.8 copy-done.13
  109.1 0.8 copy-done.14
  109.8 4.2 %dye_send.1 = bf16[256,32,128]{2,1,0:T(8,128)(2,1)S(1)} custom-call(s32[1,32]{1,0:T(1,128)S(1)} %sub.44.idx_ref, bf16[64,8192]{1,0:T(8,128)(2,1)S(1)} %copy-done.2, bf16[128,32,128]{2,1,0:T(8,128)(2,1)S(1)} %all-to-all-done.2.ret_ref, bf16[128,64]{1,0:T(8,128)(2,1)S(1)} %copy-done.14, f32[64,128]{1,0:T(8,128)S(1)} %copy-done.12, f32[64,128]{1,0:T(8,128)S(1)} %copy-done.13, ...), custom_call_target="tpu_custom_call" | custom-call | flops 4000000000 | bytes 1048576 | tf_op jit(solution)/shard_map/dye_send/pallas_call | solution.py:154
  114.0 0.0 copy-start
  114.0 1.3 copy-done
  115.4 21.6 %all-to-all-done.1.a_ref = bf16[128,64,128]{2,1,0:T(8,128)(2,1)S(1)} async-done(((bf16[128,64,128]{2,1,0:T(8,128)(2,1)}), bf16[128,64,128]{2,1,0:T(8,128)(2,1)S(1)}, u32[]{:S(2)}, u32[]{:S(2)}) %all-to-all-start.1) | async-done | bytes 2097184 | tf_op jit(solution)/shard_map/all_to_all | solution.py:492
  136.9 0.9 collective-permute-start.2
  137.9 4.7 %all-to-all-start.3 = ((bf16[128,2,32,128]{3,2,1,0:T(8,128)(2,1)}), bf16[128,2,32,128]{3,2,1,0:T(8,128)(2,1)}, u32[]{:S(2)}, u32[]{:S(2)}) async-start(bf16[128,2,32,128]{3,2,1,0:T(8,128)(2,1)} %bitcast.31), calls=%async_computation.3 | async-start | bytes 4194304 | tf_op jit(solution)/shard_map/all_to_all | solution.py:492
  142.6 0.0 collective-permute-done.2.b_ref
  142.6 0.0 copy-start.3
  142.6 0.0 copy-start.4
  142.6 0.0 copy-start.8
  142.6 0.0 copy-start.9
  142.7 21.3 %gather.1 = (f32[1,8192]{1,0:T(1,128)S(1)}, f32[1,8192]{1,0:T(1,128)S(1)}) custom-call(s32[128,128]{1,0:T(8,128)S(1)} %get-tuple-element.49.base_ref, bf16[128,64,128]{2,1,0:T(8,128)(2,1)S(1)} %all-to-all-done.1.a_ref, bf16[128,64,128]{2,1,0:T(8,128)(2,1)} %collective-permute-done.2.b_ref, s32[1,16384]{1,0:T(1,128)S(1)} %get-tuple-element.45.col_ref, ...), custom_call_target="tpu_custom_call" | custom-call | flops 10000000000 | bytes 1048576 | tf_op jit(solution)/shard_map/gather/pallas_call | solution.py:154
  164.0 8.7 %all-to-all-done.3 = bf16[128,2,32,128]{3,2,1,0:T(8,128)(2,1)} async-done(((bf16[128,2,32,128]{3,2,1,0:T(8,128)(2,1)}), bf16[128,2,32,128]{3,2,1,0:T(8,128)(2,1)}, u32[]{:S(2)}, u32[]{:S(2)}) %all-to-all-start.3) | async-done | bytes 2097184 | tf_op jit(solution)/shard_map/all_to_all | solution.py:492
  172.7 0.1 collective-permute-start.3
  172.8 0.0 copy-done.3
  172.8 0.0 copy-done.4
  172.8 0.0 copy-done.8
  172.8 0.0 copy-done.9
  172.8 4.9 %dye_recv.1 = f32[2,64,8192]{2,1,0:T(8,128)} custom-call(bf16[256,32,128]{2,1,0:T(8,128)(2,1)} %bitcast.13.x_ref, bf16[256,256]{1,0:T(8,128)(2,1)S(1)} %copy-done.4, f32[128,128]{1,0:T(8,128)S(1)} %copy-done.8, f32[128,128]{1,0:T(8,128)S(1)} %copy-done.9, bf16[256,256]{1,0:T(8,128)(2,1)S(1)} %copy-done.3), custom_call_target="tpu_custom_call" | custom-call | flops 4000000000 | bytes 1048576 | tf_op jit(solution)/shard_map/dye_recv/pallas_call | solution.py:154
  177.7 0.0 collective-permute-done.3
  177.7 0.7 maximum_select_fusion
  (19 shorter events, 0.2 us)
Async XLA Ops:
  11.9 13.6 %collective-permute-start = (f32[6,8192]{1,0:T(8,128)}, f32[6,8192]{1,0:T(8,128)S(1)}, u32[]{:S(2)}, u32[]{:S(2)}) collective-permute-start(f32[6,8192]{1,0:T(8,128)} %get-tuple-element.21), channel_id=1, source_target_pairs={{0,2},{1,3},{2,0},{3,1},{4,6},{5,7},{6,4},{7,5},{8,10},{9,11},{10,... | collective-permute-start | bytes 589832 | tf_op jit(solution)/shard_map/ppermute | solution.py:502
  14.1 11.2 %copy-start.16 = (s32[16,256]{1,0:T(8,128)S(1)}, s32[16,256]{1,0:T(8,128)}, u32[]{:S(2)}) copy-start(s32[16,256]{1,0:T(8,128)} %param.31) | copy-start | bytes 49156
  14.1 11.2 %copy-start.15 = (f32[6,8192]{1,0:T(8,128)S(1)}, f32[6,8192]{1,0:T(8,128)}, u32[]{:S(2)}) copy-start(f32[6,8192]{1,0:T(8,128)} %get-tuple-element.21) | copy-start | bytes 589828
  14.1 63.8 %all-to-all-start = ((bf16[128,2,64,128]{3,2,1,0:T(8,128)(2,1)}), bf16[128,2,64,128]{3,2,1,0:T(8,128)(2,1)}, u32[]{:S(2)}, u32[]{:S(2)}) async-start(bf16[128,2,64,128]{3,2,1,0:T(8,128)(2,1)} %bitcast.32), calls=%async_computation | async-start | bytes 8388608 | tf_op jit(solution)/shard_map/all_to_all | solution.py:492
  59.6 23.6 %copy-start.6 = (bf16[256,256]{1,0:T(8,128)(2,1)S(1)}, bf16[256,256]{1,0:T(8,128)(2,1)}, u32[]{:S(2)}) copy-start(bf16[256,256]{1,0:T(8,128)(2,1)} %constant.136.clone.w1_ref) | copy-start | bytes 393220
  59.7 3.8 %collective-permute-start.1 = (bf16[128,32,128]{2,1,0:T(8,128)(2,1)S(1)}, bf16[128,32,128]{2,1,0:T(8,128)(2,1)S(1)}, u32[]{:S(2)}, u32[]{:S(2)}) collective-permute-start(bf16[128,32,128]{2,1,0:T(8,128)(2,1)S(1)} %get-tuple-element.25), channel_id=1, source_target_pairs={{0,1},{1,0},{2,3},{3,2},{4,5},{5,4},{6,7},{7,6},{8,9},{9,8},{10,11... | collective-permute-start | bytes 3145736 | tf_op jit(solution)/shard_map/ppermute | solution.py:497
  63.4 19.5 %copy-start.17 = (s32[16,256]{1,0:T(8,128)S(1)}, s32[16,256]{1,0:T(8,128)}, u32[]{:S(2)}) copy-start(s32[16,256]{1,0:T(8,128)} %param.31) | copy-start | bytes 49156
  63.5 19.5 %copy-start.18 = (pred[16,256]{1,0:T(8,128)(4,1)S(1)}, pred[16,256]{1,0:T(8,128)(4,1)}, u32[]{:S(2)}) copy-start(pred[16,256]{1,0:T(8,128)(4,1)} %get-tuple-element.39) | copy-start | bytes 12292
  77.8 24.1 %all-to-all-start.2 = ((bf16[128,32,128]{2,1,0:T(8,128)(2,1)}), bf16[128,32,128]{2,1,0:T(8,128)(2,1)S(1)}, u32[]{:S(2)}, u32[]{:S(2)}) async-start(bf16[128,32,128]{2,1,0:T(8,128)(2,1)} %add_convert_fusion), calls=%async_computation.2 | async-start | bytes 2097152 | tf_op jit(solution)/shard_map/all_to_all | solution.py:492
  83.3 0.8 copy-start.7
  84.1 0.8 copy-start.10
  85.0 0.8 copy-start.11
  92.9 1.3 copy-start.1
  94.3 12.0 %copy-start.5 = (bf16[256,256]{1,0:T(8,128)(2,1)S(1)}, bf16[256,256]{1,0:T(8,128)(2,1)}, u32[]{:S(2)}) copy-start(bf16[256,256]{1,0:T(8,128)(2,1)} %constant.142.clone.w2_ref) | copy-start | bytes 393220
  102.0 35.0 %all-to-all-start.1 = ((bf16[128,64,128]{2,1,0:T(8,128)(2,1)}), bf16[128,64,128]{2,1,0:T(8,128)(2,1)S(1)}, u32[]{:S(2)}, u32[]{:S(2)}) async-start(bf16[128,64,128]{2,1,0:T(8,128)(2,1)} %copy-done.1), calls=%async_computation.1 | async-start | bytes 4194304 | tf_op jit(solution)/shard_map/all_to_all | solution.py:492
  106.3 1.2 copy-start.2
  107.5 0.8 copy-start.12
  108.3 0.8 copy-start.13
  109.1 0.8 copy-start.14
  114.0 1.3 copy-start
  136.9 5.7 %collective-permute-start.2 = (bf16[128,64,128]{2,1,0:T(8,128)(2,1)S(1)}, bf16[128,64,128]{2,1,0:T(8,128)(2,1)}, u32[]{:S(2)}, u32[]{:S(2)}) collective-permute-start(bf16[128,64,128]{2,1,0:T(8,128)(2,1)S(1)} %all-to-all-done.1.a_ref), channel_id=1, source_target_pairs={{0,1},{1,0},{2,3},{3,2},{4,5},{5,4},{6,7},{7,6},{8,9},{9,8},{10,11... | collective-permute-start | bytes 6291464 | tf_op jit(solution)/shard_map/ppermute | solution.py:497
  137.9 34.8 %all-to-all-start.3 = ((bf16[128,2,32,128]{3,2,1,0:T(8,128)(2,1)}), bf16[128,2,32,128]{3,2,1,0:T(8,128)(2,1)}, u32[]{:S(2)}, u32[]{:S(2)}) async-start(bf16[128,2,32,128]{3,2,1,0:T(8,128)(2,1)} %bitcast.31), calls=%async_computation.3 | async-start | bytes 4194304 | tf_op jit(solution)/shard_map/all_to_all | solution.py:492
  142.6 30.2 %copy-start.3 = (bf16[256,256]{1,0:T(8,128)(2,1)S(1)}, bf16[256,256]{1,0:T(8,128)(2,1)}, u32[]{:S(2)}) copy-start(bf16[256,256]{1,0:T(8,128)(2,1)} %constant.145.clone.v_ref) | copy-start | bytes 393220
  142.6 30.1 %copy-start.4 = (bf16[256,256]{1,0:T(8,128)(2,1)S(1)}, bf16[256,256]{1,0:T(8,128)(2,1)}, u32[]{:S(2)}) copy-start(bf16[256,256]{1,0:T(8,128)(2,1)} %constant.143.clone.w1_ref) | copy-start | bytes 393220
  142.6 30.1 %copy-start.8 = (f32[128,128]{1,0:T(8,128)S(1)}, f32[128,128]{1,0:T(8,128)}, u32[]{:S(2)}) copy-start(f32[128,128]{1,0:T(8,128)} %constant.137.clone.tc_ref) | copy-start | bytes 196612
  142.6 30.1 %copy-start.9 = (f32[128,128]{1,0:T(8,128)S(1)}, f32[128,128]{1,0:T(8,128)}, u32[]{:S(2)}) copy-start(f32[128,128]{1,0:T(8,128)} %constant.144.clone.ts_ref) | copy-start | bytes 196612
  172.7 5.0 %collective-permute-start.3 = (f32[1,8192]{1,0:T(1,128)S(1)}, f32[1,8192]{1,0:T(1,128)S(1)}, u32[]{:S(2)}, u32[]{:S(2)}) collective-permute-start(f32[1,8192]{1,0:T(1,128)S(1)} %get-tuple-element.34), channel_id=1, source_target_pairs={{0,2},{1,3},{2,0},{3,1},{4,6},{5,7},{6,4},{7,5},{8,10},{9,11},{10,... | collective-permute-start | bytes 98312 | tf_op jit(solution)/shard_map/ppermute | solution.py:502

commit v8 on v7

--- a/solution.py
+++ b/solution.py
@@ -66,7 +66,7 @@
 
 
 def stream_send_kernel(
-    wa_ref, slot_ref, row_ref, col_ref, frac_ref, amount_ref, g_ref, tc_ref, ts_ref, w2_ref, s_hbm,
+    slot_ref, row_ref, col_ref, frac_ref, amount_ref, g_ref, tc_ref, ts_ref, w2_ref, s_hbm,
     floats_ref, o_hbm, s_ref, xs, tre, tim, of, o_ref, in_sem, out_sem,
 ):
     reads = []
@@ -92,6 +92,7 @@
     for k in range(4):
         reads[k].wait()
         lax.fori_loop(16 * k, 16 * k + 16, load, 0, unroll=4)
+    first = (lax.axis_index("wide") * 8 + lax.axis_index("narrow")) * 64
     q = lax.broadcasted_iota(jnp.int32, (64, 128), 1).astype(F32)
 
     def rows(n, carry):
@@ -105,7 +106,7 @@
             are, aim, bre, bim = z[:64], z[64:128], z[128:192], z[192:]
             ure = bre + q * are
             uim = bim + q * aim
-            wa = wa_ref[0, r]
+            wa = jnp.where(first + r >= 4096, first + r - 8192, first + r).astype(F32)
             base = pl.multiple_of(r * PAD2, 8)
             vre = are * tc - aim * ts
             vim = are * ts + aim * tc
@@ -163,17 +164,17 @@
     )(*args)
 
 
-def stream_send(stream, wa, floats):
+def stream_send(stream, floats):
     return call(
         stream_send_kernel,
         [jax.ShapeDtypeStruct((6, 8192), F32), jax.ShapeDtypeStruct((256, 64, 128), BF)],
-        [SM] + [VM] * 9 + [HB],
-        [pltpu.VMEM((2, 64, 8192), BF), pltpu.VMEM((128 * PAD, 128), F32)]
-        + [pltpu.VMEM((64 * PAD2, 128), F32)] * 2
-        + [pltpu.VMEM((256 * PAD, 128), F32), pltpu.VMEM((256, 64, 128), BF)]
+        [VM] * 9 + [HB],
+        [pltpu.VMEM((2, 64, 8192), BF), pltpu.VMEM((129 * PAD, 128), F32)]
+        + [pltpu.VMEM((65 * PAD2, 128), F32)] * 2
+        + [pltpu.VMEM((257 * PAD, 128), F32), pltpu.VMEM((256, 64, 128), BF)]
         + [pltpu.SemaphoreType.DMA((4,))] * 2,
         int(6e9), 60, "stream_send",
-        wa, *floats, *send_tables(1.0, True), stream, out_specs=[VM, HB],
+        *floats, *send_tables(1.0, True), stream, out_specs=[VM, HB],
     )
 
 
@@ -221,7 +222,7 @@
         stream_recv_kernel,
         jax.ShapeDtypeStruct((128, 64, 128), BF),
         [SM] + [VM] * 5,
-        [pltpu.VMEM((256 * PAD, 128), F32), pltpu.VMEM((64 * PAD2, 128), F32)],
+        [pltpu.VMEM((257 * PAD, 128), F32), pltpu.VMEM((65 * PAD2, 128), F32)],
         int(6e9), 28, "stream_recv",
         idx, x, *recv_tables(1.0, True),
     )
@@ -293,18 +294,29 @@
         dye_send_kernel,
         jax.ShapeDtypeStruct((256, 32, 128), BF),
         [SM] + [VM] * 6,
-        [pltpu.VMEM((64 * PAD, 128), F32)] * 3 + [pltpu.VMEM((256 * PAD3, 128), F32)],
+        [pltpu.VMEM((65 * PAD, 128), F32)] * 3 + [pltpu.VMEM((257 * PAD3, 128), F32)],
         int(4e9), 24, "dye_send",
         idx, dye, ret, *send_tables(-1.0, False),
     )
 
 
-def dye_recv_kernel(x_ref, w1_ref, tc_ref, ts_ref, v_ref, o_hbm, xf, of, o_ref, out_sem):
-    def load(i, carry):
-        xf[pl.ds(pl.multiple_of(i * PAD3, 8), 32), :] = x_ref[i].astype(F32)
-        return carry
-
-    lax.fori_loop(0, 256, load, 0, unroll=8)
+def dye_recv_kernel(x_hbm, w1_ref, tc_ref, ts_ref, v_ref, o_hbm, xf, of, o_ref, x_ref, out_sem, in_sem):
+    reads = []
+    for h in range(2):
+        levels = pl.ds(16 * h, 16)
+        reads.append(
+            pltpu.make_async_copy(x_hbm.at[:, levels, :], x_ref.at[:, levels, :], in_sem.at[h])
+        )
+        reads[h].start()
+
+    def take(h):
+        def load(i, carry):
+            at = pl.ds(pl.multiple_of(i * PAD3 + 16 * h, 8), 16)
+            xf[at, :] = x_ref[i, 16 * h : 16 * h + 16].astype(F32)
+            return carry
+
+        reads[h].wait()
+        lax.fori_loop(0, 256, load, 0, unroll=8)
 
     def step(n, carry):
         d = jnp.concatenate([xf[pl.ds(2 * n + h, 256, stride=PAD3), :].astype(BF) for h in range(2)], axis=1)
@@ -331,6 +343,8 @@
 
     writes = []
     for k in range(8):
+        if k % 4 == 0:
+            take(k // 4)
         for n in range(2 * k, 2 * k + 2):
             step(n, 0)
         at = pl.ds(8 * k, 8)
@@ -347,9 +361,10 @@
     return call(
         dye_recv_kernel,
         jax.ShapeDtypeStruct((2, 64, 8192), F32),
-        [VM] * 5,
-        [pltpu.VMEM((256 * PAD3, 128), F32), pltpu.VMEM((8192, 128), F32)]
-        + [pltpu.VMEM((2, 64, 8192), F32), pltpu.SemaphoreType.DMA((8,))],
+        [HB] + [VM] * 4,
+        [pltpu.VMEM((257 * PAD3, 128), F32), pltpu.VMEM((8200, 128), F32)]
+        + [pltpu.VMEM((2, 64, 8192), F32), pltpu.VMEM((256, 32, 128), BF)]
+        + [pltpu.SemaphoreType.DMA((8,)), pltpu.SemaphoreType.DMA((2,))],
         int(4e9), 20, "dye_recv",
         x, *recv_tables(-1.0, False), out_specs=HB,
     )
@@ -479,7 +494,7 @@
         gather_kernel,
         [jax.ShapeDtypeStruct((1, 8192), F32)] * 2,
         [SM] + [VM] * 5,
-        [pltpu.VMEM((16384, 128), F32)] + [pltpu.VMEM((256, 128), F32)] * 8,
+        [pltpu.VMEM((16392, 128), F32)] + [pltpu.VMEM((256, 128), F32)] * 8,
         int(1e10), 20, "gather",
         base, a, b, col, fy, fx,
     )
@@ -507,13 +522,10 @@
     group = lax.axis_index("wide")
     core = lax.axis_index("narrow") % 2
     side = lax.axis_index("narrow") // 2 % 2
-    wave = device * 64 + jnp.arange(64)
-    wave = jnp.where(wave >= 4096, wave - 8192, wave).astype(F32)[None]
 
     line = lambda x: x.reshape(1, 8192)
     own_floats, spec = stream_send(
         stream_hat,
-        wave,
         (line(float_slot), line(float_row), line(float_col), float_frac, line(float_dye)),
     )
     their_floats = swap_chips(own_floats)

time: 179 us -> 179 us (level)
  no operation moved by 1% of the time
where the time goes in v8:
time: 179 us; the launch traced here: 178 us
  Pallas kernels  80.2 us (45%)
  waiting for transfers between devices  51.3 us (29%)
  starting transfers between devices  29.3 us (16%)
  local copies, waits for them, and re-layouts  9.71 us (5%)
  other arithmetic  6.3 us (4%)
    pallas_call x6, Pallas kernels, call(): pl.pallas_call(kernel, out_shape=outs, in_specs=specs, out_specs=out_spec...  80.2 us
    all_to_all x4, waiting for transfers between devices, spread(): return lax.all_to_all(blocks, AXES, split_axis=0, concat_axis=0, tiled=True)  51.3 us
    all_to_all x4, starting transfers between devices, spread(): return lax.all_to_all(blocks, AXES, split_axis=0, concat_axis=0, tiled=True)  24.9 us
    unnamed x39, local copies, waits for them, and re-layouts  8.72 us
  transfers between devices with their start and end apart: 8, of which 4 were waited for; matrix products, arithmetic and copies ran while one was open for 4% of the time, Pallas kernels for 39%

profile of v8, /device:TPU:1, one launch (start us, length us, event | category | flops | bytes accessed | tf_op | source)
XLA Modules:
  0.0 177.9 jit_solution(3005992641507774074)
XLA Ops:
  0.6 10.8 %stream_send.1 = (f32[6,8192]{1,0:T(8,128)}, bf16[256,64,128]{2,1,0:T(8,128)(2,1)}) custom-call(s32[1,8192]{1,0:T(1,128)} %bitcast.41, s32[1,8192]{1,0:T(1,128)} %bitcast.42, s32[1,8192]{1,0:T(1,128)} %bitcast.43, f32[2,8192]{1,0:T(2,128)} %frac_ref.1, f32[1,8192]{1,0:T(1,128)} %bitcast.44, bf16[256,128]{1,0:T(8,128)(2,1)} %constant.127.clone.g_ref, ...), custom_call_target="tpu_custom_call" | custom-call | flops 6000000000 | bytes 1048576 | tf_op jit(solution)/shard_map/stream_send/pallas_call | solution.py:155
  11.4 2.1 %collective-permute-start = (f32[6,8192]{1,0:T(8,128)}, f32[6,8192]{1,0:T(8,128)S(1)}, u32[]{:S(2)}, u32[]{:S(2)}) collective-permute-start(f32[6,8192]{1,0:T(8,128)} %get-tuple-element.21), channel_id=1, source_target_pairs={{0,2},{1,3},{2,0},{3,1},{4,6},{5,7},{6,4},{7,5},{8,10},{9,11},{10,... | collective-permute-start | bytes 589832 | tf_op jit(solution)/shard_map/ppermute | solution.py:517
  13.5 0.0 copy-start.16
  13.6 11.1 %all-to-all-start = ((bf16[128,2,64,128]{3,2,1,0:T(8,128)(2,1)}), bf16[128,2,64,128]{3,2,1,0:T(8,128)(2,1)}, u32[]{:S(2)}, u32[]{:S(2)}) async-start(bf16[128,2,64,128]{3,2,1,0:T(8,128)(2,1)} %bitcast.32), calls=%async_computation | async-start | bytes 8388608 | tf_op jit(solution)/shard_map/all_to_all | solution.py:507
  24.7 0.0 copy-done.16
  24.7 0.0 copy-done.15
  24.8 0.2 convert_reduce_fusion
  25.0 0.0 collective-permute-done
  25.0 0.3 fusion.6
  25.3 1.7 select_reduce_fusion
  27.1 32.0 %deposit.1 = (bf16[128,32,128]{2,1,0:T(8,128)(2,1)S(1)}, bf16[128,32,128]{2,1,0:T(8,128)(2,1)S(1)}) custom-call(s32[128,128]{1,0:T(8,128)S(1)} %get-tuple-element.48.idx_ref, s32[1,16384]{1,0:T(1,128)S(1)} %get-tuple-element.45.col_ref, f32[1,16384]{1,0:T(1,128)S(1)} %get-tuple-element.44.fy_ref, f32[1,16384]{1,0:T(1,128)S(1)} %get-tuple-element.43.fx_ref, ...), custom_call_target="tpu_custom_call" | custom-call | flops 20000000000 | bytes 1048576 | tf_op jit(solution)/shard_map/deposit/pallas_call | solution.py:155
  59.1 0.0 copy-start.6
  59.1 1.2 collective-permute-start.1
  60.3 0.6 convert_bitcast_fusion
  60.9 0.6 copy.42
  61.5 1.3 reduce-window.6
  62.8 0.0 collective-permute-done.1
  62.8 1.2 add_convert_fusion
  64.0 13.3 %all-to-all-done = bf16[128,2,64,128]{3,2,1,0:T(8,128)(2,1)} async-done(((bf16[128,2,64,128]{3,2,1,0:T(8,128)(2,1)}), bf16[128,2,64,128]{3,2,1,0:T(8,128)(2,1)}, u32[]{:S(2)}, u32[]{:S(2)}) %all-to-all-start) | async-done | bytes 4194336 | tf_op jit(solution)/shard_map/all_to_all | solution.py:507
  77.3 4.8 %all-to-all-start.2 = ((bf16[128,32,128]{2,1,0:T(8,128)(2,1)}), bf16[128,32,128]{2,1,0:T(8,128)(2,1)S(1)}, u32[]{:S(2)}, u32[]{:S(2)}) async-start(bf16[128,32,128]{2,1,0:T(8,128)(2,1)} %add_convert_fusion), calls=%async_computation.2 | async-start | bytes 2097152 | tf_op jit(solution)/shard_map/all_to_all | solution.py:507
  82.1 0.2 slice_reduce_fusion
  82.3 0.1 compare_bitcast_fusion
  82.4 0.0 copy-done.17
  82.4 0.0 copy-done.18
  82.4 0.1 select_reduce_fusion.2
  82.6 0.1 copy.35
  82.6 0.1 sub.39.idx_ref
  82.7 0.0 copy-done.6
  82.7 0.0 copy-start.7
  82.8 0.8 copy-done.7
  83.6 0.8 copy-done.10
  84.4 0.8 copy-done.11
  85.3 7.1 %stream_recv.1 = bf16[128,64,128]{2,1,0:T(8,128)(2,1)S(1)} custom-call(s32[1,32]{1,0:T(1,128)S(1)} %sub.39.idx_ref, bf16[256,64,128]{2,1,0:T(8,128)(2,1)} %bitcast.11.x_ref, bf16[256,256]{1,0:T(8,128)(2,1)S(1)} %copy-done.6, f32[128,128]{1,0:T(8,128)S(1)} %copy-done.7, f32[128,128]{1,0:T(8,128)S(1)} %copy-done.11, bf16[128,256]{1,0:T(8,128)(2,1)S(1)} %copy-done.10), custom_call_target="tpu_custom_call" | custom-call | flops 6000000000 | bytes 1048576 | tf_op jit(solution)/shard_map/stream_recv/pallas_call | solution.py:155
  92.4 0.0 copy-start.1
  92.4 1.3 copy-done.1
  93.7 7.7 %all-to-all-done.2.ret_ref = bf16[128,32,128]{2,1,0:T(8,128)(2,1)S(1)} async-done(((bf16[128,32,128]{2,1,0:T(8,128)(2,1)}), bf16[128,32,128]{2,1,0:T(8,128)(2,1)S(1)}, u32[]{:S(2)}, u32[]{:S(2)}) %all-to-all-start.2) | async-done | bytes 1048608 | tf_op jit(solution)/shard_map/all_to_all | solution.py:507
  101.4 4.3 %all-to-all-start.1 = ((bf16[128,64,128]{2,1,0:T(8,128)(2,1)}), bf16[128,64,128]{2,1,0:T(8,128)(2,1)S(1)}, u32[]{:S(2)}, u32[]{:S(2)}) async-start(bf16[128,64,128]{2,1,0:T(8,128)(2,1)} %copy-done.1), calls=%async_computation.1 | async-start | bytes 4194304 | tf_op jit(solution)/shard_map/all_to_all | solution.py:507
  105.8 0.0 copy-done.5
  105.8 0.0 copy-start.2
  105.8 1.2 copy-done.2
  107.0 0.8 copy-done.12
  107.8 0.8 copy-done.13
  108.5 0.8 copy-done.14
  109.3 4.2 %dye_send.1 = bf16[256,32,128]{2,1,0:T(8,128)(2,1)S(1)} custom-call(s32[1,32]{1,0:T(1,128)S(1)} %sub.39.idx_ref, bf16[64,8192]{1,0:T(8,128)(2,1)S(1)} %copy-done.2, bf16[128,32,128]{2,1,0:T(8,128)(2,1)S(1)} %all-to-all-done.2.ret_ref, bf16[128,64]{1,0:T(8,128)(2,1)S(1)} %copy-done.14, f32[64,128]{1,0:T(8,128)S(1)} %copy-done.12, f32[64,128]{1,0:T(8,128)S(1)} %copy-done.13, ...), custom_call_target="tpu_custom_call" | custom-call | flops 4000000000 | bytes 1048576 | tf_op jit(solution)/shard_map/dye_send/pallas_call | solution.py:155
  113.5 0.0 copy-start
  113.5 1.3 copy-done
  114.8 21.6 %all-to-all-done.1.a_ref = bf16[128,64,128]{2,1,0:T(8,128)(2,1)S(1)} async-done(((bf16[128,64,128]{2,1,0:T(8,128)(2,1)}), bf16[128,64,128]{2,1,0:T(8,128)(2,1)S(1)}, u32[]{:S(2)}, u32[]{:S(2)}) %all-to-all-start.1) | async-done | bytes 2097184 | tf_op jit(solution)/shard_map/all_to_all | solution.py:507
  136.4 0.9 collective-permute-start.2
  137.4 4.7 %all-to-all-start.3 = ((bf16[128,2,32,128]{3,2,1,0:T(8,128)(2,1)}), bf16[128,2,32,128]{3,2,1,0:T(8,128)(2,1)}, u32[]{:S(2)}, u32[]{:S(2)}) async-start(bf16[128,2,32,128]{3,2,1,0:T(8,128)(2,1)} %bitcast.31), calls=%async_computation.3 | async-start | bytes 4194304 | tf_op jit(solution)/shard_map/all_to_all | solution.py:507
  142.1 0.0 collective-permute-done.2.b_ref
  142.1 0.0 copy-start.3
  142.1 0.0 copy-start.4
  142.1 0.0 copy-start.8
  142.1 0.0 copy-start.9
  142.1 21.3 %gather.1 = (f32[1,8192]{1,0:T(1,128)S(1)}, f32[1,8192]{1,0:T(1,128)S(1)}) custom-call(s32[128,128]{1,0:T(8,128)S(1)} %get-tuple-element.49.base_ref, bf16[128,64,128]{2,1,0:T(8,128)(2,1)S(1)} %all-to-all-done.1.a_ref, bf16[128,64,128]{2,1,0:T(8,128)(2,1)} %collective-permute-done.2.b_ref, s32[1,16384]{1,0:T(1,128)S(1)} %get-tuple-element.45.col_ref, ...), custom_call_target="tpu_custom_call" | custom-call | flops 10000000000 | bytes 1048576 | tf_op jit(solution)/shard_map/gather/pallas_call | solution.py:155
  163.4 8.8 %all-to-all-done.3 = bf16[128,2,32,128]{3,2,1,0:T(8,128)(2,1)} async-done(((bf16[128,2,32,128]{3,2,1,0:T(8,128)(2,1)}), bf16[128,2,32,128]{3,2,1,0:T(8,128)(2,1)}, u32[]{:S(2)}, u32[]{:S(2)}) %all-to-all-start.3) | async-done | bytes 2097184 | tf_op jit(solution)/shard_map/all_to_all | solution.py:507
  172.2 0.1 collective-permute-start.3
  172.2 0.0 copy-done.3
  172.2 0.0 copy-done.4
  172.2 0.0 copy-done.8
  172.2 0.0 copy-done.9
  172.3 4.9 %dye_recv.1 = f32[2,64,8192]{2,1,0:T(8,128)} custom-call(bf16[256,32,128]{2,1,0:T(8,128)(2,1)} %bitcast.13.x_hbm, bf16[256,256]{1,0:T(8,128)(2,1)S(1)} %copy-done.4, f32[128,128]{1,0:T(8,128)S(1)} %copy-done.8, f32[128,128]{1,0:T(8,128)S(1)} %copy-done.9, bf16[256,256]{1,0:T(8,128)(2,1)S(1)} %copy-done.3), custom_call_target="tpu_custom_call" | custom-call | flops 4000000000 | bytes 1048576 | tf_op jit(solution)/shard_map/dye_recv/pallas_call | solution.py:155
  177.1 0.0 collective-permute-done.3
  177.1 0.7 maximum_select_fusion
  (18 shorter events, 0.2 us)
Async XLA Ops:
  11.4 13.6 %collective-permute-start = (f32[6,8192]{1,0:T(8,128)}, f32[6,8192]{1,0:T(8,128)S(1)}, u32[]{:S(2)}, u32[]{:S(2)}) collective-permute-start(f32[6,8192]{1,0:T(8,128)} %get-tuple-element.21), channel_id=1, source_target_pairs={{0,2},{1,3},{2,0},{3,1},{4,6},{5,7},{6,4},{7,5},{8,10},{9,11},{10,... | collective-permute-start | bytes 589832 | tf_op jit(solution)/shard_map/ppermute | solution.py:517
  13.5 11.2 %copy-start.16 = (s32[16,256]{1,0:T(8,128)S(1)}, s32[16,256]{1,0:T(8,128)}, u32[]{:S(2)}) copy-start(s32[16,256]{1,0:T(8,128)} %param.31) | copy-start | bytes 49156
  13.5 11.2 %copy-start.15 = (f32[6,8192]{1,0:T(8,128)S(1)}, f32[6,8192]{1,0:T(8,128)}, u32[]{:S(2)}) copy-start(f32[6,8192]{1,0:T(8,128)} %get-tuple-element.21) | copy-start | bytes 589828
  13.6 63.8 %all-to-all-start = ((bf16[128,2,64,128]{3,2,1,0:T(8,128)(2,1)}), bf16[128,2,64,128]{3,2,1,0:T(8,128)(2,1)}, u32[]{:S(2)}, u32[]{:S(2)}) async-start(bf16[128,2,64,128]{3,2,1,0:T(8,128)(2,1)} %bitcast.32), calls=%async_computation | async-start | bytes 8388608 | tf_op jit(solution)/shard_map/all_to_all | solution.py:507
  59.1 23.7 %copy-start.6 = (bf16[256,256]{1,0:T(8,128)(2,1)S(1)}, bf16[256,256]{1,0:T(8,128)(2,1)}, u32[]{:S(2)}) copy-start(bf16[256,256]{1,0:T(8,128)(2,1)} %constant.131.clone.w1_ref) | copy-start | bytes 393220
  59.1 3.7 %collective-permute-start.1 = (bf16[128,32,128]{2,1,0:T(8,128)(2,1)S(1)}, bf16[128,32,128]{2,1,0:T(8,128)(2,1)S(1)}, u32[]{:S(2)}, u32[]{:S(2)}) collective-permute-start(bf16[128,32,128]{2,1,0:T(8,128)(2,1)S(1)} %get-tuple-element.25), channel_id=1, source_target_pairs={{0,1},{1,0},{2,3},{3,2},{4,5},{5,4},{6,7},{7,6},{8,9},{9,8},{10,11... | collective-permute-start | bytes 3145736 | tf_op jit(solution)/shard_map/ppermute | solution.py:512
  62.8 19.6 %copy-start.17 = (s32[16,256]{1,0:T(8,128)S(1)}, s32[16,256]{1,0:T(8,128)}, u32[]{:S(2)}) copy-start(s32[16,256]{1,0:T(8,128)} %param.31) | copy-start | bytes 49156
  62.8 19.6 %copy-start.18 = (pred[16,256]{1,0:T(8,128)(4,1)S(1)}, pred[16,256]{1,0:T(8,128)(4,1)}, u32[]{:S(2)}) copy-start(pred[16,256]{1,0:T(8,128)(4,1)} %get-tuple-element.39) | copy-start | bytes 12292
  77.3 24.1 %all-to-all-start.2 = ((bf16[128,32,128]{2,1,0:T(8,128)(2,1)}), bf16[128,32,128]{2,1,0:T(8,128)(2,1)S(1)}, u32[]{:S(2)}, u32[]{:S(2)}) async-start(bf16[128,32,128]{2,1,0:T(8,128)(2,1)} %add_convert_fusion), calls=%async_computation.2 | async-start | bytes 2097152 | tf_op jit(solution)/shard_map/all_to_all | solution.py:507
  82.7 0.8 copy-start.7
  83.6 0.8 copy-start.10
  84.4 0.8 copy-start.11
  92.4 1.3 copy-start.1
  93.7 12.0 %copy-start.5 = (bf16[256,256]{1,0:T(8,128)(2,1)S(1)}, bf16[256,256]{1,0:T(8,128)(2,1)}, u32[]{:S(2)}) copy-start(bf16[256,256]{1,0:T(8,128)(2,1)} %constant.137.clone.w2_ref) | copy-start | bytes 393220
  101.4 35.0 %all-to-all-start.1 = ((bf16[128,64,128]{2,1,0:T(8,128)(2,1)}), bf16[128,64,128]{2,1,0:T(8,128)(2,1)S(1)}, u32[]{:S(2)}, u32[]{:S(2)}) async-start(bf16[128,64,128]{2,1,0:T(8,128)(2,1)} %copy-done.1), calls=%async_computation.1 | async-start | bytes 4194304 | tf_op jit(solution)/shard_map/all_to_all | solution.py:507
  105.8 1.2 copy-start.2
  107.0 0.8 copy-start.12
  107.8 0.8 copy-start.13
  108.5 0.8 copy-start.14
  113.5 1.3 copy-start
  136.4 5.7 %collective-permute-start.2 = (bf16[128,64,128]{2,1,0:T(8,128)(2,1)S(1)}, bf16[128,64,128]{2,1,0:T(8,128)(2,1)}, u32[]{:S(2)}, u32[]{:S(2)}) collective-permute-start(bf16[128,64,128]{2,1,0:T(8,128)(2,1)S(1)} %all-to-all-done.1.a_ref), channel_id=1, source_target_pairs={{0,1},{1,0},{2,3},{3,2},{4,5},{5,4},{6,7},{7,6},{8,9},{9,8},{10,11... | collective-permute-start | bytes 6291464 | tf_op jit(solution)/shard_map/ppermute | solution.py:512
  137.4 34.8 %all-to-all-start.3 = ((bf16[128,2,32,128]{3,2,1,0:T(8,128)(2,1)}), bf16[128,2,32,128]{3,2,1,0:T(8,128)(2,1)}, u32[]{:S(2)}, u32[]{:S(2)}) async-start(bf16[128,2,32,128]{3,2,1,0:T(8,128)(2,1)} %bitcast.31), calls=%async_computation.3 | async-start | bytes 4194304 | tf_op jit(solution)/shard_map/all_to_all | solution.py:507
  142.1 30.2 %copy-start.3 = (bf16[256,256]{1,0:T(8,128)(2,1)S(1)}, bf16[256,256]{1,0:T(8,128)(2,1)}, u32[]{:S(2)}) copy-start(bf16[256,256]{1,0:T(8,128)(2,1)} %constant.140.clone.v_ref) | copy-start | bytes 393220
  142.1 30.1 %copy-start.4 = (bf16[256,256]{1,0:T(8,128)(2,1)S(1)}, bf16[256,256]{1,0:T(8,128)(2,1)}, u32[]{:S(2)}) copy-start(bf16[256,256]{1,0:T(8,128)(2,1)} %constant.138.clone.w1_ref) | copy-start | bytes 393220
  142.1 30.1 %copy-start.8 = (f32[128,128]{1,0:T(8,128)S(1)}, f32[128,128]{1,0:T(8,128)}, u32[]{:S(2)}) copy-start(f32[128,128]{1,0:T(8,128)} %constant.132.clone.tc_ref) | copy-start | bytes 196612
  142.1 30.1 %copy-start.9 = (f32[128,128]{1,0:T(8,128)S(1)}, f32[128,128]{1,0:T(8,128)}, u32[]{:S(2)}) copy-start(f32[128,128]{1,0:T(8,128)} %constant.139.clone.ts_ref) | copy-start | bytes 196612
  172.2 4.9 %collective-permute-start.3 = (f32[1,8192]{1,0:T(1,128)S(1)}, f32[1,8192]{1,0:T(1,128)S(1)}, u32[]{:S(2)}, u32[]{:S(2)}) collective-permute-start(f32[1,8192]{1,0:T(1,128)S(1)} %get-tuple-element.34), channel_id=1, source_target_pairs={{0,2},{1,3},{2,0},{3,1},{4,6},{5,7},{6,4},{7,5},{8,10},{9,11},{10,... | collective-permute-start | bytes 98312 | tf_op jit(solution)/shard_map/ppermute | solution.py:517

commit v9 on v8

--- a/solution.py
+++ b/solution.py
@@ -9,9 +9,9 @@
 BF = jnp.bfloat16
 F32 = jnp.float32
 NT = (((1,), (1,)), ((), ()))
-PAD = 72
-PAD2 = 136
-PAD3 = 40
+PAD = 73
+PAD2 = 137
+PAD3 = 41
 
 
 def cs(num, den, sign):
@@ -85,7 +85,7 @@
     def load(p, carry):
         at = pl.multiple_of(p * 128, 128)
         for c in range(2):
-            row = pl.multiple_of((c * 64 + p) * PAD, 8)
+            row = (c * 64 + p) * PAD
             xs[pl.ds(row, 64), :] = s_ref[c, :, pl.ds(at, 128)].astype(F32)
         return carry
 
@@ -107,7 +107,7 @@
             ure = bre + q * are
             uim = bim + q * aim
             wa = jnp.where(first + r >= 4096, first + r - 8192, first + r).astype(F32)
-            base = pl.multiple_of(r * PAD2, 8)
+            base = r * PAD2
             vre = are * tc - aim * ts
             vim = are * ts + aim * tc
             tre[pl.ds(base, 64), :] = ure * ts + uim * tc
@@ -135,10 +135,10 @@
         lax.fori_loop(8 * k, 8 * k + 8, cols, 0, unroll=8)
 
         def store(i, carry, k=k):
-            o_ref[i, 16 * k : 16 * k + 16] = of[pl.ds(pl.multiple_of(i * PAD + 16 * k, 8), 16), :].astype(BF)
+            o_ref[i, 16 * k : 16 * k + 16] = of[pl.ds(i * PAD + 16 * k, 16), :].astype(BF)
             return carry
 
-        lax.fori_loop(0, 256, store, 0, unroll=8)
+        lax.fori_loop(0, 256, store, 0, unroll=16)
         levels = pl.ds(16 * k, 16)
         writes.append(pltpu.make_async_copy(o_ref.at[:, levels, :], o_hbm.at[:, levels, :], out_sem.at[k]))
         writes[k].start()
@@ -180,7 +180,7 @@
 
 def stream_recv_kernel(idx_ref, x_ref, w1_ref, tc_ref, ts_ref, v_ref, o_ref, xf, of):
     def load(i, carry):
-        xf[pl.ds(pl.multiple_of(i * PAD, 8), 64), :] = x_ref[i].astype(F32)
+        xf[pl.ds(i * PAD, 64), :] = x_ref[i].astype(F32)
         return carry
 
     lax.fori_loop(0, 256, load, 0, unroll=8)
@@ -209,7 +209,7 @@
     def store(n, carry):
         tile = jnp.maximum(idx_ref[0, n], 0)
         for f in range(2):
-            data = of[pl.ds(pl.multiple_of(tile * PAD2, 8) + 64 * f, 64), :].astype(BF)
+            data = of[pl.ds(tile * PAD2 + 64 * f, 64), :].astype(BF)
             for x in range(2):
                 o_ref[n // 2 * 8 + 4 * x + 2 * f + n % 2] = data
         return carry
@@ -231,7 +231,7 @@
 def dye_send_kernel(idx_ref, dye_ref, ret_ref, g_ref, tc_ref, ts_ref, w2_ref, o_ref, xs, tre, tim, of):
     def load(p, carry):
         at = pl.multiple_of(p * 128, 128)
-        xs[pl.ds(pl.multiple_of(p * PAD, 8), 64), :] = dye_ref[:, pl.ds(at, 128)].astype(F32)
+        xs[pl.ds(p * PAD, 64), :] = dye_ref[:, pl.ds(at, 128)].astype(F32)
         return carry
 
     lax.fori_loop(0, 64, load, 0, unroll=4)
@@ -244,7 +244,7 @@
             g = n // 2
             e = n % 2
             for half in range(2):
-                at = pl.ds(pl.multiple_of(tile * PAD, 8) + 32 * half, 32)
+                at = pl.ds(tile * PAD + 32 * half, 32)
                 total = xs[at, :]
                 for x in range(2):
                     total = total + ret_ref[g * 8 + 4 * x + 2 * half + e].astype(F32)
@@ -262,7 +262,7 @@
         for h in range(4):
             re = z[:64, h * 128 : h * 128 + 128]
             im = z[64:, h * 128 : h * 128 + 128]
-            base = pl.multiple_of((4 * n + h) * PAD, 8)
+            base = (4 * n + h) * PAD
             tre[pl.ds(base, 64), :] = re * tc - im * ts
             tim[pl.ds(base, 64), :] = re * ts + im * tc
         return carry
@@ -283,7 +283,7 @@
     lax.fori_loop(0, 16, cols, 0, unroll=8)
 
     def store(i, carry):
-        o_ref[i] = of[pl.ds(pl.multiple_of(i * PAD3, 8), 32), :].astype(BF)
+        o_ref[i] = of[pl.ds(i * PAD3, 32), :].astype(BF)
         return carry
 
     lax.fori_loop(0, 256, store, 0, unroll=8)
@@ -311,7 +311,7 @@
 
     def take(h):
         def load(i, carry):
-            at = pl.ds(pl.multiple_of(i * PAD3 + 16 * h, 8), 16)
+            at = pl.ds(i * PAD3 + 16 * h, 16)
             xf[at, :] = x_ref[i, 16 * h : 16 * h + 16].astype(F32)
             return carry
 

time: 179 us -> 177 us (0.989)
  Pallas kernels: 80.2 us -> 77.7 us
    pallas_call x6, Pallas kernels: 80.2 us -> 77.7 us  [call(): pl.pallas_call(kernel, out_shape=outs, in_specs=specs, out_specs=out_spec...]
where the time goes in v9:
time: 177 us; the launch traced here: 176 us
  Pallas kernels  77.7 us (44%)
  waiting for transfers between devices  52.1 us (29%)
  starting transfers between devices  29.5 us (17%)
  local copies, waits for them, and re-layouts  9.72 us (5%)
  other arithmetic  6.3 us (4%)
    pallas_call x6, Pallas kernels, call(): pl.pallas_call(kernel, out_shape=outs, in_specs=specs, out_specs=out_spec...  77.7 us
    all_to_all x4, waiting for transfers between devices, spread(): return lax.all_to_all(blocks, AXES, split_axis=0, concat_axis=0, tiled=True)  52.1 us
    all_to_all x4, starting transfers between devices, spread(): return lax.all_to_all(blocks, AXES, split_axis=0, concat_axis=0, tiled=True)  25.1 us
    unnamed x39, local copies, waits for them, and re-layouts  8.73 us
  transfers between devices with their start and end apart: 8, of which 4 were waited for; matrix products, arithmetic and copies ran while one was open for 4% of the time, Pallas kernels for 39%

profile of v9, /device:TPU:1, one launch (start us, length us, event | category | flops | bytes accessed | tf_op | source)
XLA Modules:
  0.0 176.3 jit_solution(16912798277671168227)
XLA Ops:
  0.6 9.4 %stream_send.1 = (f32[6,8192]{1,0:T(8,128)}, bf16[256,64,128]{2,1,0:T(8,128)(2,1)}) custom-call(s32[1,8192]{1,0:T(1,128)} %bitcast.41, s32[1,8192]{1,0:T(1,128)} %bitcast.42, s32[1,8192]{1,0:T(1,128)} %bitcast.43, f32[2,8192]{1,0:T(2,128)} %frac_ref.1, f32[1,8192]{1,0:T(1,128)} %bitcast.44, bf16[256,128]{1,0:T(8,128)(2,1)} %constant.127.clone.g_ref, ...), custom_call_target="tpu_custom_call" | custom-call | flops 6000000000 | bytes 1048576 | tf_op jit(solution)/shard_map/stream_send/pallas_call | solution.py:155
  10.1 2.1 %collective-permute-start = (f32[6,8192]{1,0:T(8,128)}, f32[6,8192]{1,0:T(8,128)S(1)}, u32[]{:S(2)}, u32[]{:S(2)}) collective-permute-start(f32[6,8192]{1,0:T(8,128)} %get-tuple-element.21), channel_id=1, source_target_pairs={{0,2},{1,3},{2,0},{3,1},{4,6},{5,7},{6,4},{7,5},{8,10},{9,11},{10,... | collective-permute-start | bytes 589832 | tf_op jit(solution)/shard_map/ppermute | solution.py:517
  12.2 0.0 copy-start.16
  12.2 11.1 %all-to-all-start = ((bf16[128,2,64,128]{3,2,1,0:T(8,128)(2,1)}), bf16[128,2,64,128]{3,2,1,0:T(8,128)(2,1)}, u32[]{:S(2)}, u32[]{:S(2)}) async-start(bf16[128,2,64,128]{3,2,1,0:T(8,128)(2,1)} %bitcast.32), calls=%async_computation | async-start | bytes 8388608 | tf_op jit(solution)/shard_map/all_to_all | solution.py:507
  23.3 0.0 copy-done.16
  23.4 0.0 copy-done.15
  23.4 0.2 convert_reduce_fusion
  23.6 0.0 collective-permute-done
  23.7 0.3 fusion.6
  24.0 1.7 select_reduce_fusion
  25.7 32.0 %deposit.1 = (bf16[128,32,128]{2,1,0:T(8,128)(2,1)S(1)}, bf16[128,32,128]{2,1,0:T(8,128)(2,1)S(1)}) custom-call(s32[128,128]{1,0:T(8,128)S(1)} %get-tuple-element.48.idx_ref, s32[1,16384]{1,0:T(1,128)S(1)} %get-tuple-element.45.col_ref, f32[1,16384]{1,0:T(1,128)S(1)} %get-tuple-element.44.fy_ref, f32[1,16384]{1,0:T(1,128)S(1)} %get-tuple-element.43.fx_ref, ...), custom_call_target="tpu_custom_call" | custom-call | flops 20000000000 | bytes 1048576 | tf_op jit(solution)/shard_map/deposit/pallas_call | solution.py:155
  57.6 0.0 copy-start.6
  57.7 1.3 collective-permute-start.1
  58.9 0.6 convert_bitcast_fusion
  59.5 0.6 copy.42
  60.1 1.3 reduce-window.6
  61.4 0.0 collective-permute-done.1
  61.4 1.2 add_convert_fusion
  62.6 13.3 %all-to-all-done = bf16[128,2,64,128]{3,2,1,0:T(8,128)(2,1)} async-done(((bf16[128,2,64,128]{3,2,1,0:T(8,128)(2,1)}), bf16[128,2,64,128]{3,2,1,0:T(8,128)(2,1)}, u32[]{:S(2)}, u32[]{:S(2)}) %all-to-all-start) | async-done | bytes 4194336 | tf_op jit(solution)/shard_map/all_to_all | solution.py:507
  75.9 4.8 %all-to-all-start.2 = ((bf16[128,32,128]{2,1,0:T(8,128)(2,1)}), bf16[128,32,128]{2,1,0:T(8,128)(2,1)S(1)}, u32[]{:S(2)}, u32[]{:S(2)}) async-start(bf16[128,32,128]{2,1,0:T(8,128)(2,1)} %add_convert_fusion), calls=%async_computation.2 | async-start | bytes 2097152 | tf_op jit(solution)/shard_map/all_to_all | solution.py:507
  80.7 0.2 slice_reduce_fusion
  80.9 0.1 compare_bitcast_fusion
  81.0 0.0 copy-done.17
  81.0 0.0 copy-done.18
  81.1 0.1 select_reduce_fusion.2
  81.2 0.1 copy.35
  81.3 0.1 sub.39.idx_ref
  81.4 0.0 copy-done.6
  81.4 0.0 copy-start.7
  81.4 0.8 copy-done.7
  82.2 0.8 copy-done.10
  83.1 0.8 copy-done.11
  83.9 6.8 %stream_recv.1 = bf16[128,64,128]{2,1,0:T(8,128)(2,1)S(1)} custom-call(s32[1,32]{1,0:T(1,128)S(1)} %sub.39.idx_ref, bf16[256,64,128]{2,1,0:T(8,128)(2,1)} %bitcast.11.x_ref, bf16[256,256]{1,0:T(8,128)(2,1)S(1)} %copy-done.6, f32[128,128]{1,0:T(8,128)S(1)} %copy-done.7, f32[128,128]{1,0:T(8,128)S(1)} %copy-done.11, bf16[128,256]{1,0:T(8,128)(2,1)S(1)} %copy-done.10), custom_call_target="tpu_custom_call" | custom-call | flops 6000000000 | bytes 1048576 | tf_op jit(solution)/shard_map/stream_recv/pallas_call | solution.py:155
  90.7 0.0 copy-start.1
  90.7 1.3 copy-done.1
  92.0 8.1 %all-to-all-done.2.ret_ref = bf16[128,32,128]{2,1,0:T(8,128)(2,1)S(1)} async-done(((bf16[128,32,128]{2,1,0:T(8,128)(2,1)}), bf16[128,32,128]{2,1,0:T(8,128)(2,1)S(1)}, u32[]{:S(2)}, u32[]{:S(2)}) %all-to-all-start.2) | async-done | bytes 1048608 | tf_op jit(solution)/shard_map/all_to_all | solution.py:507
  100.1 4.3 %all-to-all-start.1 = ((bf16[128,64,128]{2,1,0:T(8,128)(2,1)}), bf16[128,64,128]{2,1,0:T(8,128)(2,1)S(1)}, u32[]{:S(2)}, u32[]{:S(2)}) async-start(bf16[128,64,128]{2,1,0:T(8,128)(2,1)} %copy-done.1), calls=%async_computation.1 | async-start | bytes 4194304 | tf_op jit(solution)/shard_map/all_to_all | solution.py:507
  104.4 0.0 copy-done.5
  104.4 0.0 copy-start.2
  104.4 1.2 copy-done.2
  105.7 0.8 copy-done.12
  106.4 0.8 copy-done.13
  107.2 0.8 copy-done.14
  107.9 3.6 %dye_send.1 = bf16[256,32,128]{2,1,0:T(8,128)(2,1)S(1)} custom-call(s32[1,32]{1,0:T(1,128)S(1)} %sub.39.idx_ref, bf16[64,8192]{1,0:T(8,128)(2,1)S(1)} %copy-done.2, bf16[128,32,128]{2,1,0:T(8,128)(2,1)S(1)} %all-to-all-done.2.ret_ref, bf16[128,64]{1,0:T(8,128)(2,1)S(1)} %copy-done.14, f32[64,128]{1,0:T(8,128)S(1)} %copy-done.12, f32[64,128]{1,0:T(8,128)S(1)} %copy-done.13, ...), custom_call_target="tpu_custom_call" | custom-call | flops 4000000000 | bytes 1048576 | tf_op jit(solution)/shard_map/dye_send/pallas_call | solution.py:155
  111.5 0.0 copy-start
  111.5 1.3 copy-done
  112.9 22.2 %all-to-all-done.1.a_ref = bf16[128,64,128]{2,1,0:T(8,128)(2,1)S(1)} async-done(((bf16[128,64,128]{2,1,0:T(8,128)(2,1)}), bf16[128,64,128]{2,1,0:T(8,128)(2,1)S(1)}, u32[]{:S(2)}, u32[]{:S(2)}) %all-to-all-start.1) | async-done | bytes 2097184 | tf_op jit(solution)/shard_map/all_to_all | solution.py:507
  135.1 0.9 collective-permute-start.2
  136.0 4.9 %all-to-all-start.3 = ((bf16[128,2,32,128]{3,2,1,0:T(8,128)(2,1)}), bf16[128,2,32,128]{3,2,1,0:T(8,128)(2,1)}, u32[]{:S(2)}, u32[]{:S(2)}) async-start(bf16[128,2,32,128]{3,2,1,0:T(8,128)(2,1)} %bitcast.31), calls=%async_computation.3 | async-start | bytes 4194304 | tf_op jit(solution)/shard_map/all_to_all | solution.py:507
  140.9 0.0 collective-permute-done.2.b_ref
  140.9 0.0 copy-start.3
  140.9 0.0 copy-start.4
  140.9 0.0 copy-start.8
  140.9 0.0 copy-start.9
  140.9 21.3 %gather.1 = (f32[1,8192]{1,0:T(1,128)S(1)}, f32[1,8192]{1,0:T(1,128)S(1)}) custom-call(s32[128,128]{1,0:T(8,128)S(1)} %get-tuple-element.49.base_ref, bf16[128,64,128]{2,1,0:T(8,128)(2,1)S(1)} %all-to-all-done.1.a_ref, bf16[128,64,128]{2,1,0:T(8,128)(2,1)} %collective-permute-done.2.b_ref, s32[1,16384]{1,0:T(1,128)S(1)} %get-tuple-element.45.col_ref, ...), custom_call_target="tpu_custom_call" | custom-call | flops 10000000000 | bytes 1048576 | tf_op jit(solution)/shard_map/gather/pallas_call | solution.py:155
  162.2 8.6 %all-to-all-done.3 = bf16[128,2,32,128]{3,2,1,0:T(8,128)(2,1)} async-done(((bf16[128,2,32,128]{3,2,1,0:T(8,128)(2,1)}), bf16[128,2,32,128]{3,2,1,0:T(8,128)(2,1)}, u32[]{:S(2)}, u32[]{:S(2)}) %all-to-all-start.3) | async-done | bytes 2097184 | tf_op jit(solution)/shard_map/all_to_all | solution.py:507
  170.8 0.1 collective-permute-start.3
  170.9 0.0 copy-done.3
  170.9 0.0 copy-done.4
  170.9 0.0 copy-done.8
  170.9 0.0 copy-done.9
  170.9 4.7 %dye_recv.1 = f32[2,64,8192]{2,1,0:T(8,128)} custom-call(bf16[256,32,128]{2,1,0:T(8,128)(2,1)} %bitcast.13.x_hbm, bf16[256,256]{1,0:T(8,128)(2,1)S(1)} %copy-done.4, f32[128,128]{1,0:T(8,128)S(1)} %copy-done.8, f32[128,128]{1,0:T(8,128)S(1)} %copy-done.9, bf16[256,256]{1,0:T(8,128)(2,1)S(1)} %copy-done.3), custom_call_target="tpu_custom_call" | custom-call | flops 4000000000 | bytes 1048576 | tf_op jit(solution)/shard_map/dye_recv/pallas_call | solution.py:155
  175.5 0.0 collective-permute-done.3
  175.6 0.7 maximum_select_fusion
  (18 shorter events, 0.2 us)
Async XLA Ops:
  10.1 13.6 %collective-permute-start = (f32[6,8192]{1,0:T(8,128)}, f32[6,8192]{1,0:T(8,128)S(1)}, u32[]{:S(2)}, u32[]{:S(2)}) collective-permute-start(f32[6,8192]{1,0:T(8,128)} %get-tuple-element.21), channel_id=1, source_target_pairs={{0,2},{1,3},{2,0},{3,1},{4,6},{5,7},{6,4},{7,5},{8,10},{9,11},{10,... | collective-permute-start | bytes 589832 | tf_op jit(solution)/shard_map/ppermute | solution.py:517
  12.2 11.2 %copy-start.16 = (s32[16,256]{1,0:T(8,128)S(1)}, s32[16,256]{1,0:T(8,128)}, u32[]{:S(2)}) copy-start(s32[16,256]{1,0:T(8,128)} %param.31) | copy-start | bytes 49156
  12.2 11.2 %copy-start.15 = (f32[6,8192]{1,0:T(8,128)S(1)}, f32[6,8192]{1,0:T(8,128)}, u32[]{:S(2)}) copy-start(f32[6,8192]{1,0:T(8,128)} %get-tuple-element.21) | copy-start | bytes 589828
  12.2 63.8 %all-to-all-start = ((bf16[128,2,64,128]{3,2,1,0:T(8,128)(2,1)}), bf16[128,2,64,128]{3,2,1,0:T(8,128)(2,1)}, u32[]{:S(2)}, u32[]{:S(2)}) async-start(bf16[128,2,64,128]{3,2,1,0:T(8,128)(2,1)} %bitcast.32), calls=%async_computation | async-start | bytes 8388608 | tf_op jit(solution)/shard_map/all_to_all | solution.py:507
  57.6 23.7 %copy-start.6 = (bf16[256,256]{1,0:T(8,128)(2,1)S(1)}, bf16[256,256]{1,0:T(8,128)(2,1)}, u32[]{:S(2)}) copy-start(bf16[256,256]{1,0:T(8,128)(2,1)} %constant.131.clone.w1_ref) | copy-start | bytes 393220
  57.7 3.7 %collective-permute-start.1 = (bf16[128,32,128]{2,1,0:T(8,128)(2,1)S(1)}, bf16[128,32,128]{2,1,0:T(8,128)(2,1)S(1)}, u32[]{:S(2)}, u32[]{:S(2)}) collective-permute-start(bf16[128,32,128]{2,1,0:T(8,128)(2,1)S(1)} %get-tuple-element.25), channel_id=1, source_target_pairs={{0,1},{1,0},{2,3},{3,2},{4,5},{5,4},{6,7},{7,6},{8,9},{9,8},{10,11... | collective-permute-start | bytes 3145736 | tf_op jit(solution)/shard_map/ppermute | solution.py:512
  61.4 19.6 %copy-start.17 = (s32[16,256]{1,0:T(8,128)S(1)}, s32[16,256]{1,0:T(8,128)}, u32[]{:S(2)}) copy-start(s32[16,256]{1,0:T(8,128)} %param.31) | copy-start | bytes 49156
  61.4 19.7 %copy-start.18 = (pred[16,256]{1,0:T(8,128)(4,1)S(1)}, pred[16,256]{1,0:T(8,128)(4,1)}, u32[]{:S(2)}) copy-start(pred[16,256]{1,0:T(8,128)(4,1)} %get-tuple-element.39) | copy-start | bytes 12292
  75.9 24.1 %all-to-all-start.2 = ((bf16[128,32,128]{2,1,0:T(8,128)(2,1)}), bf16[128,32,128]{2,1,0:T(8,128)(2,1)S(1)}, u32[]{:S(2)}, u32[]{:S(2)}) async-start(bf16[128,32,128]{2,1,0:T(8,128)(2,1)} %add_convert_fusion), calls=%async_computation.2 | async-start | bytes 2097152 | tf_op jit(solution)/shard_map/all_to_all | solution.py:507
  81.4 0.8 copy-start.7
  82.2 0.8 copy-start.10
  83.1 0.8 copy-start.11
  90.7 1.3 copy-start.1
  92.0 12.4 %copy-start.5 = (bf16[256,256]{1,0:T(8,128)(2,1)S(1)}, bf16[256,256]{1,0:T(8,128)(2,1)}, u32[]{:S(2)}) copy-start(bf16[256,256]{1,0:T(8,128)(2,1)} %constant.137.clone.w2_ref) | copy-start | bytes 393220
  100.1 35.0 %all-to-all-start.1 = ((bf16[128,64,128]{2,1,0:T(8,128)(2,1)}), bf16[128,64,128]{2,1,0:T(8,128)(2,1)S(1)}, u32[]{:S(2)}, u32[]{:S(2)}) async-start(bf16[128,64,128]{2,1,0:T(8,128)(2,1)} %copy-done.1), calls=%async_computation.1 | async-start | bytes 4194304 | tf_op jit(solution)/shard_map/all_to_all | solution.py:507
  104.4 1.2 copy-start.2
  105.6 0.8 copy-start.12
  106.4 0.8 copy-start.13
  107.2 0.8 copy-start.14
  111.5 1.3 copy-start
  135.1 5.8 %collective-permute-start.2 = (bf16[128,64,128]{2,1,0:T(8,128)(2,1)S(1)}, bf16[128,64,128]{2,1,0:T(8,128)(2,1)}, u32[]{:S(2)}, u32[]{:S(2)}) collective-permute-start(bf16[128,64,128]{2,1,0:T(8,128)(2,1)S(1)} %all-to-all-done.1.a_ref), channel_id=1, source_target_pairs={{0,1},{1,0},{2,3},{3,2},{4,5},{5,4},{6,7},{7,6},{8,9},{9,8},{10,11... | collective-permute-start | bytes 6291464 | tf_op jit(solution)/shard_map/ppermute | solution.py:512
  136.0 34.8 %all-to-all-start.3 = ((bf16[128,2,32,128]{3,2,1,0:T(8,128)(2,1)}), bf16[128,2,32,128]{3,2,1,0:T(8,128)(2,1)}, u32[]{:S(2)}, u32[]{:S(2)}) async-start(bf16[128,2,32,128]{3,2,1,0:T(8,128)(2,1)} %bitcast.31), calls=%async_computation.3 | async-start | bytes 4194304 | tf_op jit(solution)/shard_map/all_to_all | solution.py:507
  140.9 30.0 %copy-start.3 = (bf16[256,256]{1,0:T(8,128)(2,1)S(1)}, bf16[256,256]{1,0:T(8,128)(2,1)}, u32[]{:S(2)}) copy-start(bf16[256,256]{1,0:T(8,128)(2,1)} %constant.140.clone.v_ref) | copy-start | bytes 393220
  140.9 30.0 %copy-start.4 = (bf16[256,256]{1,0:T(8,128)(2,1)S(1)}, bf16[256,256]{1,0:T(8,128)(2,1)}, u32[]{:S(2)}) copy-start(bf16[256,256]{1,0:T(8,128)(2,1)} %constant.138.clone.w1_ref) | copy-start | bytes 393220
  140.9 30.0 %copy-start.8 = (f32[128,128]{1,0:T(8,128)S(1)}, f32[128,128]{1,0:T(8,128)}, u32[]{:S(2)}) copy-start(f32[128,128]{1,0:T(8,128)} %constant.132.clone.tc_ref) | copy-start | bytes 196612
  140.9 29.9 %copy-start.9 = (f32[128,128]{1,0:T(8,128)S(1)}, f32[128,128]{1,0:T(8,128)}, u32[]{:S(2)}) copy-start(f32[128,128]{1,0:T(8,128)} %constant.139.clone.ts_ref) | copy-start | bytes 196612
  170.8 4.7 %collective-permute-start.3 = (f32[1,8192]{1,0:T(1,128)S(1)}, f32[1,8192]{1,0:T(1,128)S(1)}, u32[]{:S(2)}, u32[]{:S(2)}) collective-permute-start(f32[1,8192]{1,0:T(1,128)S(1)} %get-tuple-element.34), channel_id=1, source_target_pairs={{0,2},{1,3},{2,0},{3,1},{4,6},{5,7},{6,4},{7,5},{8,10},{9,11},{10,... | collective-permute-start | bytes 98312 | tf_op jit(solution)/shard_map/ppermute | solution.py:517

commit v10 on v9

--- a/solution.py
+++ b/solution.py
@@ -571,8 +571,8 @@
     front = spread(front.reshape(128, 2, 32, 128)).reshape(256, 32, 128)
 
     mine, theirs = gather(pos * 64 + row, own, other, col, fy, fx)
-    mine, theirs, front = lax.optimization_barrier((mine, theirs, front))
     back = swap_chips(theirs)
+    mine, front = lax.optimization_barrier((mine, front))
     velocity = jnp.where(side == 0, jnp.concatenate([mine, back]), jnp.concatenate([back, mine]))
     dye_hat = dye_recv(front)
     return (velocity, dye_hat)

time: 177 us -> 177 us (level)
  no operation moved by 1% of the time
where the time goes in v10:
time: 177 us; the launch traced here: 176 us
  Pallas kernels  77.9 us (44%)
  waiting for transfers between devices  52 us (29%)
  starting transfers between devices  29.4 us (17%)
  local copies, waits for them, and re-layouts  9.71 us (5%)
  other arithmetic  6.3 us (4%)
    pallas_call x6, Pallas kernels, call(): pl.pallas_call(kernel, out_shape=outs, in_specs=specs, out_specs=out_spec...  77.9 us
    all_to_all x4, waiting for transfers between devices, spread(): return lax.all_to_all(blocks, AXES, split_axis=0, concat_axis=0, tiled=True)  52 us
    all_to_all x4, starting transfers between devices, spread(): return lax.all_to_all(blocks, AXES, split_axis=0, concat_axis=0, tiled=True)  25.1 us
    unnamed x39, local copies, waits for them, and re-layouts  8.72 us
  transfers between devices with their start and end apart: 8, of which 4 were waited for; matrix products, arithmetic and copies ran while one was open for 4% of the time, Pallas kernels for 39%

profile of v10, /device:TPU:1, one launch (start us, length us, event | category | flops | bytes accessed | tf_op | source)
XLA Modules:
  0.0 176.3 jit_solution(16912798277671168227)
XLA Ops:
  0.6 9.4 %stream_send.1 = (f32[6,8192]{1,0:T(8,128)}, bf16[256,64,128]{2,1,0:T(8,128)(2,1)}) custom-call(s32[1,8192]{1,0:T(1,128)} %bitcast.41, s32[1,8192]{1,0:T(1,128)} %bitcast.42, s32[1,8192]{1,0:T(1,128)} %bitcast.43, f32[2,8192]{1,0:T(2,128)} %frac_ref.1, f32[1,8192]{1,0:T(1,128)} %bitcast.44, bf16[256,128]{1,0:T(8,128)(2,1)} %constant.127.clone.g_ref, ...), custom_call_target="tpu_custom_call" | custom-call | flops 6000000000 | bytes 1048576 | tf_op jit(solution)/shard_map/stream_send/pallas_call | solution.py:155
  10.1 2.1 %collective-permute-start = (f32[6,8192]{1,0:T(8,128)}, f32[6,8192]{1,0:T(8,128)S(1)}, u32[]{:S(2)}, u32[]{:S(2)}) collective-permute-start(f32[6,8192]{1,0:T(8,128)} %get-tuple-element.20), channel_id=1, source_target_pairs={{0,2},{1,3},{2,0},{3,1},{4,6},{5,7},{6,4},{7,5},{8,10},{9,11},{10,... | collective-permute-start | bytes 589832 | tf_op jit(solution)/shard_map/ppermute | solution.py:517
  12.2 0.0 copy-start.16
  12.2 11.1 %all-to-all-start = ((bf16[128,2,64,128]{3,2,1,0:T(8,128)(2,1)}), bf16[128,2,64,128]{3,2,1,0:T(8,128)(2,1)}, u32[]{:S(2)}, u32[]{:S(2)}) async-start(bf16[128,2,64,128]{3,2,1,0:T(8,128)(2,1)} %bitcast.32), calls=%async_computation | async-start | bytes 8388608 | tf_op jit(solution)/shard_map/all_to_all | solution.py:507
  23.3 0.0 copy-done.16
  23.4 0.0 copy-done.15
  23.4 0.2 convert_reduce_fusion
  23.6 0.0 collective-permute-done
  23.7 0.3 fusion.6
  24.0 1.7 select_reduce_fusion
  25.7 32.0 %deposit.1 = (bf16[128,32,128]{2,1,0:T(8,128)(2,1)S(1)}, bf16[128,32,128]{2,1,0:T(8,128)(2,1)S(1)}) custom-call(s32[128,128]{1,0:T(8,128)S(1)} %get-tuple-element.46.idx_ref, s32[1,16384]{1,0:T(1,128)S(1)} %get-tuple-element.43.col_ref, f32[1,16384]{1,0:T(1,128)S(1)} %get-tuple-element.42.fy_ref, f32[1,16384]{1,0:T(1,128)S(1)} %get-tuple-element.41.fx_ref, ...), custom_call_target="tpu_custom_call" | custom-call | flops 20000000000 | bytes 1048576 | tf_op jit(solution)/shard_map/deposit/pallas_call | solution.py:155
  57.7 0.0 copy-start.6
  57.7 1.2 collective-permute-start.1
  58.9 0.6 convert_bitcast_fusion
  59.5 0.6 copy.42
  60.1 1.3 reduce-window.6
  61.4 0.0 collective-permute-done.1
  61.4 1.2 add_convert_fusion
  62.6 13.3 %all-to-all-done = bf16[128,2,64,128]{3,2,1,0:T(8,128)(2,1)} async-done(((bf16[128,2,64,128]{3,2,1,0:T(8,128)(2,1)}), bf16[128,2,64,128]{3,2,1,0:T(8,128)(2,1)}, u32[]{:S(2)}, u32[]{:S(2)}) %all-to-all-start) | async-done | bytes 4194336 | tf_op jit(solution)/shard_map/all_to_all | solution.py:507
  75.9 4.8 %all-to-all-start.2 = ((bf16[128,32,128]{2,1,0:T(8,128)(2,1)}), bf16[128,32,128]{2,1,0:T(8,128)(2,1)S(1)}, u32[]{:S(2)}, u32[]{:S(2)}) async-start(bf16[128,32,128]{2,1,0:T(8,128)(2,1)} %add_convert_fusion), calls=%async_computation.2 | async-start | bytes 2097152 | tf_op jit(solution)/shard_map/all_to_all | solution.py:507
  80.7 0.2 slice_reduce_fusion
  80.9 0.1 compare_bitcast_fusion
  81.0 0.0 copy-done.17
  81.0 0.0 copy-done.18
  81.1 0.1 select_reduce_fusion.2
  81.2 0.1 copy.35
  81.3 0.1 sub.39.idx_ref
  81.4 0.0 copy-done.6
  81.4 0.0 copy-start.7
  81.4 0.8 copy-done.7
  82.2 0.8 copy-done.10
  83.1 0.8 copy-done.11
  83.9 6.8 %stream_recv.1 = bf16[128,64,128]{2,1,0:T(8,128)(2,1)S(1)} custom-call(s32[1,32]{1,0:T(1,128)S(1)} %sub.39.idx_ref, bf16[256,64,128]{2,1,0:T(8,128)(2,1)} %bitcast.11.x_ref, bf16[256,256]{1,0:T(8,128)(2,1)S(1)} %copy-done.6, f32[128,128]{1,0:T(8,128)S(1)} %copy-done.7, f32[128,128]{1,0:T(8,128)S(1)} %copy-done.11, bf16[128,256]{1,0:T(8,128)(2,1)S(1)} %copy-done.10), custom_call_target="tpu_custom_call" | custom-call | flops 6000000000 | bytes 1048576 | tf_op jit(solution)/shard_map/stream_recv/pallas_call | solution.py:155
  90.7 0.0 copy-start.1
  90.7 1.3 copy-done.1
  92.0 8.1 %all-to-all-done.2.ret_ref = bf16[128,32,128]{2,1,0:T(8,128)(2,1)S(1)} async-done(((bf16[128,32,128]{2,1,0:T(8,128)(2,1)}), bf16[128,32,128]{2,1,0:T(8,128)(2,1)S(1)}, u32[]{:S(2)}, u32[]{:S(2)}) %all-to-all-start.2) | async-done | bytes 1048608 | tf_op jit(solution)/shard_map/all_to_all | solution.py:507
  100.1 4.3 %all-to-all-start.1 = ((bf16[128,64,128]{2,1,0:T(8,128)(2,1)}), bf16[128,64,128]{2,1,0:T(8,128)(2,1)S(1)}, u32[]{:S(2)}, u32[]{:S(2)}) async-start(bf16[128,64,128]{2,1,0:T(8,128)(2,1)} %copy-done.1), calls=%async_computation.1 | async-start | bytes 4194304 | tf_op jit(solution)/shard_map/all_to_all | solution.py:507
  104.4 0.0 copy-done.5
  104.4 0.0 copy-start.2
  104.4 1.2 copy-done.2
  105.7 0.8 copy-done.12
  106.4 0.8 copy-done.13
  107.2 0.8 copy-done.14
  107.9 3.7 %dye_send.1 = bf16[256,32,128]{2,1,0:T(8,128)(2,1)S(1)} custom-call(s32[1,32]{1,0:T(1,128)S(1)} %sub.39.idx_ref, bf16[64,8192]{1,0:T(8,128)(2,1)S(1)} %copy-done.2, bf16[128,32,128]{2,1,0:T(8,128)(2,1)S(1)} %all-to-all-done.2.ret_ref, bf16[128,64]{1,0:T(8,128)(2,1)S(1)} %copy-done.14, f32[64,128]{1,0:T(8,128)S(1)} %copy-done.12, f32[64,128]{1,0:T(8,128)S(1)} %copy-done.13, ...), custom_call_target="tpu_custom_call" | custom-call | flops 4000000000 | bytes 1048576 | tf_op jit(solution)/shard_map/dye_send/pallas_call | solution.py:155
  111.7 0.0 copy-start
  111.7 1.3 copy-done
  113.0 22.0 %all-to-all-done.1.a_ref = bf16[128,64,128]{2,1,0:T(8,128)(2,1)S(1)} async-done(((bf16[128,64,128]{2,1,0:T(8,128)(2,1)}), bf16[128,64,128]{2,1,0:T(8,128)(2,1)S(1)}, u32[]{:S(2)}, u32[]{:S(2)}) %all-to-all-start.1) | async-done | bytes 2097184 | tf_op jit(solution)/shard_map/all_to_all | solution.py:507
  135.1 0.9 collective-permute-start.2
  136.0 4.9 %all-to-all-start.3 = ((bf16[128,2,32,128]{3,2,1,0:T(8,128)(2,1)}), bf16[128,2,32,128]{3,2,1,0:T(8,128)(2,1)}, u32[]{:S(2)}, u32[]{:S(2)}) async-start(bf16[128,2,32,128]{3,2,1,0:T(8,128)(2,1)} %bitcast.31), calls=%async_computation.3 | async-start | bytes 4194304 | tf_op jit(solution)/shard_map/all_to_all | solution.py:507
  140.9 0.0 collective-permute-done.2.b_ref
  140.9 0.0 copy-start.3
  140.9 0.0 copy-start.4
  140.9 0.0 copy-start.8
  140.9 0.0 copy-start.9
  140.9 21.3 %gather.1 = (f32[1,8192]{1,0:T(1,128)S(1)}, f32[1,8192]{1,0:T(1,128)S(1)}) custom-call(s32[128,128]{1,0:T(8,128)S(1)} %get-tuple-element.47.base_ref, bf16[128,64,128]{2,1,0:T(8,128)(2,1)S(1)} %all-to-all-done.1.a_ref, bf16[128,64,128]{2,1,0:T(8,128)(2,1)} %collective-permute-done.2.b_ref, s32[1,16384]{1,0:T(1,128)S(1)} %get-tuple-element.43.col_ref, ...), custom_call_target="tpu_custom_call" | custom-call | flops 10000000000 | bytes 1048576 | tf_op jit(solution)/shard_map/gather/pallas_call | solution.py:155
  162.2 8.6 %all-to-all-done.3 = bf16[128,2,32,128]{3,2,1,0:T(8,128)(2,1)} async-done(((bf16[128,2,32,128]{3,2,1,0:T(8,128)(2,1)}), bf16[128,2,32,128]{3,2,1,0:T(8,128)(2,1)}, u32[]{:S(2)}, u32[]{:S(2)}) %all-to-all-start.3) | async-done | bytes 2097184 | tf_op jit(solution)/shard_map/all_to_all | solution.py:507
  170.8 0.1 collective-permute-start.3
  170.9 0.0 copy-done.3
  170.9 0.0 copy-done.4
  170.9 0.0 copy-done.8
  170.9 0.0 copy-done.9
  170.9 4.7 %dye_recv.1 = f32[2,64,8192]{2,1,0:T(8,128)} custom-call(bf16[256,32,128]{2,1,0:T(8,128)(2,1)} %bitcast.13.x_hbm, bf16[256,256]{1,0:T(8,128)(2,1)S(1)} %copy-done.4, f32[128,128]{1,0:T(8,128)S(1)} %copy-done.8, f32[128,128]{1,0:T(8,128)S(1)} %copy-done.9, bf16[256,256]{1,0:T(8,128)(2,1)S(1)} %copy-done.3), custom_call_target="tpu_custom_call" | custom-call | flops 4000000000 | bytes 1048576 | tf_op jit(solution)/shard_map/dye_recv/pallas_call | solution.py:155
  175.5 0.0 collective-permute-done.3
  175.6 0.7 maximum_select_fusion
  (18 shorter events, 0.2 us)
Async XLA Ops:
  10.1 13.6 %collective-permute-start = (f32[6,8192]{1,0:T(8,128)}, f32[6,8192]{1,0:T(8,128)S(1)}, u32[]{:S(2)}, u32[]{:S(2)}) collective-permute-start(f32[6,8192]{1,0:T(8,128)} %get-tuple-element.20), channel_id=1, source_target_pairs={{0,2},{1,3},{2,0},{3,1},{4,6},{5,7},{6,4},{7,5},{8,10},{9,11},{10,... | collective-permute-start | bytes 589832 | tf_op jit(solution)/shard_map/ppermute | solution.py:517
  12.2 11.2 %copy-start.16 = (s32[16,256]{1,0:T(8,128)S(1)}, s32[16,256]{1,0:T(8,128)}, u32[]{:S(2)}) copy-start(s32[16,256]{1,0:T(8,128)} %param.31) | copy-start | bytes 49156
  12.2 11.2 %copy-start.15 = (f32[6,8192]{1,0:T(8,128)S(1)}, f32[6,8192]{1,0:T(8,128)}, u32[]{:S(2)}) copy-start(f32[6,8192]{1,0:T(8,128)} %get-tuple-element.20) | copy-start | bytes 589828
  12.2 63.8 %all-to-all-start = ((bf16[128,2,64,128]{3,2,1,0:T(8,128)(2,1)}), bf16[128,2,64,128]{3,2,1,0:T(8,128)(2,1)}, u32[]{:S(2)}, u32[]{:S(2)}) async-start(bf16[128,2,64,128]{3,2,1,0:T(8,128)(2,1)} %bitcast.32), calls=%async_computation | async-start | bytes 8388608 | tf_op jit(solution)/shard_map/all_to_all | solution.py:507
  57.7 23.6 %copy-start.6 = (bf16[256,256]{1,0:T(8,128)(2,1)S(1)}, bf16[256,256]{1,0:T(8,128)(2,1)}, u32[]{:S(2)}) copy-start(bf16[256,256]{1,0:T(8,128)(2,1)} %constant.131.clone.w1_ref) | copy-start | bytes 393220
  57.7 3.7 %collective-permute-start.1 = (bf16[128,32,128]{2,1,0:T(8,128)(2,1)S(1)}, bf16[128,32,128]{2,1,0:T(8,128)(2,1)S(1)}, u32[]{:S(2)}, u32[]{:S(2)}) collective-permute-start(bf16[128,32,128]{2,1,0:T(8,128)(2,1)S(1)} %get-tuple-element.24), channel_id=1, source_target_pairs={{0,1},{1,0},{2,3},{3,2},{4,5},{5,4},{6,7},{7,6},{8,9},{9,8},{10,11... | collective-permute-start | bytes 3145736 | tf_op jit(solution)/shard_map/ppermute | solution.py:512
  61.4 19.6 %copy-start.17 = (s32[16,256]{1,0:T(8,128)S(1)}, s32[16,256]{1,0:T(8,128)}, u32[]{:S(2)}) copy-start(s32[16,256]{1,0:T(8,128)} %param.31) | copy-start | bytes 49156
  61.4 19.6 %copy-start.18 = (pred[16,256]{1,0:T(8,128)(4,1)S(1)}, pred[16,256]{1,0:T(8,128)(4,1)}, u32[]{:S(2)}) copy-start(pred[16,256]{1,0:T(8,128)(4,1)} %get-tuple-element.37) | copy-start | bytes 12292
  75.9 24.1 %all-to-all-start.2 = ((bf16[128,32,128]{2,1,0:T(8,128)(2,1)}), bf16[128,32,128]{2,1,0:T(8,128)(2,1)S(1)}, u32[]{:S(2)}, u32[]{:S(2)}) async-start(bf16[128,32,128]{2,1,0:T(8,128)(2,1)} %add_convert_fusion), calls=%async_computation.2 | async-start | bytes 2097152 | tf_op jit(solution)/shard_map/all_to_all | solution.py:507
  81.4 0.8 copy-start.7
  82.2 0.8 copy-start.10
  83.1 0.8 copy-start.11
  90.7 1.3 copy-start.1
  92.0 12.4 %copy-start.5 = (bf16[256,256]{1,0:T(8,128)(2,1)S(1)}, bf16[256,256]{1,0:T(8,128)(2,1)}, u32[]{:S(2)}) copy-start(bf16[256,256]{1,0:T(8,128)(2,1)} %constant.137.clone.w2_ref) | copy-start | bytes 393220
  100.1 35.0 %all-to-all-start.1 = ((bf16[128,64,128]{2,1,0:T(8,128)(2,1)}), bf16[128,64,128]{2,1,0:T(8,128)(2,1)S(1)}, u32[]{:S(2)}, u32[]{:S(2)}) async-start(bf16[128,64,128]{2,1,0:T(8,128)(2,1)} %copy-done.1), calls=%async_computation.1 | async-start | bytes 4194304 | tf_op jit(solution)/shard_map/all_to_all | solution.py:507
  104.4 1.2 copy-start.2
  105.6 0.8 copy-start.12
  106.4 0.8 copy-start.13
  107.2 0.8 copy-start.14
  111.7 1.3 copy-start
  135.1 5.8 %collective-permute-start.2 = (bf16[128,64,128]{2,1,0:T(8,128)(2,1)S(1)}, bf16[128,64,128]{2,1,0:T(8,128)(2,1)}, u32[]{:S(2)}, u32[]{:S(2)}) collective-permute-start(bf16[128,64,128]{2,1,0:T(8,128)(2,1)S(1)} %all-to-all-done.1.a_ref), channel_id=1, source_target_pairs={{0,1},{1,0},{2,3},{3,2},{4,5},{5,4},{6,7},{7,6},{8,9},{9,8},{10,11... | collective-permute-start | bytes 6291464 | tf_op jit(solution)/shard_map/ppermute | solution.py:512
  136.0 34.8 %all-to-all-start.3 = ((bf16[128,2,32,128]{3,2,1,0:T(8,128)(2,1)}), bf16[128,2,32,128]{3,2,1,0:T(8,128)(2,1)}, u32[]{:S(2)}, u32[]{:S(2)}) async-start(bf16[128,2,32,128]{3,2,1,0:T(8,128)(2,1)} %bitcast.31), calls=%async_computation.3 | async-start | bytes 4194304 | tf_op jit(solution)/shard_map/all_to_all | solution.py:507
  140.9 30.0 %copy-start.3 = (bf16[256,256]{1,0:T(8,128)(2,1)S(1)}, bf16[256,256]{1,0:T(8,128)(2,1)}, u32[]{:S(2)}) copy-start(bf16[256,256]{1,0:T(8,128)(2,1)} %constant.140.clone.v_ref) | copy-start | bytes 393220
  140.9 30.0 %copy-start.4 = (bf16[256,256]{1,0:T(8,128)(2,1)S(1)}, bf16[256,256]{1,0:T(8,128)(2,1)}, u32[]{:S(2)}) copy-start(bf16[256,256]{1,0:T(8,128)(2,1)} %constant.138.clone.w1_ref) | copy-start | bytes 393220
  140.9 30.0 %copy-start.8 = (f32[128,128]{1,0:T(8,128)S(1)}, f32[128,128]{1,0:T(8,128)}, u32[]{:S(2)}) copy-start(f32[128,128]{1,0:T(8,128)} %constant.132.clone.tc_ref) | copy-start | bytes 196612
  140.9 29.9 %copy-start.9 = (f32[128,128]{1,0:T(8,128)S(1)}, f32[128,128]{1,0:T(8,128)}, u32[]{:S(2)}) copy-start(f32[128,128]{1,0:T(8,128)} %constant.139.clone.ts_ref) | copy-start | bytes 196612
  170.8 4.7 %collective-permute-start.3 = (f32[1,8192]{1,0:T(1,128)S(1)}, f32[1,8192]{1,0:T(1,128)S(1)}, u32[]{:S(2)}, u32[]{:S(2)}) collective-permute-start(f32[1,8192]{1,0:T(1,128)S(1)} %get-tuple-element.32), channel_id=1, source_target_pairs={{0,2},{1,3},{2,0},{3,1},{4,6},{5,7},{6,4},{7,5},{8,10},{9,11},{10,... | collective-permute-start | bytes 98312 | tf_op jit(solution)/shard_map/ppermute | solution.py:517
